TPU v7x, 32 devices: a whole 2x2x4 slice. The times are simulated.
32 devices in a mesh: group: 2 (over y), blk: 4 (over z), tensor: 4 (over x, core).
Axes of the slice: x: 2, y: 2, z: 4, core: 2. Of those that a mesh axis runs over, the one named last changes fastest.
Arguments:
- queries: bfloat16 [8, 256, 64, 128], P(('group', 'blk'), None, 'tensor'), parts along dimension 0, may hold values from -36 to 36
- new_kv: bfloat16 [2, 8, 256, 8, 128], P(None, ('group', 'blk'), None, 'tensor'), parts along dimension 1, may hold values from -24 to 24
- pool: bfloat16 [192, 2, 128, 8, 128], P(('group', 'blk'), None, None, 'tensor'), parts along dimension 0, may hold values from -6 to 6
- prefix_slot: int32 [8, 32], P(('group', 'blk')), parts along dimension 0, may hold values from 0 to 23
- prefix_owner: int32 [8, 32], P(('group', 'blk')), parts along dimension 0, may hold values from 0 to 3, as said below
- prefix_len: int32 [8], P(('group', 'blk')), parts along dimension 0, may hold values from 1 to 32, as said below
- write_slot: int32 [8, 2], P(('group', 'blk')), parts along dimension 0, may hold values from 0 to 23
- write_owner: int32 [8, 2], P(('group', 'blk')), parts along dimension 0, may hold values from 0 to 3, as said below
Outputs:
- attended: bfloat16 [8, 256, 64, 128], P(('group', 'blk'), None, 'tensor'), parts along dimension 0
- new_pool: bfloat16 [192, 2, 128, 8, 128], P(('group', 'blk'), None, None, 'tensor'), parts along dimension 0
There are 2 independent parts, one for each index of `group`. A program takes and returns all parts, laid end to end along the dimension named above; each array names one. Nothing has to cross between parts.
Inputs may be any that keep to these rules, and one draw needn't show every extreme that they name: `prefix_owner`: in the rows of one request no owner appears more than 8 times; some owner appears exactly 8 times in every request's row. `prefix_len`: some request has exactly 32 prefix blocks. `write_owner`: no two new blocks go to the same pool row; the new blocks of the requests of one index of blk go to different owners; every owner receives exactly 2 new blocks (the requests' new blocks spread evenly over the owners).
All inputs are finite; a program needn't handle non-finite values.
Results may differ from a plain program's by a relative error of at most 0.0065.
Values may be sent and summed in bfloat16 or wider, within the bound.
No kernel may reach another device: no remote copies, remote signals or barrier semaphores. Data moves between devices by JAX's collectives and lax.ppermute only.
A program may use at most 64 MiB of HBM per device.

v0:
```python
import math

import jax
import jax.numpy as jnp
from jax import lax
from jax.sharding import PartitionSpec as P


def owner_rank(owners):
    places = jnp.arange(owners.shape[1])
    earlier = (owners[:, :, None] == owners[:, None, :]) & (
        places[None, None, :] < places[None, :, None]
    )
    return jnp.sum(earlier.astype(jnp.int32), axis=2)


def slot_table(owners, slot_ids, rank_ids, targets, capacity):
    matched = (owners[None, :, None, :] == targets[:, None, None, None]) & (
        rank_ids[None, :, None, :] == jnp.arange(capacity)[None, None, :, None]
    )
    return jnp.sum(jnp.where(matched, slot_ids[None, :, None, :], 0), axis=3)


def per_device(
    queries, new_kv, pool, prefix_slot, prefix_owner, prefix_len, write_slot, write_owner
):
    num_blk = lax.axis_size("blk")
    my_index = lax.axis_index("blk")
    req_dev, suffix, heads_dev, head_dim = queries.shape
    kv_dev = new_kv.shape[3]
    pool_dev = pool.shape[0]
    block_tok = pool.shape[2]
    prefix_blocks = prefix_slot.shape[1]
    new_count = suffix // block_tok
    capacity = max(2, (prefix_blocks + num_blk - 1) // num_blk)
    group = heads_dev // kv_dev
    scale = head_dim ** (-0.5)
    owner_ids = jnp.arange(num_blk, dtype=jnp.int32)
    rank_ids = owner_rank(prefix_owner)
    wanted = slot_table(prefix_owner, prefix_slot, rank_ids, owner_ids, capacity).reshape(
        num_blk, req_dev * capacity
    )
    asked = lax.all_to_all(wanted, "blk", split_axis=0, concat_axis=0, tiled=True)
    outgoing = pool[asked.reshape(-1)].reshape((num_blk, req_dev * capacity) + pool.shape[1:])
    arrived = lax.all_to_all(outgoing, "blk", split_axis=0, concat_axis=0, tiled=True)
    arrived = arrived.reshape((num_blk * req_dev * capacity,) + pool.shape[1:])
    picks = (
        prefix_owner * (req_dev * capacity)
        + jnp.arange(req_dev, dtype=jnp.int32)[:, None] * capacity
        + rank_ids
    )
    fetched = arrived[picks]
    per_step = math.gcd(prefix_blocks, max(1, 512 // block_tok))
    step_count = prefix_blocks // per_step
    key_count = per_step * block_tok
    starts = jnp.arange(step_count, dtype=jnp.int32) * key_count
    query_rows = queries[0].reshape(suffix, kv_dev, group, head_dim)
    scores = (
        jnp.einsum("ikgd,jkd->kgij", query_rows, new_kv[0, 0], preferred_element_type=jnp.float32)
        * scale
    )
    causal = jnp.arange(suffix)[None, :] <= jnp.arange(suffix)[:, None]
    scores = jnp.where(causal, scores, -jnp.inf)
    running = jnp.max(scores, axis=3)
    weights = jnp.exp(scores - running[..., None])
    total = jnp.sum(weights, axis=3)
    summed = jnp.einsum(
        "kgij,jkd->kgid",
        weights.astype(jnp.bfloat16),
        new_kv[1, 0],
        preferred_element_type=jnp.float32,
    )
    limit = prefix_len[0] * block_tok
    grouped = fetched[0].reshape(step_count, per_step, 2, block_tok, kv_dev, head_dim)
    keys_all = grouped[:, :, 0].reshape(step_count, key_count, kv_dev, head_dim)
    values_all = grouped[:, :, 1].reshape(step_count, key_count, kv_dev, head_dim)

    def absorb(carry, inputs):
        running_max, running_total, running_sum = carry
        keys_part, values_part, start = inputs
        part_scores = (
            jnp.einsum("ikgd,jkd->kgij", query_rows, keys_part, preferred_element_type=jnp.float32)
            * scale
        )
        usable = start + jnp.arange(key_count) < limit
        part_scores = jnp.where(usable, part_scores, -jnp.inf)
        newest = jnp.maximum(running_max, jnp.max(part_scores, axis=3))
        part_weights = jnp.exp(part_scores - newest[..., None])
        factor = jnp.exp(running_max - newest)
        running_total = running_total * factor + jnp.sum(part_weights, axis=3)
        running_sum = running_sum * factor[..., None] + jnp.einsum(
            "kgij,jkd->kgid",
            part_weights.astype(jnp.bfloat16),
            values_part,
            preferred_element_type=jnp.float32,
        )
        return (newest, running_total, running_sum)

    def visit(carry, inputs):
        return (absorb(carry, inputs), None)

    (running, total, summed), unused = lax.scan(
        visit, (running, total, summed), (keys_all, values_all, starts)
    )
    result = summed / total[..., None]
    outputs = [
        jnp.transpose(result, (2, 0, 1, 3))
        .reshape(suffix, heads_dev, head_dim)
        .astype(jnp.bfloat16)
    ]
    attended = jnp.stack(outputs, axis=0)
    fresh = new_kv.reshape(2, req_dev, new_count, block_tok, kv_dev, head_dim)
    fresh = jnp.transpose(fresh, (1, 2, 0, 3, 4, 5)).reshape(
        (req_dev * new_count,) + pool.shape[1:]
    )
    flat_owner = write_owner.reshape(-1)
    flat_slot = write_slot.reshape(-1)
    landed, landed_owner, landed_slot = (
        lax.all_gather(fresh, "blk", axis=0, tiled=True),
        lax.all_gather(flat_owner, "blk", axis=0, tiled=True),
        lax.all_gather(flat_slot, "blk", axis=0, tiled=True),
    )
    targets = jnp.where(landed_owner == my_index, landed_slot, pool_dev)
    new_pool = pool.at[targets].set(landed, mode="drop")
    return (attended, new_pool)


def solution(mesh):
    in_specs = (
        P(("group", "blk"), None, "tensor", None),
        P(None, ("group", "blk"), None, "tensor", None),
        P(("group", "blk"), None, None, "tensor", None),
        P(("group", "blk"), None),
        P(("group", "blk"), None),
        P(("group", "blk")),
        P(("group", "blk"), None),
        P(("group", "blk"), None),
    )
    out_specs = (
        P(("group", "blk"), None, "tensor", None),
        P(("group", "blk"), None, None, "tensor", None),
    )
    return jax.shard_map(
        per_device, mesh=mesh, in_specs=in_specs, out_specs=out_specs, check_vma=False
    )
```

profile of v0, /device:TPU:0, one launch (start us, length us, event | category | flops | bytes accessed | tf_op | source)
XLA Modules:
  0.0 271.5 jit_solution(9353449056323621493)
XLA Ops:
  7.2 7.8 %copy.104 = bf16[24,2,128,2,128]{4,3,2,1,0:T(2,128)(2,1)} copy(bf16[24,2,128,2,128]{4,3,2,1,0:T(2,128)(2,1)} %param.12) | data formatting | bytes 6291456
  15.4 11.7 %all_to_all.14 = s32[4,1,8]{2,1,0:T(1,128)S(1)} all-to-all(s32[4,1,8]{2,1,0:T(1,128)S(1)} %bitcast.111), channel_id=1, replica_groups=mesh['group'=2,'blk'=4,'tensor'=4] {'blk'}, dimensions={0} | all-to-all | bytes 256 | tf_op jit(solution)/shard_map/all_to_all | solution.py:43
  27.5 0.7 reduce.5
  28.3 12.0 %gather_fusion = bf16[32,2,128,2,128]{4,3,2,1,0:T(2,128)(2,1)} fusion(bf16[24,2,128,2,128]{4,3,2,1,0:T(2,128)(2,1)} %copy.104, s32[1024]{0:T(1024)S(1)} %pad_clamp_fusion.1), kind=kCustom, calls=%fused_computation | custom fusion | bytes 8388736 | tf_op jit(solution)/shard_map/gather | solution.py:44
  40.4 5.3 %copy.64 = bf16[4,8,2,128,2,128]{5,3,4,2,1,0:T(8,128)(2,1)} copy(bf16[4,8,2,128,2,128]{5,4,3,2,1,0:T(2,128)(2,1)} %bitcast.105) | data formatting | bytes 8388608 | tf_op jit(solution)/shard_map/reshape | solution.py:44
  45.7 5.0 %all-to-all-start.1 = ((bf16[4,8,2,128,2,128]{5,3,4,2,1,0:T(8,128)(2,1)}), bf16[4,8,2,128,2,128]{5,3,4,2,1,0:T(8,128)(2,1)}, u32[]{:S(2)}, u32[]{:S(2)}) async-start(bf16[4,8,2,128,2,128]{5,3,4,2,1,0:T(8,128)(2,1)} %copy.64), calls=%async_computation.1 | async-start | bytes 8388608 | tf_op jit(solution)/shard_map/all_to_all | solution.py:45
  50.8 0.7 copy.69
  52.9 106.8 %all-reduce.2 = (s32[8]{0:T(128)S(1)}, s32[8]{0:T(128)S(1)}) all-reduce(s32[8]{0:T(128)S(1)} %bitcast_dynamic-update-slice_fusion, s32[8]{0:T(128)S(1)} %bitcast_dynamic-update-slice_fusion.1), channel_id=3, replica_groups=mesh['group'=2,'blk'=4,'tensor'=4] {'blk'}, use_global_device_ids=true, to_apply=%add.1 | all-reduce | flops 16 | bytes 128
  161.0 0.7 fusion.19
  161.7 0.9 fusion.18
  162.6 1.2 fusion.20
  163.8 3.3 %copy.70 = bf16[8,2,128,2,128]{4,3,2,1,0:T(2,128)(2,1)} copy(bf16[8,2,128,2,128]{4,2,3,1,0:T(8,128)(2,1)} %bitcast.108) | data formatting | bytes 2097152 | tf_op jit(solution)/shard_map/all_gather | solution.py:119
  167.1 7.2 %scatter_fusion = bf16[24,2,128,2,128]{4,3,2,1,0:T(2,128)(2,1)} fusion(bf16[24,2,128,2,128]{4,3,2,1,0:T(2,128)(2,1)} %copy.104, s32[8]{0:T(128)S(1)} %compare_select_fusion, bf16[8,2,128,2,128]{4,3,2,1,0:T(2,128)(2,1)} %copy.70), kind=kCustom, calls=%fused_computation.2 | custom fusion | bytes 3145760 | tf_op jit(solution)/shard_map/scatter | solution.py:124
  174.3 5.2 %gather_fusion.1 = bf16[32,2,128,2,128]{4,2,3,1,0:T(8,128)(2,1)} fusion(bf16[32,2,128,2,128]{4,2,3,1,0:T(8,128)(2,1)} %bitcast.23, s32[1024]{0:T(1024)S(1)} %pad_clamp_fusion), kind=kCustom, calls=%fused_computation.1 | custom fusion | bytes 8388736 | tf_op jit(solution)/shard_map/gather | solution.py:52
  179.5 2.7 %fusion.33 = (bf16[8,4,1,128,2,128]{5,3,4,2,1,0:T(8,128)(2,1)S(1)}, bf16[8,4,1,128,2,128]{5,3,4,2,1,0:T(8,128)(2,1)S(1)}) fusion(bf16[8,4,2,128,2,128]{5,3,4,2,1,0:T(8,128)(2,1)} %bitcast.104), kind=kLoop, calls=%fused_computation.61 | loop fusion | bytes 8388608 | tf_op jit(solution)/shard_map/slice | solution.py:76
  182.3 1.6 copy.65
  183.9 1.5 copy.66
  185.4 76.8 %while.14 = (s32[]{:T(128)}, f32[2,8,256]{2,1,0:T(8,128)S(1)}, f32[2,8,256]{2,1,0:T(8,128)S(1)}, f32[2,8,256,128]{3,2,1,0:T(8,128)S(1)}, s32[8]{0:T(128)S(1)}, /...) while((s32[]{:T(128)}, f32[2,8,256]{2,1,0:T(8,128)S(1)}, ...), condition=%wide.region_7.8_spmd, body=%wide.region_4.7_spmd.sunk | while | flops 1097868288 | bytes 31198328 | solution.py:102
  186.0 0.7 add_compare_fusion.2
  186.7 2.2 bitcast_reduce_fusion.2
  188.9 2.0 fusion.44
  190.9 4.1 %multiply_add_fusion.5 = f32[2,8,256,128]{3,2,1,0:T(8,128)S(1)} fusion(f32[2,8,256,128]{3,2,1,0:T(8,128)S(1)} %get-tuple-element.158, f32[2,512,256,8]{2,1,3,0:T(8,128)S(1)} %get-tuple-element.142, f32[2,8,256]{2,1,0:T(8,128)S(1)} %max.4, pred[512]{0:T(512)(128)(4,1)S(1)} %add_compare_fusion.2, f32[2,8,256]{2,1,0:T(8,128)S(1)} %get-tuple-element.144, ...), kind=kOutput, calls=%fused_computation.11.clone.1 | convolution fusion | flops 546308096 | bytes 12878848 | tf_op jit(solution)/shard_map/while/body/eval_jaxpr/kgij,jkd->kgid/dot_general | solution.py:91
  195.6 0.7 add_compare_fusion.2
  196.3 2.2 bitcast_reduce_fusion.2
  198.5 2.0 fusion.44
  200.5 4.1 %multiply_add_fusion.5 = f32[2,8,256,128]{3,2,1,0:T(8,128)S(1)} fusion(f32[2,8,256,128]{3,2,1,0:T(8,128)S(1)} %get-tuple-element.158, f32[2,512,256,8]{2,1,3,0:T(8,128)S(1)} %get-tuple-element.142, f32[2,8,256]{2,1,0:T(8,128)S(1)} %max.4, pred[512]{0:T(512)(128)(4,1)S(1)} %add_compare_fusion.2, f32[2,8,256]{2,1,0:T(8,128)S(1)} %get-tuple-element.144, ...), kind=kOutput, calls=%fused_computation.11.clone.1 | convolution fusion | flops 546308096 | bytes 12878848 | tf_op jit(solution)/shard_map/while/body/eval_jaxpr/kgij,jkd->kgid/dot_general | solution.py:91
  205.2 0.7 add_compare_fusion.2
  205.9 2.2 bitcast_reduce_fusion.2
  208.1 2.0 fusion.44
  210.1 4.1 %multiply_add_fusion.5 = f32[2,8,256,128]{3,2,1,0:T(8,128)S(1)} fusion(f32[2,8,256,128]{3,2,1,0:T(8,128)S(1)} %get-tuple-element.158, f32[2,512,256,8]{2,1,3,0:T(8,128)S(1)} %get-tuple-element.142, f32[2,8,256]{2,1,0:T(8,128)S(1)} %max.4, pred[512]{0:T(512)(128)(4,1)S(1)} %add_compare_fusion.2, f32[2,8,256]{2,1,0:T(8,128)S(1)} %get-tuple-element.144, ...), kind=kOutput, calls=%fused_computation.11.clone.1 | convolution fusion | flops 546308096 | bytes 12878848 | tf_op jit(solution)/shard_map/while/body/eval_jaxpr/kgij,jkd->kgid/dot_general | solution.py:91
  214.8 0.7 add_compare_fusion.2
  215.5 2.2 bitcast_reduce_fusion.2
  217.7 2.0 fusion.44
  219.7 4.1 %multiply_add_fusion.5 = f32[2,8,256,128]{3,2,1,0:T(8,128)S(1)} fusion(f32[2,8,256,128]{3,2,1,0:T(8,128)S(1)} %get-tuple-element.158, f32[2,512,256,8]{2,1,3,0:T(8,128)S(1)} %get-tuple-element.142, f32[2,8,256]{2,1,0:T(8,128)S(1)} %max.4, pred[512]{0:T(512)(128)(4,1)S(1)} %add_compare_fusion.2, f32[2,8,256]{2,1,0:T(8,128)S(1)} %get-tuple-element.144, ...), kind=kOutput, calls=%fused_computation.11.clone.1 | convolution fusion | flops 546308096 | bytes 12878848 | tf_op jit(solution)/shard_map/while/body/eval_jaxpr/kgij,jkd->kgid/dot_general | solution.py:91
  225.1 2.2 bitcast_reduce_fusion.2
  227.3 2.0 fusion.44
  229.3 4.1 %multiply_add_fusion.5 = f32[2,8,256,128]{3,2,1,0:T(8,128)S(1)} fusion(f32[2,8,256,128]{3,2,1,0:T(8,128)S(1)} %get-tuple-element.158, f32[2,512,256,8]{2,1,3,0:T(8,128)S(1)} %get-tuple-element.142, f32[2,8,256]{2,1,0:T(8,128)S(1)} %max.4, pred[512]{0:T(512)(128)(4,1)S(1)} %add_compare_fusion.2, f32[2,8,256]{2,1,0:T(8,128)S(1)} %get-tuple-element.144, ...), kind=kOutput, calls=%fused_computation.11.clone.1 | convolution fusion | flops 546308096 | bytes 12878848 | tf_op jit(solution)/shard_map/while/body/eval_jaxpr/kgij,jkd->kgid/dot_general | solution.py:91
  234.7 2.2 bitcast_reduce_fusion.2
  236.9 2.0 fusion.44
  238.9 4.1 %multiply_add_fusion.5 = f32[2,8,256,128]{3,2,1,0:T(8,128)S(1)} fusion(f32[2,8,256,128]{3,2,1,0:T(8,128)S(1)} %get-tuple-element.158, f32[2,512,256,8]{2,1,3,0:T(8,128)S(1)} %get-tuple-element.142, f32[2,8,256]{2,1,0:T(8,128)S(1)} %max.4, pred[512]{0:T(512)(128)(4,1)S(1)} %add_compare_fusion.2, f32[2,8,256]{2,1,0:T(8,128)S(1)} %get-tuple-element.144, ...), kind=kOutput, calls=%fused_computation.11.clone.1 | convolution fusion | flops 546308096 | bytes 12878848 | tf_op jit(solution)/shard_map/while/body/eval_jaxpr/kgij,jkd->kgid/dot_general | solution.py:91
  244.3 2.2 bitcast_reduce_fusion.2
  246.6 2.0 fusion.44
  248.5 4.1 %multiply_add_fusion.5 = f32[2,8,256,128]{3,2,1,0:T(8,128)S(1)} fusion(f32[2,8,256,128]{3,2,1,0:T(8,128)S(1)} %get-tuple-element.158, f32[2,512,256,8]{2,1,3,0:T(8,128)S(1)} %get-tuple-element.142, f32[2,8,256]{2,1,0:T(8,128)S(1)} %max.4, pred[512]{0:T(512)(128)(4,1)S(1)} %add_compare_fusion.2, f32[2,8,256]{2,1,0:T(8,128)S(1)} %get-tuple-element.144, ...), kind=kOutput, calls=%fused_computation.11.clone.1 | convolution fusion | flops 546308096 | bytes 12878848 | tf_op jit(solution)/shard_map/while/body/eval_jaxpr/kgij,jkd->kgid/dot_general | solution.py:91
  253.9 2.2 bitcast_reduce_fusion.2
  256.2 2.0 fusion.44
  258.2 4.1 %multiply_add_fusion.5 = f32[2,8,256,128]{3,2,1,0:T(8,128)S(1)} fusion(f32[2,8,256,128]{3,2,1,0:T(8,128)S(1)} %get-tuple-element.158, f32[2,512,256,8]{2,1,3,0:T(8,128)S(1)} %get-tuple-element.142, f32[2,8,256]{2,1,0:T(8,128)S(1)} %max.4, pred[512]{0:T(512)(128)(4,1)S(1)} %add_compare_fusion.2, f32[2,8,256]{2,1,0:T(8,128)S(1)} %get-tuple-element.144, ...), kind=kOutput, calls=%fused_computation.11.clone.1 | convolution fusion | flops 546308096 | bytes 12878848 | tf_op jit(solution)/shard_map/while/body/eval_jaxpr/kgij,jkd->kgid/dot_general | solution.py:91
  262.3 0.7 fusion.26
  263.0 1.6 copy.86
  (75 shorter events, 9.8 us)
Async XLA Ops:
  7.2 8.0 %copy-start.2 = (s32[1,32]{1,0:T(1,128)S(1)}, s32[1,32]{1,0:T(1,128)}, u32[]{:S(2)}) copy-start(s32[1,32]{1,0:T(1,128)} %param.13) | copy-start | bytes 388
  7.2 7.8 %copy-start.5 = (s32[1,32]{1,0:T(1,128)S(1)}, s32[1,32]{1,0:T(1,128)}, u32[]{:S(2)}) copy-start(s32[1,32]{1,0:T(1,128)} %param.14) | copy-start | bytes 388
  45.7 5.1 %copy-start.1 = (bf16[2,1,256,2,128]{4,3,2,1,0:T(2,128)(2,1)S(1)}, bf16[2,1,256,2,128]{4,3,2,1,0:T(2,128)(2,1)}, u32[]{:S(2)}) copy-start(bf16[2,1,256,2,128]{4,3,2,1,0:T(2,128)(2,1)} %param.11) | copy-start | bytes 786436
  45.7 5.9 %copy-start.6 = (u32[32]{0:T(128)S(1)}, u32[32]{0:T(128)}, u32[]{:S(2)}) copy-start(u32[32]{0:T(128)} %constant.53) | copy-start | bytes 388
  45.7 7.0 %copy-start.3 = (s32[1,2]{1,0:T(1,128)S(1)}, s32[1,2]{1,0:T(1,128)}, u32[]{:S(2)}) copy-start(s32[1,2]{1,0:T(1,128)} %param.16) | copy-start | bytes 28
  45.7 7.1 %copy-start.4 = (s32[1,2]{1,0:T(1,128)S(1)}, s32[1,2]{1,0:T(1,128)}, u32[]{:S(2)}) copy-start(s32[1,2]{1,0:T(1,128)} %param.17) | copy-start | bytes 28
  45.7 114.1 %copy-start = (bf16[1,256,16,128]{3,2,1,0:T(8,128)(2,1)S(1)}, bf16[1,256,16,128]{3,2,1,0:T(8,128)(2,1)}, u32[]{:S(2)}) copy-start(bf16[1,256,16,128]{3,2,1,0:T(8,128)(2,1)} %param.10) | copy-start | bytes 3145732
  45.7 128.6 %all-to-all-start.1 = ((bf16[4,8,2,128,2,128]{5,3,4,2,1,0:T(8,128)(2,1)}), bf16[4,8,2,128,2,128]{5,3,4,2,1,0:T(8,128)(2,1)}, u32[]{:S(2)}, u32[]{:S(2)}) async-start(bf16[4,8,2,128,2,128]{5,3,4,2,1,0:T(8,128)(2,1)} %copy.64), calls=%async_computation.1 | async-start | bytes 8388608 | tf_op jit(solution)/shard_map/all_to_all | solution.py:45
  50.7 113.1 %all-gather.5.cloned.1.call-start = ((), (), s32[]{:S(2)}) async-start(), calls=%async_computation.2 | async-start | bytes 1310720 | tf_op jit(solution)/shard_map/all_gather | solution.py:119
Sparse Core Ops, SparseCore 0:
  53.7 48.2 all-gather.4
where the time goes:
time: 273 us; the launch traced here: 272 us
  blocking collectives  118 us (43%)
  local copies, waits for them, and re-layouts  55.7 us (20%)
  matrix products  52.5 us (19%)
  other arithmetic  23.7 us (9%)
  between operations  15.5 us (6%)
  starting transfers between devices  5.04 us (2%)
    unnamed x1, blocking collectives  107 us
    dot_general x8, matrix products, absorb(): jnp.einsum('kgij,jkd->kgid', part_weights.astype(jnp.bfloat16), values_pa...  32.7 us
    dot_general x8, matrix products, absorb(): jnp.einsum('ikgd,jkd->kgij', query_rows, keys_part, preferred_element_typ...  17.8 us
    reduce_sum x8, other arithmetic, absorb(): running_total = running_total * factor + jnp.sum(part_weights, axis=3)  15.7 us
    gather x1, local copies, waits for them, and re-layouts, per_device(): pool[asked.reshape(-1)]  12 us
    all_to_all x1, blocking collectives, per_device(): lax.all_to_all(wanted, 'blk', split_axis=0, concat_axis=0, tiled=True)  11.7 us
    unnamed x22, local copies, waits for them, and re-layouts  8.91 us
    scatter x1, local copies, waits for them, and re-layouts, per_device(): new_pool = pool.at[targets].set(landed, mode='drop')  7.16 us
  transfers between devices with their start and end apart: 2, of which 0 were waited for; matrix products, arithmetic and copies ran while one was open for 6% of the time, Pallas kernels for 0%

commit v1 on v0

v1 whole, which is shorter than its diff:
```python
import functools
import math

import jax
import jax.numpy as jnp
from jax import lax
from jax.experimental import pallas as pl
from jax.experimental.pallas import tpu as pltpu
from jax.sharding import PartitionSpec as P

HBM = pl.BlockSpec(memory_space=pl.ANY)
SMEM = pl.BlockSpec(memory_space=pltpu.SMEM)
VMEM_LIMIT = 48 * 1024 * 1024


def pick_fresh_kernel(num_blk, block_tok, owner_ref, new_ref, *rest):
    outs, sems = rest[:-1], rest[-1]
    me = lax.axis_index("blk")
    copies = []
    for d, out in enumerate(outs, start=1):
        target = lax.rem(me + d, num_blk)
        chosen = jnp.int32(0)
        for b in range(1, owner_ref.shape[1]):
            chosen = jnp.where(owner_ref[0, b] == target, b, chosen)
        for kv in range(2):
            copies.append(
                pltpu.make_async_copy(
                    new_ref.at[kv, 0, pl.ds(chosen * block_tok, block_tok)],
                    out.at[kv],
                    sems.at[d - 1, kv],
                )
            )
    for copy in copies:
        copy.start()
    for copy in copies:
        copy.wait()


def slots_of(meta_ref, first, pool_dev, prefix_blocks, table_ref, row, capacity):
    for k in range(capacity + 1):
        table_ref[row, k] = 0

    def step(j, count):
        slot = meta_ref[0, j] - first
        mine = (slot >= 0) & (slot < pool_dev)
        table_ref[row, count] = jnp.where(mine, slot, 0)
        return jnp.where(mine, jnp.minimum(count + 1, capacity), count)

    lax.fori_loop(0, prefix_blocks, step, jnp.int32(0))


def gather_kernel(plan, pool_dev, prefix_blocks, capacity, *refs):
    count = len(plan)
    metas, pool_ref, refs = refs[:count], refs[count], refs[count + 1 :]
    outs, table_ref, sems = refs[:-2], refs[-2], refs[-1]
    first = lax.axis_index("blk") * pool_dev
    copies = []
    at = 0
    for row, sizes in enumerate(plan):
        slots_of(metas[row], first, pool_dev, prefix_blocks, table_ref, row, capacity)
        k = 0
        for size in sizes:
            for place in range(size):
                copy = pltpu.make_async_copy(
                    pool_ref.at[table_ref[row, k]], outs[at].at[place], sems.at[row, k]
                )
                copy.start()
                copies.append(copy)
                k += 1
            at += 1
    for copy in copies:
        copy.wait()


def gather(metas, pool, plan, capacity, prefix_blocks):
    pool_dev = pool.shape[0]
    shapes = [
        jax.ShapeDtypeStruct((size,) + pool.shape[1:], pool.dtype)
        for sizes in plan
        for size in sizes
    ]
    return pl.pallas_call(
        functools.partial(gather_kernel, plan, pool_dev, prefix_blocks, capacity),
        out_shape=shapes,
        in_specs=[SMEM] * len(metas) + [HBM],
        out_specs=[HBM] * len(shapes),
        scratch_shapes=[
            pltpu.SMEM((len(metas), capacity + 1), jnp.int32),
            pltpu.SemaphoreType.DMA((len(metas), capacity)),
        ],
        cost_estimate=pl.CostEstimate(
            flops=0,
            bytes_accessed=2 * sum(math.prod(s.shape) for s in shapes) * 2,
            transcendentals=0,
        ),
    )(*metas, pool)


def write_back_kernel(num_blk, prefix_blocks, new_count, block_tok, *refs):
    metas, refs = refs[:num_blk], refs[num_blk:]
    pool_ref, new_ref, refs = refs[0], refs[1], refs[2:]
    fresh, out_ref, sems, last = refs[: num_blk - 1], refs[-3], refs[-2], refs[-1]
    pool_dev = pool_ref.shape[0]
    first = lax.axis_index("blk") * pool_dev
    for b in range(pool_dev):
        pltpu.make_async_copy(pool_ref.at[b], out_ref.at[b], sems.at[b]).start()
    for b in range(pool_dev):
        pltpu.make_async_copy(pool_ref.at[b], out_ref.at[b], sems.at[b]).wait()
    for source in range(num_blk):
        for b in range(new_count):
            slot = metas[source][0, prefix_blocks + b] - first

            @pl.when((slot >= 0) & (slot < pool_dev))
            def write():
                for kv in range(2):
                    if source == 0:
                        src = new_ref.at[kv, 0, pl.ds(b * block_tok, block_tok)]
                    else:
                        src = fresh[source - 1].at[kv]
                    copy = pltpu.make_async_copy(src, out_ref.at[slot, kv], last)
                    copy.start()
                    copy.wait()


def write_back(metas, pool, new_kv, fresh, prefix_blocks, new_count):
    num_blk = len(metas)
    return pl.pallas_call(
        functools.partial(write_back_kernel, num_blk, prefix_blocks, new_count, pool.shape[2]),
        out_shape=jax.ShapeDtypeStruct(pool.shape, pool.dtype),
        in_specs=[SMEM] * num_blk + [HBM] * (num_blk + 1),
        out_specs=HBM,
        scratch_shapes=[
            pltpu.SemaphoreType.DMA((pool.shape[0],)),
            pltpu.SemaphoreType.DMA,
        ],
        cost_estimate=pl.CostEstimate(
            flops=0, bytes_accessed=4 * math.prod(pool.shape), transcendentals=0
        ),
    )(*metas, pool, new_kv, *fresh)


def attend_kernel(
    sizes, kv_dev, group, block_tok, rows, first, final, valid_ref, q_ref, *refs
):
    parts, refs = refs[: len(sizes)], refs[len(sizes) :]
    if first:
        new_ref, refs = refs[0], refs[1:]
    else:
        acc_in, stat_in, refs = refs[0], refs[1], refs[2:]
    if final:
        out_ref, refs = refs[0], refs[1:]
    else:
        acc_out, stat_out, refs = refs[0], refs[1], refs[2:]
    key_ref, value_ref, stage_ref = refs
    tile = pl.program_id(0)
    tile_tok, heads_dev, head_dim = q_ref.shape
    factor = head_dim**-0.5 * math.log2(math.e)
    prefix_keys = sum(sizes) * block_tok
    suffix = new_ref.shape[1] // kv_dev if first else 0
    keys = prefix_keys + suffix

    def unpack(raw, kv, at, length):
        target = key_ref if kv == 0 else value_ref
        if kv_dev == 1:
            target[0, pl.ds(at, length), pl.ds(0, head_dim)] = raw
            return
        stage_ref[...] = raw.astype(jnp.float32)
        for h in range(kv_dev):
            target[h, pl.ds(at, length), pl.ds(0, head_dim)] = stage_ref[
                pl.ds(h, length, stride=kv_dev), :
            ].astype(jnp.bfloat16)

    @pl.when(tile == 0)
    def prepare():
        value_ref[:, :, head_dim:] = jnp.ones(
            (kv_dev, keys, value_ref.shape[2] - head_dim), jnp.bfloat16
        )
        base = 0
        for part, size in zip(parts, sizes):

            def block(b, carry, part=part, base=base):
                at = pl.multiple_of(base + b * block_tok, block_tok)
                for kv in range(2):
                    unpack(part[b, kv], kv, at, block_tok)
                return carry

            lax.fori_loop(0, size, block, 0)
            base += size * block_tok
        for piece in range(suffix // block_tok):
            for kv in range(2):
                unpack(
                    new_ref[kv, pl.ds(piece * block_tok * kv_dev, block_tok * kv_dev), :],
                    kv,
                    base + piece * block_tok,
                    block_tok,
                )

    def run(masked):
        tok_rows = rows // group

        def sub(index, carry):
            tok = pl.multiple_of(index * tok_rows, tok_rows)
            q_all = q_ref[pl.ds(tok, tok_rows)].astype(jnp.float32)
            results = []
            for h in range(kv_dev):
                q = (
                    q_all[:, h * group : (h + 1) * group, :]
                    .reshape(rows, head_dim)
                    .astype(jnp.bfloat16)
                )
                scores = (
                    lax.dot_general(
                        q, key_ref[h], (((1,), (1,)), ((), ())), preferred_element_type=jnp.float32
                    )
                    * factor
                )
                if masked or first:
                    column = lax.broadcasted_iota(jnp.int32, (1, keys), 1)
                    allowed = jnp.zeros((1, keys), jnp.bool_)
                    base = 0
                    for i, size in enumerate(sizes):
                        allowed |= (column >= base) & (
                            column < base + jnp.minimum(valid_ref[0, i], size) * block_tok
                        )
                        base += size * block_tok
                    if first:
                        place = (
                            lax.broadcasted_iota(jnp.int32, (rows, 1), 0) // group
                            + tok
                            + tile * tile_tok
                        )
                        limit = place + prefix_keys
                        allowed = allowed | ((column >= prefix_keys) & (column <= limit))
                    scores = jnp.where(allowed, scores, -jnp.inf)
                peak = jnp.max(scores, axis=1, keepdims=True)
                at = pl.ds(pl.multiple_of(index * rows, rows), rows)
                if not first:
                    old = stat_in[h, at, 0:1]
                    old_total = stat_in[h, at, head_dim // 2 : head_dim // 2 + 1]
                    peak = jnp.maximum(peak, old)
                weights = jnp.exp2(scores - peak).astype(jnp.bfloat16)
                both = jnp.dot(weights, value_ref[h], preferred_element_type=jnp.float32)
                summed = both[:, :head_dim]
                total = both[:, head_dim:]
                if not first:
                    shrink = jnp.exp2(old - peak)
                    summed += acc_in[h, at, :] * shrink
                    total += old_total * shrink
                if final:
                    results.append((summed / total).reshape(tok_rows, group, head_dim))
                else:
                    acc_out[h, at, :] = summed
                    lane = lax.broadcasted_iota(jnp.int32, (rows, head_dim), 1)
                    stat_out[h, at, :] = jnp.where(lane < head_dim // 2, peak, total)
            if final:
                out_ref[pl.ds(tok, tok_rows)] = jnp.concatenate(results, axis=1).astype(
                    jnp.bfloat16
                )
            return carry

        lax.fori_loop(0, tile_tok // tok_rows, sub, 0)

    if first:
        run(True)
    else:
        full = valid_ref[0, 0] >= sizes[0]
        for i in range(1, len(sizes)):
            full = full & (valid_ref[0, i] >= sizes[i])

        @pl.when(full)
        def unmasked():
            run(False)

        @pl.when(jnp.logical_not(full))
        def masked():
            run(True)


def attend(valid, queries, parts, new_kv, state, final):
    suffix, heads_dev, head_dim = queries.shape
    kv_dev = parts[0].shape[3]
    block_tok = parts[0].shape[2]
    group = heads_dev // kv_dev
    sizes = tuple(part.shape[0] for part in parts)
    first = state is None
    tile_tok = min(suffix, 64)
    rows = min(256, tile_tok * group)
    keys = sum(sizes) * block_tok + (suffix if first else 0)
    raw = [part.reshape(part.shape[0], 2, block_tok * kv_dev, head_dim) for part in parts]
    whole = pl.BlockSpec(memory_space=pltpu.VMEM)
    q_spec = pl.BlockSpec((tile_tok, heads_dev, head_dim), lambda t: (t, 0, 0))
    state_spec = pl.BlockSpec((kv_dev, tile_tok * group, head_dim), lambda t: (0, t, 0))
    state_shape = jax.ShapeDtypeStruct((kv_dev, suffix * group, head_dim), jnp.float32)
    if first:
        extra, extra_specs = [new_kv.reshape(2, suffix * kv_dev, head_dim)], [whole]
    else:
        extra, extra_specs = list(state), [state_spec] * 2
    if final:
        out_shape = jax.ShapeDtypeStruct(queries.shape, queries.dtype)
        out_specs = q_spec
    else:
        out_shape = [state_shape] * 2
        out_specs = [state_spec] * 2
    return pl.pallas_call(
        functools.partial(
            attend_kernel, sizes, kv_dev, group, block_tok, rows, first, final
        ),
        out_shape=out_shape,
        grid=(suffix // tile_tok,),
        in_specs=[SMEM, q_spec] + [whole] * len(raw) + extra_specs,
        out_specs=out_specs,
        scratch_shapes=[
            pltpu.VMEM((kv_dev, keys, head_dim), jnp.bfloat16),
            pltpu.VMEM((kv_dev, keys, 2 * head_dim), jnp.bfloat16),
            pltpu.VMEM((block_tok * kv_dev, head_dim), jnp.float32),
        ],
        compiler_params=pltpu.CompilerParams(vmem_limit_bytes=VMEM_LIMIT),
        cost_estimate=pl.CostEstimate(
            flops=4 * suffix * heads_dev * keys * head_dim,
            bytes_accessed=keys * kv_dev * head_dim * 4 + 16 * suffix * heads_dev * head_dim,
            transcendentals=suffix * heads_dev * keys,
        ),
    )(valid, queries, *raw, *extra)


def per_device(
    queries, new_kv, pool, prefix_slot, prefix_owner, prefix_len, write_slot, write_owner
):
    num_blk = lax.axis_size("blk")
    me = lax.axis_index("blk")
    pool_dev, block_tok = pool.shape[0], pool.shape[2]
    prefix_blocks = prefix_slot.shape[1]
    new_count = write_slot.shape[1]
    capacity = max(2, (prefix_blocks + num_blk - 1) // num_blk)

    def shift(array, d):
        return lax.ppermute(array, "blk", [(i, (i + d) % num_blk) for i in range(num_blk)])

    meta = jnp.concatenate(
        [prefix_owner * pool_dev + prefix_slot, write_owner * pool_dev + write_slot], axis=1
    )
    metas = [meta] + [shift(meta, num_blk - d) for d in range(1, num_blk)]

    fresh_shape = jax.ShapeDtypeStruct((2,) + pool.shape[2:], pool.dtype)
    fresh_out = pl.pallas_call(
        functools.partial(pick_fresh_kernel, num_blk, block_tok),
        out_shape=[fresh_shape] * (num_blk - 1),
        in_specs=[SMEM, HBM],
        out_specs=[HBM] * (num_blk - 1),
        scratch_shapes=[pltpu.SemaphoreType.DMA((num_blk - 1, 2))],
    )(write_owner, new_kv)
    arrived_fresh = {d: shift(fresh_out[d - 1], d) for d in range(1, num_blk)}

    half = capacity // 2
    sizes = (half, capacity - half)
    outgoing = gather(metas[1:], pool, (sizes,) * (num_blk - 1), capacity, prefix_blocks)
    order = sorted(range(1, num_blk), key=lambda d: -min(d, num_blk - d))
    arrived = {}
    for c in range(len(sizes)):
        for d in order:
            arrived[c, d] = shift(outgoing[(d - 1) * len(sizes) + c], d)

    places = jnp.arange(prefix_blocks, dtype=jnp.int32)[None, :]
    sources = lax.rem(me - jnp.arange(num_blk, dtype=jnp.int32) + num_blk, num_blk)[:, None]
    counted = jnp.sum(
        ((prefix_owner == sources) & (places < prefix_len[:, None])).astype(jnp.int32), axis=1
    )

    def valid(keys):
        return jnp.stack([counted[d] - sum(sizes[:c]) for c, d in keys])[None, :]

    (local,) = gather(metas[:1], pool, ((capacity,),), capacity, prefix_blocks)
    state = attend(counted[0][None, None], queries[0], [local], new_kv, None, False)
    new_pool = write_back(
        metas,
        pool,
        new_kv,
        [arrived_fresh[num_blk - d] for d in range(1, num_blk)],
        prefix_blocks,
        new_count,
    )
    calls = []
    for c in range(len(sizes)):
        calls.append([(c, order[0])])
        rest = [(c, d) for d in order[1:]]
        calls += [rest[i : i + 4] for i in range(0, len(rest), 4)]
    calls = [call for call in calls if call]
    for i, call in enumerate(calls):
        state = attend(
            valid(call), queries[0], [arrived[k] for k in call], None, state, i == len(calls) - 1
        )
    return state[None], new_pool


def solution(mesh):
    in_specs = (
        P(("group", "blk"), None, "tensor", None),
        P(None, ("group", "blk"), None, "tensor", None),
        P(("group", "blk"), None, None, "tensor", None),
        P(("group", "blk"), None),
        P(("group", "blk"), None),
        P(("group", "blk")),
        P(("group", "blk"), None),
        P(("group", "blk"), None),
    )
    out_specs = (
        P(("group", "blk"), None, "tensor", None),
        P(("group", "blk"), None, None, "tensor", None),
    )
    return jax.shard_map(
        per_device, mesh=mesh, in_specs=in_specs, out_specs=out_specs, check_vma=False
    )
```

time: 273 us -> 356 us (1.30)
  the two profiles are of different devices: /device:TPU:0 before, /device:TPU:14 now
where the time goes in v1:
time: 356 us; the launch traced here: 352 us
  Pallas kernels  317 us (89%)
  starting transfers between devices  17.4 us (5%)
  local copies, waits for them, and re-layouts  11 us (3%)
    pallas_call x2, Pallas kernels, gather(): pl.pallas_call(functools.partial(gather_kernel, plan, pool_dev, prefix_bl...  132 us
    pallas_call x1, Pallas kernels, write_back(): pl.pallas_call(functools.partial(write_back_kernel, num_blk, prefix_block...  110 us
    pallas_call x5, Pallas kernels, attend(): pl.pallas_call(functools.partial(attend_kernel, sizes, kv_dev, group, blo...  62.5 us
    ppermute x12, starting transfers between devices, shift(): lax.ppermute(array, 'blk', [(i, (i + d) % num_blk) for i in range(num_blk)])  17.4 us
    pallas_call x1, Pallas kernels, per_device(): pl.pallas_call(functools.partial(pick_fresh_kernel, num_blk, block_tok),...  13.7 us
    unnamed x32, local copies, waits for them, and re-layouts  10.3 us
  transfers between devices with their start and end apart: 12, of which 0 were waited for; matrix products, arithmetic and copies ran while one was open for 1% of the time, Pallas kernels for 86%

profile of v1, /device:TPU:14, one launch (start us, length us, event | category | flops | bytes accessed | tf_op | source)
XLA Modules:
  0.0 352.1 jit_solution(16223859325034996544)
XLA Ops:
  0.6 0.0 copy-start.15
  0.6 0.7 multiply_add_fusion
  1.3 0.7 multiply_add_fusion.1
  2.0 0.1 pad_add_fusion.refs_0_
  2.1 0.4 collective-permute-start
  2.5 2.6 collective-permute-start.1
  5.1 2.5 collective-permute-start.2
  7.6 13.7 %shard_map.102 = (bf16[2,128,2,128]{3,2,1,0:T(2,128)(2,1)}, bf16[2,128,2,128]{3,2,1,0:T(2,128)(2,1)}, bf16[2,128,2,128]{3,2,1,0:T(2,128)(2,1)}) custom-call(s32[1,2]{1,0:T(1,128)} %owner_ref.1, bf16[2,1,256,2,128]{4,3,2,1,0:T(2,128)(2,1)} %refs_5_.1), custom_call_target="tpu_custom_call" | custom-call | tf_op jit(solution)/shard_map/pallas_call | solution.py:345
  21.3 1.0 collective-permute-start.10
  22.3 0.1 collective-permute-start.11
  23.1 2.0 collective-permute-start.9
  25.1 0.0 collective-permute-done.1.refs_1_.refs_2_
  25.1 0.0 collective-permute-done.2.refs_2_.refs_3_
  25.1 0.5 copy-done.13
  25.6 0.6 copy-done.14
  26.2 97.6 %shard_map.95 = (bf16[4,2,128,2,128]{4,3,2,1,0:T(2,128)(2,1)}, bf16[4,2,128,2,128]{4,3,2,1,0:T(2,128)(2,1)}, bf16[4,2,128,2,128]{4,3,2,1,0:T(2,128)(2,1)}, bf16[...) custom-call(s32[1,34]{1,0:T(1,128)} %copy-done.12, ...), custom_call_target="tpu_custom_call" | custom-call | bytes 6291456 | tf_op jit(solution)/shard_map/pallas_call | solution.py:82
  123.7 2.1 collective-permute-start.8
  125.8 0.2 convert_reduce_fusion
  126.0 0.0 copy-start
  126.0 0.0 copy-start.4
  126.0 34.0 %shard_map.96 = bf16[8,2,128,2,128]{4,3,2,1,0:T(2,128)(2,1)} custom-call(s32[1,34]{1,0:T(1,128)} %copy-done.11, bf16[24,2,128,2,128]{4,3,2,1,0:T(2,128)(2,1)} %refs_4_.1), custom_call_target="tpu_custom_call" | custom-call | bytes 2097152 | tf_op jit(solution)/shard_map/pallas_call | solution.py:82
  160.1 0.6 fusion.1
  160.7 0.4 collective-permute-start.7
  161.1 1.7 collective-permute-start.6
  162.8 1.2 copy-done.3
  164.0 13.8 %shard_map.97 = (f32[2,2048,128]{2,1,0:T(8,128)S(1)}, f32[2,2048,128]{2,1,0:T(8,128)}) custom-call(s32[1,1]{1,0:T(1,128)} %bitcast.13.valid_ref, bf16[256,16,128]{2,1,0:T(8,128)(2,1)S(1)} %bitcast.20, bf16[8,2,256,128]{3,2,1,0:T(8,128)(2,1)S(1)} %bitcast.25, bf16[2,512,128]{2,1,0:T(8,128)(2,1)S(1)} %bitcast.26), custom_call_target="tpu_custom_call" | custom-call | flops 2684354560 | bytes 9699328 | tf_op jit(solution)/shard_map/pallas_call | solution.py:304
  177.8 1.3 copy-done.1
  179.1 0.0 collective-permute-done.11.refs_8_
  179.1 0.7 copy-done.9
  179.8 2.7 collective-permute-start.5
  182.5 0.0 collective-permute-done.9.refs_6_
  182.5 0.7 copy-done.10
  183.1 0.0 collective-permute-start.3
  183.1 2.0 collective-permute-start.4
  185.2 1.3 add_bitcast_fusion.1.valid_ref
  188.3 0.1 add_bitcast_fusion.valid_ref
  188.4 109.6 %shard_map.103 = bf16[24,2,128,2,128]{4,3,2,1,0:T(2,128)(2,1)} custom-call(s32[1,34]{1,0:T(1,128)} %copy-done.11, s32[1,34]{1,0:T(1,128)} %copy-done.12, s32[1,34]{1,0:T(1,128)} %copy-done.13, s32[1,34]{1,0:T(1,128)} %copy-done.14, bf16[24,2,128,2,128]{4,3,2,1,0:T(2,128)(2,1)} %refs_4_.1, bf16[2,1,256,2,128]{4,3,2,1,0:T(2,128)(2,1)} %refs_5_.1, ...), custom_call_target="tpu_custom_call" | custom-call | bytes 6291456 | tf_op jit(solution)/shard_map/pallas_call | solution.py:127
  298.0 11.5 %shard_map.98 = (f32[2,2048,128]{2,1,0:T(8,128)S(1)}, f32[2,2048,128]{2,1,0:T(8,128)S(1)}) custom-call(s32[1,1]{1,0:T(1,128)} %bitcast.11.valid_ref, bf16[256,16,128]{2,1,0:T(8,128)(2,1)S(1)} %bitcast.21, bf16[4,2,256,128]{3,2,1,0:T(8,128)(2,1)S(1)} %bitcast.27, f32[2,2048,128]{2,1,0:T(8,128)} %copy-done.1, f32[2,2048,128]{2,1,0:T(8,128)} %get-tuple-element.26.refs_2_), custom_call_target="tpu_custom_call" | custom-call | flops 1073741824 | bytes 8912896 | tf_op jit(solution)/shard_map/pallas_call | solution.py:304
  309.6 1.3 copy-done.5
  310.9 1.4 copy-done.6
  312.3 0.0 collective-permute-done.7
  312.3 0.0 collective-permute-done.6
  312.3 13.2 %shard_map.99 = (f32[2,2048,128]{2,1,0:T(8,128)S(1)}, f32[2,2048,128]{2,1,0:T(8,128)}) custom-call(s32[1,2]{1,0:T(1,128)S(1)} %add_bitcast_fusion.1.valid_ref, bf16[256,16,128]{2,1,0:T(8,128)(2,1)S(1)} %bitcast.22, bf16[4,2,256,128]{3,2,1,0:T(8,128)(2,1)} %bitcast.9.refs_0_, bf16[4,2,256,128]{3,2,1,0:T(8,128)(2,1)S(1)} %bitcast.29, ...), custom_call_target="tpu_custom_call" | custom-call | flops 2147483648 | bytes 9437184 | tf_op jit(solution)/shard_map/pallas_call | solution.py:304
  325.5 1.3 copy-done.2
  326.8 0.0 collective-permute-done.5
  326.8 11.0 %shard_map.100 = (f32[2,2048,128]{2,1,0:T(8,128)S(1)}, f32[2,2048,128]{2,1,0:T(8,128)S(1)}) custom-call(s32[1,1]{1,0:T(1,128)} %bitcast.6.valid_ref, bf16[256,16,128]{2,1,0:T(8,128)(2,1)S(1)} %bitcast.23, bf16[4,2,256,128]{3,2,1,0:T(8,128)(2,1)S(1)} %bitcast.28, f32[2,2048,128]{2,1,0:T(8,128)} %copy-done.2, f32[2,2048,128]{2,1,0:T(8,128)} %get-tuple-element.30.refs_2_), custom_call_target="tpu_custom_call" | custom-call | flops 1073741824 | bytes 8912896 | tf_op jit(solution)/shard_map/pallas_call | solution.py:304
  337.8 1.4 copy-done.7
  339.2 12.9 %shard_map.101 = bf16[256,16,128]{2,1,0:T(8,128)(2,1)} custom-call(s32[1,2]{1,0:T(1,128)S(1)} %add_bitcast_fusion.valid_ref, bf16[256,16,128]{2,1,0:T(8,128)(2,1)S(1)} %bitcast.24, bf16[4,2,256,128]{3,2,1,0:T(8,128)(2,1)S(1)} %bitcast.30, bf16[4,2,256,128]{3,2,1,0:T(8,128)(2,1)} %bitcast.5.refs_1_, f32[2,2048,128]{2,1,0:T(8,128)S(1)} %get-tuple-element.31.refs_2_, ...), custom_call_target="tpu_custom_call" | custom-call | flops 2147483648 | bytes 9437184 | tf_op jit(solution)/shard_map/pallas_call | solution.py:304
  (26 shorter events, 0.1 us)
Async XLA Ops:
  0.6 125.2 %copy-start.15 = (s32[1,32]{1,0:T(1,128)S(1)}, s32[1,32]{1,0:T(1,128)}, u32[]{:S(2)}) copy-start(s32[1,32]{1,0:T(1,128)} %param.12) | copy-start | bytes 388
  2.1 123.9 %copy-start.11 = (s32[1,34]{1,0:T(1,128)}, s32[1,34]{1,0:T(1,128)S(1)}, u32[]{:S(2)}) copy-start(s32[1,34]{1,0:T(1,128)S(1)} %pad_add_fusion.refs_0_) | copy-start | bytes 412
  2.1 21.0 %collective-permute-start = (s32[1,34]{1,0:T(1,128)S(1)}, s32[1,34]{1,0:T(1,128)S(1)}, u32[]{:S(2)}, u32[]{:S(2)}) collective-permute-start(s32[1,34]{1,0:T(1,128)S(1)} %pad_add_fusion.refs_0_), channel_id=1, source_target_pairs={{0,12},{4,0},{8,4},{12,8},{1,13},{5,1},{9,5},{13,9},{2,14},{6,2},{... | collective-permute-start | bytes 416 | tf_op jit(solution)/shard_map/ppermute | solution.py:337
  2.5 22.5 %collective-permute-start.1 = (s32[1,34]{1,0:T(1,128)S(1)}, s32[1,34]{1,0:T(1,128)S(1)}, u32[]{:S(2)}, u32[]{:S(2)}) collective-permute-start(s32[1,34]{1,0:T(1,128)S(1)} %pad_add_fusion.refs_0_), channel_id=1, source_target_pairs={{0,8},{4,12},{8,0},{12,4},{1,9},{5,13},{9,1},{13,5},{2,10},{6,14},... | collective-permute-start | bytes 416 | tf_op jit(solution)/shard_map/ppermute | solution.py:337
  5.1 20.0 %collective-permute-start.2 = (s32[1,34]{1,0:T(1,128)S(1)}, s32[1,34]{1,0:T(1,128)S(1)}, u32[]{:S(2)}, u32[]{:S(2)}) collective-permute-start(s32[1,34]{1,0:T(1,128)S(1)} %pad_add_fusion.refs_0_), channel_id=1, source_target_pairs={{0,4},{4,8},{8,12},{12,0},{1,5},{5,9},{9,13},{13,1},{2,6},{6,10},{... | collective-permute-start | bytes 416 | tf_op jit(solution)/shard_map/ppermute | solution.py:337
  21.3 139.7 %collective-permute-start.10 = (bf16[2,128,2,128]{3,2,1,0:T(2,128)(2,1)}, bf16[2,128,2,128]{3,2,1,0:T(2,128)(2,1)S(1)}, u32[]{:S(2)}, u32[]{:S(2)}) collective-permute-start(bf16[2,128,2,128]{3,2,1,0:T(2,128)(2,1)} %get-tuple-element.34), channel_id=1, source_target_pairs={{0,8},{4,12},{8,0},{12,4},{1,9},{5,13},{9,1},{13,5},{2,10},{6,14},... | collective-permute-start | bytes 393224 | tf_op jit(solution)/shard_map/ppermute | solution.py:337
  22.3 156.8 %collective-permute-start.11 = (bf16[2,128,2,128]{3,2,1,0:T(2,128)(2,1)}, bf16[2,128,2,128]{3,2,1,0:T(2,128)(2,1)S(1)}, u32[]{:S(2)}, u32[]{:S(2)}) collective-permute-start(bf16[2,128,2,128]{3,2,1,0:T(2,128)(2,1)} %get-tuple-element.35), channel_id=1, source_target_pairs={{0,4},{4,8},{8,12},{12,0},{1,5},{5,9},{9,13},{13,1},{2,6},{6,10},{... | collective-permute-start | bytes 393224 | tf_op jit(solution)/shard_map/ppermute | solution.py:337
  23.1 2.0 copy-start.12
  23.1 159.4 %collective-permute-start.9 = (bf16[2,128,2,128]{3,2,1,0:T(2,128)(2,1)}, bf16[2,128,2,128]{3,2,1,0:T(2,128)(2,1)S(1)}, u32[]{:S(2)}, u32[]{:S(2)}) collective-permute-start(bf16[2,128,2,128]{3,2,1,0:T(2,128)(2,1)} %get-tuple-element.33), channel_id=1, source_target_pairs={{0,12},{4,0},{8,4},{12,8},{1,13},{5,1},{9,5},{13,9},{2,14},{6,2},{... | collective-permute-start | bytes 393224 | tf_op jit(solution)/shard_map/ppermute | solution.py:337
  25.1 0.5 copy-start.13
  25.6 0.6 copy-start.14
  123.7 59.4 %collective-permute-start.8 = (bf16[4,2,128,2,128]{4,3,2,1,0:T(2,128)(2,1)}, bf16[4,2,128,2,128]{4,3,2,1,0:T(2,128)(2,1)S(1)}, u32[]{:S(2)}, u32[]{:S(2)}) collective-permute-start(bf16[4,2,128,2,128]{4,3,2,1,0:T(2,128)(2,1)} %get-tuple-element.24), channel_id=1, source_target_pairs={{0,8},{4,12},{8,0},{12,4},{1,9},{5,13},{9,1},{13,5},{2,10},{6,14},... | collective-permute-start | bytes 1572872 | tf_op jit(solution)/shard_map/ppermute | solution.py:337
  126.0 36.7 %copy-start = (bf16[1,256,16,128]{3,2,1,0:T(8,128)(2,1)S(1)}, bf16[1,256,16,128]{3,2,1,0:T(8,128)(2,1)}, u32[]{:S(2)}) copy-start(bf16[1,256,16,128]{3,2,1,0:T(8,128)(2,1)} %param.8) | copy-start | bytes 3145732
  126.0 36.7 %copy-start.4 = (bf16[2,1,256,2,128]{4,3,2,1,0:T(2,128)(2,1)S(1)}, bf16[2,1,256,2,128]{4,3,2,1,0:T(2,128)(2,1)}, u32[]{:S(2)}) copy-start(bf16[2,1,256,2,128]{4,3,2,1,0:T(2,128)(2,1)} %refs_5_.1) | copy-start | bytes 786436
  160.7 151.6 %collective-permute-start.7 = (bf16[4,2,128,2,128]{4,3,2,1,0:T(2,128)(2,1)}, bf16[4,2,128,2,128]{4,3,2,1,0:T(2,128)(2,1)S(1)}, u32[]{:S(2)}, u32[]{:S(2)}) collective-permute-start(bf16[4,2,128,2,128]{4,3,2,1,0:T(2,128)(2,1)} %get-tuple-element.23), channel_id=1, source_target_pairs={{0,12},{4,0},{8,4},{12,8},{1,13},{5,1},{9,5},{13,9},{2,14},{6,2},{... | collective-permute-start | bytes 1572872 | tf_op jit(solution)/shard_map/ppermute | solution.py:337
  161.1 16.7 %copy-start.8 = (bf16[2,128,2,128]{3,2,1,0:T(2,128)(2,1)}, bf16[2,128,2,128]{3,2,1,0:T(2,128)(2,1)S(1)}, u32[]{:S(2)}) copy-start(bf16[2,128,2,128]{3,2,1,0:T(2,128)(2,1)S(1)} %collective-permute-done.10.refs_7_) | copy-start | bytes 393220
  161.1 151.2 %collective-permute-start.6 = (bf16[4,2,128,2,128]{4,3,2,1,0:T(2,128)(2,1)}, bf16[4,2,128,2,128]{4,3,2,1,0:T(2,128)(2,1)}, u32[]{:S(2)}, u32[]{:S(2)}) collective-permute-start(bf16[4,2,128,2,128]{4,3,2,1,0:T(2,128)(2,1)} %get-tuple-element.22), channel_id=1, source_target_pairs={{0,4},{4,8},{8,12},{12,0},{1,5},{5,9},{9,13},{13,1},{2,6},{6,10},{... | collective-permute-start | bytes 1572872 | tf_op jit(solution)/shard_map/ppermute | solution.py:337
  162.8 1.2 copy-start.3
  177.8 1.3 copy-start.1
  179.1 0.7 copy-start.9
  179.8 147.1 %collective-permute-start.5 = (bf16[4,2,128,2,128]{4,3,2,1,0:T(2,128)(2,1)}, bf16[4,2,128,2,128]{4,3,2,1,0:T(2,128)(2,1)S(1)}, u32[]{:S(2)}, u32[]{:S(2)}) collective-permute-start(bf16[4,2,128,2,128]{4,3,2,1,0:T(2,128)(2,1)} %get-tuple-element.21), channel_id=1, source_target_pairs={{0,8},{4,12},{8,0},{12,4},{1,9},{5,13},{9,1},{13,5},{2,10},{6,14},... | collective-permute-start | bytes 1572872 | tf_op jit(solution)/shard_map/ppermute | solution.py:337
  182.5 0.7 copy-start.10
  183.1 156.1 %collective-permute-start.3 = (bf16[4,2,128,2,128]{4,3,2,1,0:T(2,128)(2,1)}, bf16[4,2,128,2,128]{4,3,2,1,0:T(2,128)(2,1)S(1)}, u32[]{:S(2)}, u32[]{:S(2)}) collective-permute-start(bf16[4,2,128,2,128]{4,3,2,1,0:T(2,128)(2,1)} %get-tuple-element.19), channel_id=1, source_target_pairs={{0,4},{4,8},{8,12},{12,0},{1,5},{5,9},{9,13},{13,1},{2,6},{6,10},{... | collective-permute-start | bytes 1572872 | tf_op jit(solution)/shard_map/ppermute | solution.py:337
  183.1 156.1 %collective-permute-start.4 = (bf16[4,2,128,2,128]{4,3,2,1,0:T(2,128)(2,1)}, bf16[4,2,128,2,128]{4,3,2,1,0:T(2,128)(2,1)}, u32[]{:S(2)}, u32[]{:S(2)}) collective-permute-start(bf16[4,2,128,2,128]{4,3,2,1,0:T(2,128)(2,1)} %get-tuple-element.20), channel_id=1, source_target_pairs={{0,12},{4,0},{8,4},{12,8},{1,13},{5,1},{9,5},{13,9},{2,14},{6,2},{... | collective-permute-start | bytes 1572872 | tf_op jit(solution)/shard_map/ppermute | solution.py:337
  309.6 1.3 copy-start.5
  310.9 1.4 copy-start.6
  325.5 1.3 copy-start.2
  337.8 1.4 copy-start.7

commit v2 on v0

v2 whole, which is shorter than its diff:
```python
import functools
import math

import jax
import jax.numpy as jnp
from jax import lax
from jax.experimental import pallas as pl
from jax.experimental.pallas import tpu as pltpu
from jax.sharding import PartitionSpec as P

ANY = pl.BlockSpec(memory_space=pl.ANY)
HBM = pl.BlockSpec(memory_space=pltpu.HBM)
SMEM = pl.BlockSpec(memory_space=pltpu.SMEM)
VMEM = pl.BlockSpec(memory_space=pltpu.VMEM)
WHOLE_LIMIT = 60 * 1024 * 1024
VMEM_LIMIT = 16 * 1024 * 1024
ATTEND_LIMIT = 32 * 1024 * 1024
QUERY_ROWS = 1024
LEVELS = (3, 2, 2, 1)


def prepare_kernel(capacity, *refs):
    sources, refs = refs[:5], refs[5:]
    num_blk = refs[0].shape[1] // 2
    count_ref, asked, refs = refs[0], refs[1 : 1 + num_blk], refs[1 + num_blk :]
    held, (table_ref, used_ref, counted_ref, load_sems) = refs[:5], refs[5:]
    loads = [
        pltpu.make_async_copy(source, target, load_sems.at[i])
        for i, (source, target) in enumerate(zip(sources, held))
    ]
    for load in loads:
        load.start()
    slot_ref, owner_ref, len_ref, write_slot_ref, write_owner_ref = held
    me = lax.axis_index("blk")
    for owner in range(num_blk):
        used_ref[owner] = 0
        counted_ref[owner] = 0
        for k in range(capacity):
            table_ref[owner, k] = 0
    for load in loads:
        load.wait()

    def step(j, carry):
        owner = owner_ref[0, j]
        place = used_ref[owner]
        table_ref[owner, jnp.minimum(place, capacity)] = slot_ref[0, j]
        used_ref[owner] = place + 1
        counted_ref[owner] += jnp.where(j < len_ref[0], 1, 0)
        return carry

    lax.fori_loop(0, owner_ref.shape[1], step, 0, unroll=8)
    for d in range(num_blk):
        owner = lax.rem(me + d, num_blk)
        count_ref[0, d] = counted_ref[owner]
        for k in range(capacity):
            asked[d][0, k] = table_ref[owner, k]
        slot = jnp.int32(-1)
        chosen = jnp.int32(0)
        for b in range(write_owner_ref.shape[1]):
            goes = write_owner_ref[0, b] == owner
            slot = jnp.where(goes, write_slot_ref[0, b], slot)
            chosen = jnp.where(goes, b, chosen)
        asked[d][0, capacity] = slot
        count_ref[0, num_blk + d] = chosen


def prepare(prefix_slot, prefix_owner, prefix_len, write_slot, write_owner, capacity, num_blk):
    operands = (prefix_slot, prefix_owner, prefix_len, write_slot, write_owner)
    row = jax.ShapeDtypeStruct((1, capacity + 1), jnp.int32)
    results = pl.pallas_call(
        functools.partial(prepare_kernel, capacity),
        out_shape=[jax.ShapeDtypeStruct((1, 2 * num_blk), jnp.int32)] + [row] * num_blk,
        in_specs=[HBM] * 5,
        out_specs=[SMEM] * (num_blk + 1),
        scratch_shapes=[pltpu.SMEM(operand.shape, operand.dtype) for operand in operands]
        + [
            pltpu.SMEM((num_blk, capacity + 1), jnp.int32),
            pltpu.SMEM((num_blk,), jnp.int32),
            pltpu.SMEM((num_blk,), jnp.int32),
            pltpu.SemaphoreType.DMA((5,)),
        ],
        compiler_params=pltpu.CompilerParams(vmem_limit_bytes=WHOLE_LIMIT),
    )(*operands)
    return results[0], results[1:]


def pick_fresh_kernel(num_blk, block_rows, count_ref, new_ref, *refs):
    fresh, (held, load_sem, sems) = refs[: num_blk - 1], refs[num_blk - 1 :]
    load = pltpu.make_async_copy(new_ref, held, load_sem)
    load.start()
    load.wait()
    copies = []
    for d in range(1, num_blk):
        chosen = count_ref[0, num_blk + d]
        at = pl.ds(pl.multiple_of(chosen * block_rows, block_rows), block_rows)
        copies.append(pltpu.make_async_copy(held.at[:, at], fresh[d - 1], sems.at[d - 1]))
    for copy in copies:
        copy.start()
    for copy in copies:
        copy.wait()


def pick_fresh(counts, new_rows, block_rows, num_blk):
    shape = jax.ShapeDtypeStruct((2, block_rows, new_rows.shape[2]), new_rows.dtype)
    return pl.pallas_call(
        functools.partial(pick_fresh_kernel, num_blk, block_rows),
        out_shape=[shape] * (num_blk - 1),
        in_specs=[SMEM, HBM],
        out_specs=[HBM] * (num_blk - 1),
        scratch_shapes=[
            pltpu.VMEM(new_rows.shape, new_rows.dtype),
            pltpu.SemaphoreType.DMA,
            pltpu.SemaphoreType.DMA((num_blk - 1,)),
        ],
        compiler_params=pltpu.CompilerParams(vmem_limit_bytes=VMEM_LIMIT),
    )(counts, new_rows)


def gather_kernel(plan, count, *refs):
    asked, pool_ref, refs = refs[:count], refs[count], refs[-len(plan) - 3 :]
    outs, held, in_sems, out_sems = refs[:-3], refs[-3], refs[-2], refs[-1]
    moves = []
    for (row, start, size), out in zip(plan, outs):
        for place in range(size):
            i = len(moves)
            load = pltpu.make_async_copy(
                pool_ref.at[asked[row][0, start + place]], held.at[i], in_sems.at[i]
            )
            moves.append((load, pltpu.make_async_copy(held.at[i], out.at[place], out_sems.at[i])))
            load.start()
    for load, store in moves:
        load.wait()
        store.start()
    for load, store in moves:
        store.wait()


def gather(asked, pool, plan, after=()):
    shapes = [jax.ShapeDtypeStruct((size,) + pool.shape[1:], pool.dtype) for _, _, size in plan]
    blocks = sum(size for _, _, size in plan)
    return pl.pallas_call(
        functools.partial(gather_kernel, plan, len(asked)),
        out_shape=shapes,
        in_specs=[SMEM] * len(asked) + [HBM] + [ANY] * len(after),
        out_specs=[HBM] * len(shapes),
        scratch_shapes=[
            pltpu.VMEM((blocks,) + pool.shape[1:], pool.dtype),
            pltpu.SemaphoreType.DMA((blocks,)),
            pltpu.SemaphoreType.DMA((blocks,)),
        ],
        compiler_params=pltpu.CompilerParams(vmem_limit_bytes=VMEM_LIMIT),
        cost_estimate=pl.CostEstimate(
            flops=0, bytes_accessed=4 * blocks * math.prod(pool.shape[1:]), transcendentals=0
        ),
    )(*asked, pool, *after)


def write_back_kernel(capacity, block_rows, count, owner_ref, slot_ref, *refs):
    asked, refs = refs[:count], refs[count:]
    pool_ref, new_ref, refs = refs[0], refs[1], refs[2:]
    fresh, (out_ref, held, sems, last) = refs[:count], refs[-4:]
    me = lax.axis_index("blk")
    blocks = range(pool_ref.shape[0])
    loads = [pltpu.make_async_copy(pool_ref.at[b], held.at[b], sems.at[b]) for b in blocks]
    stores = [pltpu.make_async_copy(held.at[b], out_ref.at[b], sems.at[b]) for b in blocks]
    for load in loads:
        load.start()
    for load in loads:
        load.wait()

    def put(wanted, src, slot):
        @pl.when(wanted)
        def write():
            copy = pltpu.make_async_copy(src, held.at[slot], last)
            copy.start()
            copy.wait()

    for i in range(count):
        slot = asked[i][0, capacity]
        put(slot >= 0, fresh[i], slot)
    for b in range(owner_ref.shape[1]):
        rows = pl.ds(b * block_rows, block_rows)
        put(owner_ref[0, b] == me, new_ref.at[:, rows], slot_ref[0, b])
    for store in stores:
        store.start()
    for store in stores:
        store.wait()


def write_back(write_owner, write_slot, asked, pool, new_rows, fresh, capacity, after):
    count = len(asked)
    return pl.pallas_call(
        functools.partial(write_back_kernel, capacity, pool.shape[2], count),
        out_shape=jax.ShapeDtypeStruct(pool.shape, pool.dtype),
        in_specs=[SMEM] * (count + 2) + [HBM] * (count + 2) + [ANY] * len(after),
        out_specs=HBM,
        scratch_shapes=[
            pltpu.VMEM(pool.shape, pool.dtype),
            pltpu.SemaphoreType.DMA((pool.shape[0],)),
            pltpu.SemaphoreType.DMA,
        ],
        compiler_params=pltpu.CompilerParams(vmem_limit_bytes=VMEM_LIMIT),
        cost_estimate=pl.CostEstimate(
            flops=0, bytes_accessed=4 * math.prod(pool.shape), transcendentals=0
        ),
    )(write_owner, write_slot, *asked, pool, new_rows, *fresh, *after)


def attend_kernel(spans, kv_dev, group, block_tok, rows, first, final, count_ref, q_ref, *refs):
    parts, refs = refs[: len(spans)], refs[len(spans) :]
    if first:
        new_ref, q_out, acc_out, stat_out = refs[:4]
        head_dim = q_ref.shape[2]
        suffix = new_ref.shape[1] // kv_dev
    else:
        acc_in, stat_in = refs[:2]
        head_dim = q_ref.shape[2]
        suffix = 0
        if final:
            out_ref = refs[2]
        else:
            acc_out, stat_out = refs[2:4]
    key_ref, value_ref, stage_ref = refs[-3:]
    factor = head_dim**-0.5 * math.log2(math.e)
    prefix_keys = sum(size for _, _, size in spans) * block_tok
    keys = prefix_keys + suffix

    def unpack(raw, kv, at):
        stage_ref[...] = raw.astype(jnp.float32)
        for h in range(kv_dev):
            head = stage_ref[pl.ds(h, block_tok, stride=kv_dev), :]
            if kv == 0:
                key_ref[h, pl.ds(at, block_tok)] = head.astype(jnp.bfloat16)
            else:
                value_ref[h, :head_dim, pl.ds(at, block_tok)] = head.T.astype(jnp.bfloat16)

    value_ref[:, head_dim:, :] = jnp.ones(
        (kv_dev, value_ref.shape[1] - head_dim, keys), jnp.bfloat16
    )
    base = 0
    for part, (_, _, size) in zip(parts, spans):
        for b in range(size):
            for kv in range(2):
                unpack(part[b, kv], kv, base + b * block_tok)
        base += size * block_tok
    for piece in range(suffix // block_tok):
        for kv in range(2):
            raw = new_ref[kv, pl.ds(piece * block_tok * kv_dev, block_tok * kv_dev), :]
            unpack(raw, kv, base + piece * block_tok)

    if first:
        for h in range(kv_dev):
            heads = q_ref[...].astype(jnp.float32)[:, h * group : (h + 1) * group, :]
            q_out[h] = heads.reshape(-1, head_dim).astype(jnp.bfloat16)
        q_rows = q_out
    else:
        q_rows = q_ref

    def run(masked):
        def product(start, stop, h, at):
            return lax.dot_general(
                key_ref[h, start:stop],
                q_rows[h, at],
                (((1,), (1,)), ((), ())),
                preferred_element_type=jnp.float32,
            )

        def sub(index, carry):
            at = pl.ds(pl.multiple_of(index * rows, rows), rows)
            results = []
            for h in range(kv_dev):
                pieces = []
                if spans:
                    scores = product(0, prefix_keys, h, at)
                    if masked:
                        place = lax.broadcasted_iota(jnp.int32, (prefix_keys, 1), 0)
                        allowed = jnp.zeros((prefix_keys, 1), jnp.bool_)
                        base = 0
                        for row, start, size in spans:
                            end = base + jnp.minimum(count_ref[0, row] - start, size) * block_tok
                            allowed |= (place >= base) & (place < end)
                            base += size * block_tok
                        scores = jnp.where(allowed, scores, -jnp.inf)
                    pieces.append((scores, 0))
                if first:
                    scores = product(prefix_keys, keys, h, at)
                    token = lax.broadcasted_iota(jnp.int32, (1, rows), 1) + index * rows
                    place = lax.broadcasted_iota(jnp.int32, (suffix, rows), 0)
                    scores = jnp.where(place * group <= token, scores, -jnp.inf)
                    pieces.append((scores, prefix_keys))
                peak = factor * functools.reduce(
                    jnp.maximum, [jnp.max(scores, axis=0, keepdims=True) for scores, _ in pieces]
                )
                if not first:
                    old = stat_in[h, 0:1, at]
                    peak = jnp.maximum(peak, old)
                both = sum(
                    jnp.dot(
                        value_ref[h, :, start : start + scores.shape[0]],
                        jnp.exp2(scores * factor - peak).astype(jnp.bfloat16),
                        preferred_element_type=jnp.float32,
                    )
                    for scores, start in pieces
                )
                summed = both[:head_dim]
                total = both[head_dim : head_dim + 1]
                if not first:
                    shrink = jnp.exp2(old - peak)
                    summed += acc_in[h, :, at] * shrink
                    total += stat_in[h, 1:2, at] * shrink
                if final:
                    results.append((summed / total).T.reshape(rows // group, group, head_dim))
                else:
                    acc_out[h, :, at] = summed
                    stat_out[h, 0:1, at] = peak
                    stat_out[h, 1:2, at] = total
            if final:
                tok = pl.multiple_of(index * (rows // group), rows // group)
                out_ref[pl.ds(tok, rows // group)] = jnp.concatenate(results, axis=1).astype(
                    jnp.bfloat16
                )
            return carry

        lax.fori_loop(0, q_rows.shape[1] // rows, sub, 0)

    full = functools.reduce(
        jnp.logical_and, [count_ref[0, row] >= start + size for row, start, size in spans]
    )

    @pl.when(full)
    def unmasked():
        run(False)

    @pl.when(jnp.logical_not(full))
    def masked():
        run(True)


def attend(counts, queries, parts, spans, kv_dev, block_tok, new_rows, state, final):
    suffix, heads_dev, head_dim = queries.shape
    group = heads_dev // kv_dev
    first = state is None
    rows = min(QUERY_ROWS, suffix * group)
    keys = sum(size for _, _, size in spans) * block_tok + (suffix if first else 0)
    state_shape = [
        jax.ShapeDtypeStruct((kv_dev, suffix * group, head_dim), jnp.bfloat16),
        jax.ShapeDtypeStruct((kv_dev, head_dim, suffix * group), jnp.float32),
        jax.ShapeDtypeStruct((kv_dev, 8, suffix * group), jnp.float32),
    ]
    if first:
        operands = [queries, *parts, new_rows]
        out_shape = state_shape
    else:
        operands = [state[0], *parts, *state[1:]]
        out_shape = jax.ShapeDtypeStruct(queries.shape, queries.dtype) if final else state_shape[1:]
    result = pl.pallas_call(
        functools.partial(attend_kernel, spans, kv_dev, group, block_tok, rows, first, final),
        out_shape=out_shape,
        in_specs=[SMEM] + [VMEM] * len(operands),
        out_specs=VMEM if final else [VMEM] * len(out_shape),
        scratch_shapes=[
            pltpu.VMEM((kv_dev, keys, head_dim), jnp.bfloat16),
            pltpu.VMEM((kv_dev, head_dim + 16, keys), jnp.bfloat16),
            pltpu.VMEM((block_tok * kv_dev, head_dim), jnp.float32),
        ],
        compiler_params=pltpu.CompilerParams(vmem_limit_bytes=ATTEND_LIMIT),
        cost_estimate=pl.CostEstimate(
            flops=4 * suffix * heads_dev * keys * head_dim,
            bytes_accessed=keys * kv_dev * head_dim * 4 + 16 * suffix * heads_dev * head_dim,
            transcendentals=suffix * heads_dev * keys,
        ),
    )(counts, *operands)
    if first or final:
        return result
    return [state[0], *result]


def per_device(
    queries, new_kv, pool, prefix_slot, prefix_owner, prefix_len, write_slot, write_owner
):
    num_blk = lax.axis_size("blk")
    pool_dev, _, block_tok, kv_dev, head_dim = pool.shape
    suffix = queries.shape[1]
    prefix_blocks = prefix_slot.shape[1]
    capacity = max(2, (prefix_blocks + num_blk - 1) // num_blk)
    shifts = sorted(range(1, num_blk), key=lambda d: -min(d, num_blk - d))
    pool_rows = pool.reshape(pool_dev, 2, block_tok * kv_dev, head_dim)
    new_rows = new_kv.reshape(2, suffix * kv_dev, head_dim)

    def shift(array, d):
        return lax.ppermute(array, "blk", [(i, (i + d) % num_blk) for i in range(num_blk)])

    counts, asks = prepare(
        prefix_slot, prefix_owner, prefix_len, write_slot, write_owner, capacity, num_blk
    )
    asked = {d: shift(asks[d], d) for d in shifts}
    fresh = pick_fresh(counts, new_rows, block_tok * kv_dev, num_blk)
    arrived_fresh = {d: shift(fresh[d - 1], d) for d in shifts}

    levels = []
    left = capacity
    for size in LEVELS:
        if left:
            levels.append((capacity - left, min(size, left)))
            left -= min(size, left)
    if left:
        levels.append((capacity - left, left))

    arrived = {}

    def send(start, size, after):
        plan = tuple((i, start, size) for i in range(num_blk - 1))
        sent = gather([asked[d] for d in shifts], pool_rows, plan, after)
        for d, blocks in zip(shifts, sent):
            arrived[start, d] = shift(blocks, num_blk - d)
        return sent

    sent = send(*levels[0], ())
    (local,) = gather([asks[0]], pool_rows, ((0, 0, capacity),), sent[:1])
    state = attend(
        counts,
        queries[0],
        [local],
        ((0, 0, capacity),),
        kv_dev,
        block_tok,
        new_rows,
        None,
        False,
    )
    for i, (start, size) in enumerate(levels):
        if i + 1 < len(levels):
            send(*levels[i + 1], state[2:])
        for at in range(0, len(shifts), 4):
            spans = tuple((d, start, size) for d in shifts[at : at + 4])
            state = attend(
                counts,
                queries[0],
                [arrived[start, d] for d, _, _ in spans],
                spans,
                kv_dev,
                block_tok,
                None,
                state,
                i == len(levels) - 1 and at + 4 >= len(shifts),
            )
        if i == 0:
            new_pool = write_back(
                write_owner,
                write_slot,
                [asked[d] for d in shifts],
                pool_rows,
                new_rows,
                [arrived_fresh[d] for d in shifts],
                capacity,
                state[2:],
            )
    return state[None], new_pool.reshape(pool.shape)


def solution(mesh):
    in_specs = (
        P(("group", "blk"), None, "tensor", None),
        P(None, ("group", "blk"), None, "tensor", None),
        P(("group", "blk"), None, None, "tensor", None),
        P(("group", "blk"), None),
        P(("group", "blk"), None),
        P(("group", "blk")),
        P(("group", "blk"), None),
        P(("group", "blk"), None),
    )
    out_specs = (
        P(("group", "blk"), None, "tensor", None),
        P(("group", "blk"), None, None, "tensor", None),
    )
    return jax.shard_map(
        per_device, mesh=mesh, in_specs=in_specs, out_specs=out_specs, check_vma=False
    )
```

time: 273 us -> 134 us (0.49)
  blocking collectives: 118 us -> 0 us
  Pallas kernels: 0 us -> 59.4 us
  local copies, waits for them, and re-layouts: 55.7 us -> 1.93 us
  matrix products: 52.5 us -> 0 us
  starting transfers between devices: 5.04 us -> 51.2 us
  other arithmetic: 23.7 us -> 0 us
  waiting for transfers between devices: 0.04 us -> 20.2 us
  between operations: 15.5 us -> 1.5 us
    unnamed x1 -> x0, blocking collectives: 107 us -> none
    pallas_call x0 -> x13, Pallas kernels: none -> 59.4 us  [the longest x5 35.8 us: attend(): pl.pallas_call(functools.partial(attend_kernel, spans, kv_dev, group, blo...]
    dot_general x18 -> x0, matrix products: 52.5 us -> none  [the longest x8 32.7 us: absorb(): jnp.einsum('kgij,jkd->kgid', part_weights.astype(jnp.bfloat16), values_pa...]
    ppermute x0 -> x18, starting transfers between devices: none -> 51.2 us  [shift(): lax.ppermute(array, 'blk', [(i, (i + d) % num_blk) for i in range(num_blk)])]
    ppermute x0 -> x18, waiting for transfers between devices: none -> 20.2 us  [shift(): lax.ppermute(array, 'blk', [(i, (i + d) % num_blk) for i in range(num_blk)])]
    gather x2 -> x0, local copies, waits for them, and re-layouts: 17.3 us -> none  [the longest x1 12 us: per_device(): pool[asked.reshape(-1)]]
    reduce_sum x11 -> x0, other arithmetic: 16.9 us -> none  [the longest x8 15.7 us: absorb(): running_total = running_total * factor + jnp.sum(part_weights, axis=3)]
    all_to_all x1 -> x0, blocking collectives: 11.7 us -> none  [per_device(): lax.all_to_all(wanted, 'blk', split_axis=0, concat_axis=0, tiled=True)]
  transfers between devices with their start and end apart: 2 -> 18, of which waited for: 0 -> 3; matrix products, arithmetic and copies ran while one was open for 6% -> 0% of each run, Pallas kernels for 0% -> 36%
where the time goes in v2:
time: 134 us
  Pallas kernels  59.4 us (44%)
  starting transfers between devices  51.2 us (38%)
  waiting for transfers between devices  20.2 us (15%)
  local copies, waits for them, and re-layouts  1.93 us (1%)
  between operations  1.5 us (1%)
    ppermute x18, starting transfers between devices, shift(): lax.ppermute(array, 'blk', [(i, (i + d) % num_blk) for i in range(num_blk)])  51.2 us
    pallas_call x5, Pallas kernels, attend(): pl.pallas_call(functools.partial(attend_kernel, spans, kv_dev, group, blo...  35.8 us
    ppermute x18, waiting for transfers between devices, shift(): lax.ppermute(array, 'blk', [(i, (i + d) % num_blk) for i in range(num_blk)])  20.2 us
    pallas_call x5, Pallas kernels, gather(): pl.pallas_call(functools.partial(gather_kernel, plan, len(asked)), out_sh...  14.3 us
    pallas_call x1, Pallas kernels, write_back(): pl.pallas_call(functools.partial(write_back_kernel, capacity, pool.shape[...  6.81 us
  transfers between devices with their start and end apart: 18, of which 3 were waited for; matrix products, arithmetic and copies ran while one was open for 0% of the time, Pallas kernels for 36%

profile of v2, /device:TPU:0, one launch (start us, length us, event | category | flops | bytes accessed | tf_op | source)
XLA Modules:
  0.0 134.2 jit_solution(3493438894265974165)
XLA Ops:
  1.3 1.5 %shard_map.95 = (s32[1,8]{1,0:T(1,128)}, s32[1,9]{1,0:T(1,128)}, s32[1,9]{1,0:T(1,128)}, s32[1,9]{1,0:T(1,128)}, s32[1,9]{1,0:T(1,128)}) custom-call(s32[1,32]{1,0:T(1,128)} %refs_0_.1, s32[1,32]{1,0:T(1,128)} %refs_1_.1, s32[1]{0:T(128)S(6)} %copy.10.refs_2_, s32[1,2]{1,0:T(1,128)} %slot_ref.1, s32[1,2]{1,0:T(1,128)} %owner_ref.1), custom_call_target="tpu_custom_call" | custom-call | tf_op jit(solution)/shard_map/pallas_call | solution.py:70
  2.8 0.0 copy-start.6
  2.8 4.1 %collective-permute-start = (s32[1,9]{1,0:T(1,128)}, s32[1,9]{1,0:T(1,128)S(1)}, u32[]{:S(2)}, u32[]{:S(2)}) collective-permute-start(s32[1,9]{1,0:T(1,128)} %get-tuple-element.33), channel_id=1, source_target_pairs={{0,8},{4,12},{8,0},{12,4},{1,9},{5,13},{9,1},{13,5},{2,10},{6,14},... | collective-permute-start | bytes 116 | tf_op jit(solution)/shard_map/ppermute | solution.py:391
  6.9 1.6 %collective-permute-start.1 = (s32[1,9]{1,0:T(1,128)}, s32[1,9]{1,0:T(1,128)S(1)}, u32[]{:S(2)}, u32[]{:S(2)}) collective-permute-start(s32[1,9]{1,0:T(1,128)} %get-tuple-element.34), channel_id=1, source_target_pairs={{0,4},{4,8},{8,12},{12,0},{1,5},{5,9},{9,13},{13,1},{2,6},{6,10},{... | collective-permute-start | bytes 116 | tf_op jit(solution)/shard_map/ppermute | solution.py:391
  8.5 2.2 %collective-permute-start.2 = (s32[1,9]{1,0:T(1,128)}, s32[1,9]{1,0:T(1,128)S(1)}, u32[]{:S(2)}, u32[]{:S(2)}) collective-permute-start(s32[1,9]{1,0:T(1,128)} %get-tuple-element.35), channel_id=1, source_target_pairs={{0,12},{4,0},{8,4},{12,8},{1,13},{5,1},{9,5},{13,9},{2,14},{6,2},{... | collective-permute-start | bytes 116 | tf_op jit(solution)/shard_map/ppermute | solution.py:391
  10.8 0.0 collective-permute-done.refs_0_
  10.8 1.7 %collective-permute-done.1.refs_1_ = s32[1,9]{1,0:T(1,128)S(1)} collective-permute-done((s32[1,9]{1,0:T(1,128)}, s32[1,9]{1,0:T(1,128)S(1)}, u32[]{:S(2)}, u32[]{:S(2)}) %collective-permute-start.1) | collective-permute-done | bytes 68 | tf_op jit(solution)/shard_map/ppermute | solution.py:391
  12.5 0.0 collective-permute-done.2.refs_2_
  12.5 1.9 %copy-done = bf16[24,2,128,2,128]{4,3,2,1,0:T(2,128)(2,1)S(1)} copy-done((bf16[24,2,128,2,128]{4,3,2,1,0:T(2,128)(2,1)S(1)}, bf16[24,2,128,2,128]{4,3,2,1,0:T(2,128)(2,1)}, u32[]{:S(2)}) %copy-start) | copy-done | bytes 3145752
  14.4 3.8 %shard_map.96 = (bf16[3,2,256,128]{3,2,1,0:T(8,128)(2,1)S(1)}, bf16[3,2,256,128]{3,2,1,0:T(8,128)(2,1)S(1)}, bf16[3,2,256,128]{3,2,1,0:T(8,128)(2,1)S(1)}) custom-call(s32[1,9]{1,0:T(1,128)S(1)} %collective-permute-done.refs_0_, s32[1,9]{1,0:T(1,128)S(1)} %collective-permute-done.1.refs_1_, s32[1,9]{1,0:T(1,128)S(1)} %collective-permute-done.2.refs_2_, ...), custom_call_target="tpu_custom_call" | custom-call | bytes 2359296 | tf_op jit(solution)/shard_map/pallas_call | solution.py:141
  18.2 0.6 collective-permute-start.6
  18.8 3.2 %collective-permute-start.7 = (bf16[3,2,256,128]{3,2,1,0:T(8,128)(2,1)S(1)}, bf16[3,2,256,128]{3,2,1,0:T(8,128)(2,1)S(1)}, u32[]{:S(2)}, u32[]{:S(2)}) collective-permute-start(bf16[3,2,256,128]{3,2,1,0:T(8,128)(2,1)S(1)} %get-tuple-element.42), channel_id=1, source_target_pairs={{0,12},{4,0},{8,4},{12,8},{1,13},{5,1},{9,5},{13,9},{2,14},{6,2},{... | collective-permute-start | bytes 1179656 | tf_op jit(solution)/shard_map/ppermute | solution.py:391
  22.0 0.5 collective-permute-start.8
  22.5 0.0 copy-start.7
  22.5 3.4 %shard_map.97.refs_0_ = bf16[8,2,256,128]{3,2,1,0:T(8,128)(2,1)S(1)} custom-call(s32[1,9]{1,0:T(1,128)S(1)} %copy-done.6, bf16[24,2,256,128]{3,2,1,0:T(8,128)(2,1)S(1)} %bitcast.6, bf16[3,2,256,128]{3,2,1,0:T(8,128)(2,1)S(1)} %get-tuple-element.36.refs_2_), custom_call_target="tpu_custom_call" | custom-call | bytes 2097152 | tf_op jit(solution)/shard_map/pallas_call | solution.py:141
  26.0 9.0 %shard_map.98 = (bf16[2,2048,128]{2,1,0:T(8,128)(2,1)S(1)}, f32[2,128,2048]{2,1,0:T(8,128)S(1)}, f32[2,8,2048]{2,1,0:T(8,128)S(1)}) custom-call(s32[1,8]{1,0:T(1,128)S(1)} %copy-done.3, bf16[256,16,128]{2,1,0:T(8,128)(2,1)S(1)} %bitcast.14, bf16[8,2,256,128]{3,2,1,0:T(8,128)(2,1)S(1)} %shard_map.97.refs_0_, bf16[2,512,128]{2,1,0:T(8,128)(2,1)S(1)} %bitcast.11), custom_call_target="tpu_custom_call" | custom-call | flops 2684354560 | bytes 9699328 | tf_op jit(solution)/shard_map/pallas_call | solution.py:356
  35.0 2.7 %shard_map.99 = (bf16[2,2,256,128]{3,2,1,0:T(8,128)(2,1)S(1)}, bf16[2,2,256,128]{3,2,1,0:T(8,128)(2,1)S(1)}, bf16[2,2,256,128]{3,2,1,0:T(8,128)(2,1)S(1)}) custom-call(s32[1,9]{1,0:T(1,128)S(1)} %collective-permute-done.refs_0_, s32[1,9]{1,0:T(1,128)S(1)} %collective-permute-done.1.refs_1_, s32[1,9]{1,0:T(1,128)S(1)} %collective-permute-done.2.refs_2_, ...), custom_call_target="tpu_custom_call" | custom-call | bytes 1572864 | tf_op jit(solution)/shard_map/pallas_call | solution.py:141
  37.7 1.5 %collective-permute-start.3 = (bf16[2,2,256,128]{3,2,1,0:T(8,128)(2,1)S(1)}, bf16[2,2,256,128]{3,2,1,0:T(8,128)(2,1)S(1)}, u32[]{:S(2)}, u32[]{:S(2)}) collective-permute-start(bf16[2,2,256,128]{3,2,1,0:T(8,128)(2,1)S(1)} %get-tuple-element.39), channel_id=1, source_target_pairs={{0,8},{4,12},{8,0},{12,4},{1,9},{5,13},{9,1},{13,5},{2,10},{6,14},... | collective-permute-start | bytes 786440 | tf_op jit(solution)/shard_map/ppermute | solution.py:391
  39.3 0.9 shard_map.106
  40.2 1.5 %collective-permute-start.15 = (bf16[2,256,128]{2,1,0:T(8,128)(2,1)S(1)}, bf16[2,256,128]{2,1,0:T(8,128)(2,1)S(1)}, u32[]{:S(2)}, u32[]{:S(2)}) collective-permute-start(bf16[2,256,128]{2,1,0:T(8,128)(2,1)S(1)} %get-tuple-element.57), channel_id=1, source_target_pairs={{0,8},{4,12},{8,0},{12,4},{1,9},{5,13},{9,1},{13,5},{2,10},{6,14},... | collective-permute-start | bytes 393224 | tf_op jit(solution)/shard_map/ppermute | solution.py:391
  41.7 11.0 %collective-permute-done.6.refs_0_ = bf16[3,2,256,128]{3,2,1,0:T(8,128)(2,1)S(1)} collective-permute-done((bf16[3,2,256,128]{3,2,1,0:T(8,128)(2,1)S(1)}, bf16[3,2,256,128]{3,2,1,0:T(8,128)(2,1)S(1)}, u32[]{:S(2)}, u32[]{:S(2)}) %collective-permute-start.6) | collective-permute-done | bytes 393248 | tf_op jit(solution)/shard_map/ppermute | solution.py:391
  52.7 0.0 collective-permute-start.4
  52.7 16.9 %collective-permute-start.5 = (bf16[2,2,256,128]{3,2,1,0:T(8,128)(2,1)S(1)}, bf16[2,2,256,128]{3,2,1,0:T(8,128)(2,1)S(1)}, u32[]{:S(2)}, u32[]{:S(2)}) collective-permute-start(bf16[2,2,256,128]{3,2,1,0:T(8,128)(2,1)S(1)} %get-tuple-element.41), channel_id=1, source_target_pairs={{0,4},{4,8},{8,12},{12,0},{1,5},{5,9},{9,13},{13,1},{2,6},{6,10},{... | collective-permute-start | bytes 786440 | tf_op jit(solution)/shard_map/ppermute | solution.py:391
  69.6 8.6 %shard_map.100 = (f32[2,128,2048]{2,1,0:T(8,128)S(1)}, f32[2,8,2048]{2,1,0:T(8,128)S(1)}) custom-call(s32[1,8]{1,0:T(1,128)S(1)} %copy-done.3, bf16[2,2048,128]{2,1,0:T(8,128)(2,1)S(1)} %get-tuple-element.37.q_ref, bf16[3,2,256,128]{3,2,1,0:T(8,128)(2,1)S(1)} %collective-permute-done.6.refs_0_, bf16[3,2,256,128]{3,2,1,0:T(8,128)(2,1)S(1)} %collective-permute-done.7.refs_1_, ...), custom_call_target="tpu_custom_call" | custom-call | flops 2415919104 | bytes 9568256 | tf_op jit(solution)/shard_map/pallas_call | solution.py:356
  78.2 2.7 %shard_map.103 = (bf16[2,2,256,128]{3,2,1,0:T(8,128)(2,1)S(1)}, bf16[2,2,256,128]{3,2,1,0:T(8,128)(2,1)S(1)}, bf16[2,2,256,128]{3,2,1,0:T(8,128)(2,1)S(1)}) custom-call(s32[1,9]{1,0:T(1,128)S(1)} %collective-permute-done.refs_0_, s32[1,9]{1,0:T(1,128)S(1)} %collective-permute-done.1.refs_1_, s32[1,9]{1,0:T(1,128)S(1)} %collective-permute-done.2.refs_2_, ...), custom_call_target="tpu_custom_call" | custom-call | bytes 1572864 | tf_op jit(solution)/shard_map/pallas_call | solution.py:141
  80.9 0.1 collective-permute-start.12
  81.0 2.3 %collective-permute-start.13 = (bf16[2,2,256,128]{3,2,1,0:T(8,128)(2,1)S(1)}, bf16[2,2,256,128]{3,2,1,0:T(8,128)(2,1)S(1)}, u32[]{:S(2)}, u32[]{:S(2)}) collective-permute-start(bf16[2,2,256,128]{3,2,1,0:T(8,128)(2,1)S(1)} %get-tuple-element.52), channel_id=1, source_target_pairs={{0,12},{4,0},{8,4},{12,8},{1,13},{5,1},{9,5},{13,9},{2,14},{6,2},{... | collective-permute-start | bytes 786440 | tf_op jit(solution)/shard_map/ppermute | solution.py:391
  83.4 0.0 collective-permute-done.3.refs_0_
  83.4 0.0 collective-permute-start.14
  83.4 0.0 collective-permute-done.4.refs_1_
  83.4 1.9 %collective-permute-start.16 = (bf16[2,256,128]{2,1,0:T(8,128)(2,1)S(1)}, bf16[2,256,128]{2,1,0:T(8,128)(2,1)S(1)}, u32[]{:S(2)}, u32[]{:S(2)}) collective-permute-start(bf16[2,256,128]{2,1,0:T(8,128)(2,1)S(1)} %get-tuple-element.58), channel_id=1, source_target_pairs={{0,4},{4,8},{8,12},{12,0},{1,5},{5,9},{9,13},{13,1},{2,6},{6,10},{... | collective-permute-start | bytes 393224 | tf_op jit(solution)/shard_map/ppermute | solution.py:391
  85.3 2.0 %collective-permute-start.17 = (bf16[2,256,128]{2,1,0:T(8,128)(2,1)S(1)}, bf16[2,256,128]{2,1,0:T(8,128)(2,1)S(1)}, u32[]{:S(2)}, u32[]{:S(2)}) collective-permute-start(bf16[2,256,128]{2,1,0:T(8,128)(2,1)S(1)} %get-tuple-element.59), channel_id=1, source_target_pairs={{0,12},{4,0},{8,4},{12,8},{1,13},{5,1},{9,5},{13,9},{2,14},{6,2},{... | collective-permute-start | bytes 393224 | tf_op jit(solution)/shard_map/ppermute | solution.py:391
  87.3 6.5 %shard_map.101 = (f32[2,128,2048]{2,1,0:T(8,128)S(1)}, f32[2,8,2048]{2,1,0:T(8,128)S(1)}) custom-call(s32[1,8]{1,0:T(1,128)S(1)} %copy-done.3, bf16[2,2048,128]{2,1,0:T(8,128)(2,1)S(1)} %get-tuple-element.37.q_ref, bf16[2,2,256,128]{3,2,1,0:T(8,128)(2,1)S(1)} %collective-permute-done.3.refs_0_, bf16[2,2,256,128]{3,2,1,0:T(8,128)(2,1)S(1)} %collective-permute-done.4.refs_1_, ...), custom_call_target="tpu_custom_call" | custom-call | flops 1610612736 | bytes 9175040 | tf_op jit(solution)/shard_map/pallas_call | solution.py:356
  93.8 0.0 copy-start.4
  93.8 0.0 copy-start.5
  93.8 1.6 %shard_map.102 = (bf16[1,2,256,128]{3,2,1,0:T(8,128)(2,1)S(1)}, bf16[1,2,256,128]{3,2,1,0:T(8,128)(2,1)S(1)}, bf16[1,2,256,128]{3,2,1,0:T(8,128)(2,1)S(1)}) custom-call(s32[1,9]{1,0:T(1,128)S(1)} %collective-permute-done.refs_0_, s32[1,9]{1,0:T(1,128)S(1)} %collective-permute-done.1.refs_1_, s32[1,9]{1,0:T(1,128)S(1)} %collective-permute-done.2.refs_2_, ...), custom_call_target="tpu_custom_call" | custom-call | bytes 786432 | tf_op jit(solution)/shard_map/pallas_call | solution.py:141
  95.4 7.4 %collective-permute-done.16.refs_6_ = bf16[2,256,128]{2,1,0:T(8,128)(2,1)S(1)} collective-permute-done((bf16[2,256,128]{2,1,0:T(8,128)(2,1)S(1)}, bf16[2,256,128]{2,1,0:T(8,128)(2,1)S(1)}, u32[]{:S(2)}, u32[]{:S(2)}) %collective-permute-start.16) | collective-permute-done | bytes 131104 | tf_op jit(solution)/shard_map/ppermute | solution.py:391
  102.9 2.2 %collective-permute-start.10 = (bf16[1,2,256,128]{3,2,1,0:T(8,128)(2,1)S(1)}, bf16[1,2,256,128]{3,2,1,0:T(8,128)(2,1)S(1)}, u32[]{:S(2)}, u32[]{:S(2)}) collective-permute-start(bf16[1,2,256,128]{3,2,1,0:T(8,128)(2,1)S(1)} %get-tuple-element.49), channel_id=1, source_target_pairs={{0,12},{4,0},{8,4},{12,8},{1,13},{5,1},{9,5},{13,9},{2,14},{6,2},{... | collective-permute-start | bytes 393224 | tf_op jit(solution)/shard_map/ppermute | solution.py:391
  105.0 0.0 collective-permute-done.17.refs_7_
  105.1 6.6 %collective-permute-start.11 = (bf16[1,2,256,128]{3,2,1,0:T(8,128)(2,1)S(1)}, bf16[1,2,256,128]{3,2,1,0:T(8,128)(2,1)S(1)}, u32[]{:S(2)}, u32[]{:S(2)}) collective-permute-start(bf16[1,2,256,128]{3,2,1,0:T(8,128)(2,1)S(1)} %get-tuple-element.50), channel_id=1, source_target_pairs={{0,4},{4,8},{8,12},{12,0},{1,5},{5,9},{9,13},{13,1},{2,6},{6,10},{... | collective-permute-start | bytes 393224 | tf_op jit(solution)/shard_map/ppermute | solution.py:391
  111.6 6.8 %shard_map.107 = bf16[24,2,256,128]{3,2,1,0:T(8,128)(2,1)} custom-call(s32[1,2]{1,0:T(1,128)S(1)} %copy-done.5, s32[1,2]{1,0:T(1,128)S(1)} %copy-done.4, s32[1,9]{1,0:T(1,128)S(1)} %collective-permute-done.refs_0_, s32[1,9]{1,0:T(1,128)S(1)} %collective-permute-done.1.refs_1_, s32[1,9]{1,0:T(1,128)S(1)} %collective-permute-done.2.refs_2_, ...), custom_call_target="tpu_custom_call" | custom-call | bytes 6291456 | tf_op jit(solution)/shard_map/pallas_call | solution.py:192
  118.5 0.0 collective-permute-done.12.refs_0_
  118.5 4.0 %collective-permute-start.9 = (bf16[1,2,256,128]{3,2,1,0:T(8,128)(2,1)S(1)}, bf16[1,2,256,128]{3,2,1,0:T(8,128)(2,1)S(1)}, u32[]{:S(2)}, u32[]{:S(2)}) collective-permute-start(bf16[1,2,256,128]{3,2,1,0:T(8,128)(2,1)S(1)} %get-tuple-element.48), channel_id=1, source_target_pairs={{0,8},{4,12},{8,0},{12,4},{1,9},{5,13},{9,1},{13,5},{2,10},{6,14},... | collective-permute-start | bytes 393224 | tf_op jit(solution)/shard_map/ppermute | solution.py:391
  122.5 0.0 collective-permute-done.14.refs_2_
  122.5 6.5 %shard_map.104 = (f32[2,128,2048]{2,1,0:T(8,128)S(1)}, f32[2,8,2048]{2,1,0:T(8,128)S(1)}) custom-call(s32[1,8]{1,0:T(1,128)S(1)} %copy-done.3, bf16[2,2048,128]{2,1,0:T(8,128)(2,1)S(1)} %get-tuple-element.37.q_ref, bf16[2,2,256,128]{3,2,1,0:T(8,128)(2,1)S(1)} %collective-permute-done.12.refs_0_, ...), custom_call_target="tpu_custom_call" | custom-call | flops 1610612736 | bytes 9175040 | tf_op jit(solution)/shard_map/pallas_call | solution.py:356
  129.0 0.0 collective-permute-done.10.refs_1_
  129.0 0.0 collective-permute-done.11.refs_2_
  129.0 5.2 %shard_map.105 = bf16[256,16,128]{2,1,0:T(8,128)(2,1)} custom-call(s32[1,8]{1,0:T(1,128)S(1)} %copy-done.3, bf16[2,2048,128]{2,1,0:T(8,128)(2,1)S(1)} %get-tuple-element.37.q_ref, bf16[1,2,256,128]{3,2,1,0:T(8,128)(2,1)S(1)} %collective-permute-done.9.refs_0_, bf16[1,2,256,128]{3,2,1,0:T(8,128)(2,1)S(1)} %collective-permute-done.10.refs_1_, ...), custom_call_target="tpu_custom_call" | custom-call | flops 805306368 | bytes 8781824 | tf_op jit(solution)/shard_map/pallas_call | solution.py:356
  (17 shorter events, 0.0 us)
Async XLA Ops:
  2.8 19.7 %copy-start.6 = (s32[1,9]{1,0:T(1,128)S(1)}, s32[1,9]{1,0:T(1,128)}, u32[]{:S(2)}) copy-start(s32[1,9]{1,0:T(1,128)} %get-tuple-element.32.refs_0_) | copy-start | bytes 112
  2.8 7.9 %collective-permute-start = (s32[1,9]{1,0:T(1,128)}, s32[1,9]{1,0:T(1,128)S(1)}, u32[]{:S(2)}, u32[]{:S(2)}) collective-permute-start(s32[1,9]{1,0:T(1,128)} %get-tuple-element.33), channel_id=1, source_target_pairs={{0,8},{4,12},{8,0},{12,4},{1,9},{5,13},{9,1},{13,5},{2,10},{6,14},... | collective-permute-start | bytes 116 | tf_op jit(solution)/shard_map/ppermute | solution.py:391
  6.9 5.5 %collective-permute-start.1 = (s32[1,9]{1,0:T(1,128)}, s32[1,9]{1,0:T(1,128)S(1)}, u32[]{:S(2)}, u32[]{:S(2)}) collective-permute-start(s32[1,9]{1,0:T(1,128)} %get-tuple-element.34), channel_id=1, source_target_pairs={{0,4},{4,8},{8,12},{12,0},{1,5},{5,9},{9,13},{13,1},{2,6},{6,10},{... | collective-permute-start | bytes 116 | tf_op jit(solution)/shard_map/ppermute | solution.py:391
  8.5 4.0 %collective-permute-start.2 = (s32[1,9]{1,0:T(1,128)}, s32[1,9]{1,0:T(1,128)S(1)}, u32[]{:S(2)}, u32[]{:S(2)}) collective-permute-start(s32[1,9]{1,0:T(1,128)} %get-tuple-element.35), channel_id=1, source_target_pairs={{0,12},{4,0},{8,4},{12,8},{1,13},{5,1},{9,5},{13,9},{2,14},{6,2},{... | collective-permute-start | bytes 116 | tf_op jit(solution)/shard_map/ppermute | solution.py:391
  12.5 1.9 %copy-start = (bf16[24,2,128,2,128]{4,3,2,1,0:T(2,128)(2,1)S(1)}, bf16[24,2,128,2,128]{4,3,2,1,0:T(2,128)(2,1)}, u32[]{:S(2)}) copy-start(bf16[24,2,128,2,128]{4,3,2,1,0:T(2,128)(2,1)} %param.10) | copy-start | bytes 9437188
  14.4 8.1 %copy-start.1 = (bf16[24,2,128,2,128]{4,3,2,1,0:T(2,128)(2,1)S(1)}, bf16[24,2,128,2,128]{4,3,2,1,0:T(2,128)(2,1)}, u32[]{:S(2)}) copy-start(bf16[24,2,128,2,128]{4,3,2,1,0:T(2,128)(2,1)} %param.10) | copy-start | bytes 9437188
  18.2 34.5 %collective-permute-start.6 = (bf16[3,2,256,128]{3,2,1,0:T(8,128)(2,1)S(1)}, bf16[3,2,256,128]{3,2,1,0:T(8,128)(2,1)S(1)}, u32[]{:S(2)}, u32[]{:S(2)}) collective-permute-start(bf16[3,2,256,128]{3,2,1,0:T(8,128)(2,1)S(1)} %get-tuple-element.36.refs_2_), channel_id=1, source_target_pairs={{0,8},{4,12},{8,0},{12,4},{1,9},{5,13},{9,1},{13,5},{2,10},{6,14},... | collective-permute-start | bytes 1179656 | tf_op jit(solution)/shard_map/ppermute | solution.py:391
  18.8 33.8 %collective-permute-start.7 = (bf16[3,2,256,128]{3,2,1,0:T(8,128)(2,1)S(1)}, bf16[3,2,256,128]{3,2,1,0:T(8,128)(2,1)S(1)}, u32[]{:S(2)}, u32[]{:S(2)}) collective-permute-start(bf16[3,2,256,128]{3,2,1,0:T(8,128)(2,1)S(1)} %get-tuple-element.42), channel_id=1, source_target_pairs={{0,12},{4,0},{8,4},{12,8},{1,13},{5,1},{9,5},{13,9},{2,14},{6,2},{... | collective-permute-start | bytes 1179656 | tf_op jit(solution)/shard_map/ppermute | solution.py:391
  22.0 47.6 %collective-permute-start.8 = (bf16[3,2,256,128]{3,2,1,0:T(8,128)(2,1)S(1)}, bf16[3,2,256,128]{3,2,1,0:T(8,128)(2,1)S(1)}, u32[]{:S(2)}, u32[]{:S(2)}) collective-permute-start(bf16[3,2,256,128]{3,2,1,0:T(8,128)(2,1)S(1)} %get-tuple-element.43), channel_id=1, source_target_pairs={{0,4},{4,8},{8,12},{12,0},{1,5},{5,9},{9,13},{13,1},{2,6},{6,10},{... | collective-permute-start | bytes 1179656 | tf_op jit(solution)/shard_map/ppermute | solution.py:391
  22.5 3.5 %copy-start.2 = (bf16[2,1,256,2,128]{4,3,2,1,0:T(2,128)(2,1)S(1)}, bf16[2,1,256,2,128]{4,3,2,1,0:T(2,128)(2,1)}, u32[]{:S(2)}) copy-start(bf16[2,1,256,2,128]{4,3,2,1,0:T(2,128)(2,1)} %param.9) | copy-start | bytes 786436
  22.5 3.5 %copy-start.3 = (s32[1,8]{1,0:T(1,128)S(1)}, s32[1,8]{1,0:T(1,128)}, u32[]{:S(2)}) copy-start(s32[1,8]{1,0:T(1,128)} %get-tuple-element.31.count_ref) | copy-start | bytes 100
  22.5 3.5 %copy-start.7 = (bf16[1,256,16,128]{3,2,1,0:T(8,128)(2,1)S(1)}, bf16[1,256,16,128]{3,2,1,0:T(8,128)(2,1)}, u32[]{:S(2)}) copy-start(bf16[1,256,16,128]{3,2,1,0:T(8,128)(2,1)} %param.8) | copy-start | bytes 3145732
  37.7 45.6 %collective-permute-start.3 = (bf16[2,2,256,128]{3,2,1,0:T(8,128)(2,1)S(1)}, bf16[2,2,256,128]{3,2,1,0:T(8,128)(2,1)S(1)}, u32[]{:S(2)}, u32[]{:S(2)}) collective-permute-start(bf16[2,2,256,128]{3,2,1,0:T(8,128)(2,1)S(1)} %get-tuple-element.39), channel_id=1, source_target_pairs={{0,8},{4,12},{8,0},{12,4},{1,9},{5,13},{9,1},{13,5},{2,10},{6,14},... | collective-permute-start | bytes 786440 | tf_op jit(solution)/shard_map/ppermute | solution.py:391
  40.2 40.9 %collective-permute-start.15 = (bf16[2,256,128]{2,1,0:T(8,128)(2,1)S(1)}, bf16[2,256,128]{2,1,0:T(8,128)(2,1)S(1)}, u32[]{:S(2)}, u32[]{:S(2)}) collective-permute-start(bf16[2,256,128]{2,1,0:T(8,128)(2,1)S(1)} %get-tuple-element.57), channel_id=1, source_target_pairs={{0,8},{4,12},{8,0},{12,4},{1,9},{5,13},{9,1},{13,5},{2,10},{6,14},... | collective-permute-start | bytes 393224 | tf_op jit(solution)/shard_map/ppermute | solution.py:391
  52.7 30.7 %collective-permute-start.4 = (bf16[2,2,256,128]{3,2,1,0:T(8,128)(2,1)S(1)}, bf16[2,2,256,128]{3,2,1,0:T(8,128)(2,1)S(1)}, u32[]{:S(2)}, u32[]{:S(2)}) collective-permute-start(bf16[2,2,256,128]{3,2,1,0:T(8,128)(2,1)S(1)} %get-tuple-element.40), channel_id=1, source_target_pairs={{0,12},{4,0},{8,4},{12,8},{1,13},{5,1},{9,5},{13,9},{2,14},{6,2},{... | collective-permute-start | bytes 786440 | tf_op jit(solution)/shard_map/ppermute | solution.py:391
  52.7 32.6 %collective-permute-start.5 = (bf16[2,2,256,128]{3,2,1,0:T(8,128)(2,1)S(1)}, bf16[2,2,256,128]{3,2,1,0:T(8,128)(2,1)S(1)}, u32[]{:S(2)}, u32[]{:S(2)}) collective-permute-start(bf16[2,2,256,128]{3,2,1,0:T(8,128)(2,1)S(1)} %get-tuple-element.41), channel_id=1, source_target_pairs={{0,4},{4,8},{8,12},{12,0},{1,5},{5,9},{9,13},{13,1},{2,6},{6,10},{... | collective-permute-start | bytes 786440 | tf_op jit(solution)/shard_map/ppermute | solution.py:391
  80.9 37.5 %collective-permute-start.12 = (bf16[2,2,256,128]{3,2,1,0:T(8,128)(2,1)S(1)}, bf16[2,2,256,128]{3,2,1,0:T(8,128)(2,1)S(1)}, u32[]{:S(2)}, u32[]{:S(2)}) collective-permute-start(bf16[2,2,256,128]{3,2,1,0:T(8,128)(2,1)S(1)} %get-tuple-element.51), channel_id=1, source_target_pairs={{0,8},{4,12},{8,0},{12,4},{1,9},{5,13},{9,1},{13,5},{2,10},{6,14},... | collective-permute-start | bytes 786440 | tf_op jit(solution)/shard_map/ppermute | solution.py:391
  81.0 41.4 %collective-permute-start.13 = (bf16[2,2,256,128]{3,2,1,0:T(8,128)(2,1)S(1)}, bf16[2,2,256,128]{3,2,1,0:T(8,128)(2,1)S(1)}, u32[]{:S(2)}, u32[]{:S(2)}) collective-permute-start(bf16[2,2,256,128]{3,2,1,0:T(8,128)(2,1)S(1)} %get-tuple-element.52), channel_id=1, source_target_pairs={{0,12},{4,0},{8,4},{12,8},{1,13},{5,1},{9,5},{13,9},{2,14},{6,2},{... | collective-permute-start | bytes 786440 | tf_op jit(solution)/shard_map/ppermute | solution.py:391
  83.4 39.1 %collective-permute-start.14 = (bf16[2,2,256,128]{3,2,1,0:T(8,128)(2,1)S(1)}, bf16[2,2,256,128]{3,2,1,0:T(8,128)(2,1)S(1)}, u32[]{:S(2)}, u32[]{:S(2)}) collective-permute-start(bf16[2,2,256,128]{3,2,1,0:T(8,128)(2,1)S(1)} %get-tuple-element.53), channel_id=1, source_target_pairs={{0,4},{4,8},{8,12},{12,0},{1,5},{5,9},{9,13},{13,1},{2,6},{6,10},{... | collective-permute-start | bytes 786440 | tf_op jit(solution)/shard_map/ppermute | solution.py:391
  83.4 19.5 %collective-permute-start.16 = (bf16[2,256,128]{2,1,0:T(8,128)(2,1)S(1)}, bf16[2,256,128]{2,1,0:T(8,128)(2,1)S(1)}, u32[]{:S(2)}, u32[]{:S(2)}) collective-permute-start(bf16[2,256,128]{2,1,0:T(8,128)(2,1)S(1)} %get-tuple-element.58), channel_id=1, source_target_pairs={{0,4},{4,8},{8,12},{12,0},{1,5},{5,9},{9,13},{13,1},{2,6},{6,10},{... | collective-permute-start | bytes 393224 | tf_op jit(solution)/shard_map/ppermute | solution.py:391
  85.3 19.8 %collective-permute-start.17 = (bf16[2,256,128]{2,1,0:T(8,128)(2,1)S(1)}, bf16[2,256,128]{2,1,0:T(8,128)(2,1)S(1)}, u32[]{:S(2)}, u32[]{:S(2)}) collective-permute-start(bf16[2,256,128]{2,1,0:T(8,128)(2,1)S(1)} %get-tuple-element.59), channel_id=1, source_target_pairs={{0,12},{4,0},{8,4},{12,8},{1,13},{5,1},{9,5},{13,9},{2,14},{6,2},{... | collective-permute-start | bytes 393224 | tf_op jit(solution)/shard_map/ppermute | solution.py:391
  93.8 17.9 %copy-start.4 = (s32[1,2]{1,0:T(1,128)S(1)}, s32[1,2]{1,0:T(1,128)}, u32[]{:S(2)}) copy-start(s32[1,2]{1,0:T(1,128)} %slot_ref.1) | copy-start | bytes 28
  93.8 17.8 %copy-start.5 = (s32[1,2]{1,0:T(1,128)S(1)}, s32[1,2]{1,0:T(1,128)}, u32[]{:S(2)}) copy-start(s32[1,2]{1,0:T(1,128)} %owner_ref.1) | copy-start | bytes 28
  102.9 26.1 %collective-permute-start.10 = (bf16[1,2,256,128]{3,2,1,0:T(8,128)(2,1)S(1)}, bf16[1,2,256,128]{3,2,1,0:T(8,128)(2,1)S(1)}, u32[]{:S(2)}, u32[]{:S(2)}) collective-permute-start(bf16[1,2,256,128]{3,2,1,0:T(8,128)(2,1)S(1)} %get-tuple-element.49), channel_id=1, source_target_pairs={{0,12},{4,0},{8,4},{12,8},{1,13},{5,1},{9,5},{13,9},{2,14},{6,2},{... | collective-permute-start | bytes 393224 | tf_op jit(solution)/shard_map/ppermute | solution.py:391
  105.1 23.9 %collective-permute-start.11 = (bf16[1,2,256,128]{3,2,1,0:T(8,128)(2,1)S(1)}, bf16[1,2,256,128]{3,2,1,0:T(8,128)(2,1)S(1)}, u32[]{:S(2)}, u32[]{:S(2)}) collective-permute-start(bf16[1,2,256,128]{3,2,1,0:T(8,128)(2,1)S(1)} %get-tuple-element.50), channel_id=1, source_target_pairs={{0,4},{4,8},{8,12},{12,0},{1,5},{5,9},{9,13},{13,1},{2,6},{6,10},{... | collective-permute-start | bytes 393224 | tf_op jit(solution)/shard_map/ppermute | solution.py:391
  118.5 10.5 %collective-permute-start.9 = (bf16[1,2,256,128]{3,2,1,0:T(8,128)(2,1)S(1)}, bf16[1,2,256,128]{3,2,1,0:T(8,128)(2,1)S(1)}, u32[]{:S(2)}, u32[]{:S(2)}) collective-permute-start(bf16[1,2,256,128]{3,2,1,0:T(8,128)(2,1)S(1)} %get-tuple-element.48), channel_id=1, source_target_pairs={{0,8},{4,12},{8,0},{12,4},{1,9},{5,13},{9,1},{13,5},{2,10},{6,14},... | collective-permute-start | bytes 393224 | tf_op jit(solution)/shard_map/ppermute | solution.py:391

commit v3 on v2

--- a/solution.py
+++ b/solution.py
@@ -16,7 +16,6 @@
 VMEM_LIMIT = 16 * 1024 * 1024
 ATTEND_LIMIT = 32 * 1024 * 1024
 QUERY_ROWS = 1024
-LEVELS = (3, 2, 2, 1)
 
 
 def prepare_kernel(capacity, *refs):
@@ -84,118 +83,79 @@
     return results[0], results[1:]
 
 
-def pick_fresh_kernel(num_blk, block_rows, count_ref, new_ref, *refs):
-    fresh, (held, load_sem, sems) = refs[: num_blk - 1], refs[num_blk - 1 :]
-    load = pltpu.make_async_copy(new_ref, held, load_sem)
-    load.start()
-    load.wait()
+def gather_kernel(plan, count, block_rows, count_ref, *refs):
+    asked, pool_ref, new_ref = refs[:count], refs[count], refs[count + 1]
+    outs, sems = refs[-len(plan) - 1 : -1], refs[-1]
     copies = []
-    for d in range(1, num_blk):
-        chosen = count_ref[0, num_blk + d]
-        at = pl.ds(pl.multiple_of(chosen * block_rows, block_rows), block_rows)
-        copies.append(pltpu.make_async_copy(held.at[:, at], fresh[d - 1], sems.at[d - 1]))
+
+    def move(source, target):
+        copy = pltpu.make_async_copy(source, target, sems.at[len(copies)])
+        copy.start()
+        copies.append(copy)
+
+    for (row, start, size, to), out in zip(plan, outs):
+        for place in range(size):
+            move(pool_ref.at[asked[row][0, start + place]], out.at[place])
+        if to is not None:
+            chosen = count_ref[0, count_ref.shape[1] // 2 + to]
+            at = pl.ds(pl.multiple_of(chosen * block_rows, block_rows), block_rows)
+            move(new_ref.at[:, at], out.at[size])
+    for copy in copies:
+        copy.wait()
+
+
+def gather(counts, asked, pool, new_rows, plan, after=()):
+    sizes = [size + (to is not None) for _, _, size, to in plan]
+    return pl.pallas_call(
+        functools.partial(gather_kernel, plan, len(asked), pool.shape[2]),
+        out_shape=[jax.ShapeDtypeStruct((size,) + pool.shape[1:], pool.dtype) for size in sizes],
+        in_specs=[SMEM] * (1 + len(asked)) + [VMEM] * 2 + [ANY] * len(after),
+        out_specs=[ANY] * len(plan),
+        scratch_shapes=[pltpu.SemaphoreType.DMA((sum(sizes),))],
+        compiler_params=pltpu.CompilerParams(vmem_limit_bytes=VMEM_LIMIT),
+        cost_estimate=pl.CostEstimate(
+            flops=0, bytes_accessed=4 * sum(sizes) * math.prod(pool.shape[1:]), transcendentals=0
+        ),
+    )(counts, *asked, pool, new_rows, *after)
+
+
+def write_back_kernel(capacity, block_rows, count, owner_ref, slot_ref, *refs):
+    asked, refs = refs[:count], refs[count:]
+    pool_ref, new_ref, fresh, refs = refs[0], refs[1], refs[2 : count + 2], refs[count + 2 :]
+    out_ref, sems, last = refs
+    me = lax.axis_index("blk")
+    copies = [
+        pltpu.make_async_copy(pool_ref.at[b], out_ref.at[b], sems.at[b])
+        for b in range(pool_ref.shape[0])
+    ]
     for copy in copies:
         copy.start()
     for copy in copies:
         copy.wait()
 
-
-def pick_fresh(counts, new_rows, block_rows, num_blk):
-    shape = jax.ShapeDtypeStruct((2, block_rows, new_rows.shape[2]), new_rows.dtype)
-    return pl.pallas_call(
-        functools.partial(pick_fresh_kernel, num_blk, block_rows),
-        out_shape=[shape] * (num_blk - 1),
-        in_specs=[SMEM, HBM],
-        out_specs=[HBM] * (num_blk - 1),
-        scratch_shapes=[
-            pltpu.VMEM(new_rows.shape, new_rows.dtype),
-            pltpu.SemaphoreType.DMA,
-            pltpu.SemaphoreType.DMA((num_blk - 1,)),
-        ],
-        compiler_params=pltpu.CompilerParams(vmem_limit_bytes=VMEM_LIMIT),
-    )(counts, new_rows)
-
-
-def gather_kernel(plan, count, *refs):
-    asked, pool_ref, refs = refs[:count], refs[count], refs[-len(plan) - 3 :]
-    outs, held, in_sems, out_sems = refs[:-3], refs[-3], refs[-2], refs[-1]
-    moves = []
-    for (row, start, size), out in zip(plan, outs):
-        for place in range(size):
-            i = len(moves)
-            load = pltpu.make_async_copy(
-                pool_ref.at[asked[row][0, start + place]], held.at[i], in_sems.at[i]
-            )
-            moves.append((load, pltpu.make_async_copy(held.at[i], out.at[place], out_sems.at[i])))
-            load.start()
-    for load, store in moves:
-        load.wait()
-        store.start()
-    for load, store in moves:
-        store.wait()
-
-
-def gather(asked, pool, plan, after=()):
-    shapes = [jax.ShapeDtypeStruct((size,) + pool.shape[1:], pool.dtype) for _, _, size in plan]
-    blocks = sum(size for _, _, size in plan)
-    return pl.pallas_call(
-        functools.partial(gather_kernel, plan, len(asked)),
-        out_shape=shapes,
-        in_specs=[SMEM] * len(asked) + [HBM] + [ANY] * len(after),
-        out_specs=[HBM] * len(shapes),
-        scratch_shapes=[
-            pltpu.VMEM((blocks,) + pool.shape[1:], pool.dtype),
-            pltpu.SemaphoreType.DMA((blocks,)),
-            pltpu.SemaphoreType.DMA((blocks,)),
-        ],
-        compiler_params=pltpu.CompilerParams(vmem_limit_bytes=VMEM_LIMIT),
-        cost_estimate=pl.CostEstimate(
-            flops=0, bytes_accessed=4 * blocks * math.prod(pool.shape[1:]), transcendentals=0
-        ),
-    )(*asked, pool, *after)
-
-
-def write_back_kernel(capacity, block_rows, count, owner_ref, slot_ref, *refs):
-    asked, refs = refs[:count], refs[count:]
-    pool_ref, new_ref, refs = refs[0], refs[1], refs[2:]
-    fresh, (out_ref, held, sems, last) = refs[:count], refs[-4:]
-    me = lax.axis_index("blk")
-    blocks = range(pool_ref.shape[0])
-    loads = [pltpu.make_async_copy(pool_ref.at[b], held.at[b], sems.at[b]) for b in blocks]
-    stores = [pltpu.make_async_copy(held.at[b], out_ref.at[b], sems.at[b]) for b in blocks]
-    for load in loads:
-        load.start()
-    for load in loads:
-        load.wait()
-
     def put(wanted, src, slot):
         @pl.when(wanted)
         def write():
-            copy = pltpu.make_async_copy(src, held.at[slot], last)
+            copy = pltpu.make_async_copy(src, out_ref.at[slot], last)
             copy.start()
             copy.wait()
 
     for i in range(count):
         slot = asked[i][0, capacity]
-        put(slot >= 0, fresh[i], slot)
+        put(slot >= 0, fresh[i].at[fresh[i].shape[0] - 1], slot)
     for b in range(owner_ref.shape[1]):
         rows = pl.ds(b * block_rows, block_rows)
         put(owner_ref[0, b] == me, new_ref.at[:, rows], slot_ref[0, b])
-    for store in stores:
-        store.start()
-    for store in stores:
-        store.wait()
-
-
-def write_back(write_owner, write_slot, asked, pool, new_rows, fresh, capacity, after):
+
+
+def write_back(write_owner, write_slot, asked, pool, new_rows, fresh, capacity):
     count = len(asked)
     return pl.pallas_call(
         functools.partial(write_back_kernel, capacity, pool.shape[2], count),
         out_shape=jax.ShapeDtypeStruct(pool.shape, pool.dtype),
-        in_specs=[SMEM] * (count + 2) + [HBM] * (count + 2) + [ANY] * len(after),
-        out_specs=HBM,
+        in_specs=[SMEM] * (count + 2) + [VMEM] * (count + 2),
+        out_specs=ANY,
         scratch_shapes=[
-            pltpu.VMEM(pool.shape, pool.dtype),
             pltpu.SemaphoreType.DMA((pool.shape[0],)),
             pltpu.SemaphoreType.DMA,
         ],
@@ -203,11 +163,16 @@
         cost_estimate=pl.CostEstimate(
             flops=0, bytes_accessed=4 * math.prod(pool.shape), transcendentals=0
         ),
-    )(write_owner, write_slot, *asked, pool, new_rows, *fresh, *after)
-
-
-def attend_kernel(spans, kv_dev, group, block_tok, rows, first, final, count_ref, q_ref, *refs):
+    )(write_owner, write_slot, *asked, pool, new_rows, *fresh)
+
+
+def attend_kernel(
+    spans, relays, kv_dev, group, block_tok, rows, first, final, count_ref, q_ref, *refs
+):
     parts, refs = refs[: len(spans)], refs[len(spans) :]
+    ins = 1 if first else 2
+    outs = 1 if final else 3 if first else 2
+    refs = refs[:ins] + refs[ins + relays : ins + relays + outs] + refs[-3:]
     if first:
         new_ref, q_out, acc_out, stat_out = refs[:4]
         head_dim = q_ref.shape[2]
@@ -336,7 +301,9 @@
         run(True)
 
 
-def attend(counts, queries, parts, spans, kv_dev, block_tok, new_rows, state, final):
+def attend(
+    counts, queries, parts, spans, kv_dev, block_tok, new_rows=None, state=None, final=False, relay=()
+):
     suffix, heads_dev, head_dim = queries.shape
     group = heads_dev // kv_dev
     first = state is None
@@ -352,12 +319,19 @@
         out_shape = state_shape
     else:
         operands = [state[0], *parts, *state[1:]]
-        out_shape = jax.ShapeDtypeStruct(queries.shape, queries.dtype) if final else state_shape[1:]
+        out_shape = state_shape[1:]
+        if final:
+            out_shape = [jax.ShapeDtypeStruct(queries.shape, queries.dtype)]
     result = pl.pallas_call(
-        functools.partial(attend_kernel, spans, kv_dev, group, block_tok, rows, first, final),
-        out_shape=out_shape,
-        in_specs=[SMEM] + [VMEM] * len(operands),
-        out_specs=VMEM if final else [VMEM] * len(out_shape),
+        functools.partial(
+            attend_kernel, spans, len(relay), kv_dev, group, block_tok, rows, first, final
+        ),
+        out_shape=out_shape + [jax.ShapeDtypeStruct(x.shape, x.dtype) for x in relay],
+        in_specs=[SMEM] + [VMEM] * len(operands) + [ANY] * len(relay),
+        out_specs=[VMEM] * len(out_shape) + [ANY] * len(relay),
+        input_output_aliases={
+            1 + len(operands) + i: len(out_shape) + i for i in range(len(relay))
+        },
         scratch_shapes=[
             pltpu.VMEM((kv_dev, keys, head_dim), jnp.bfloat16),
             pltpu.VMEM((kv_dev, head_dim + 16, keys), jnp.bfloat16),
@@ -369,10 +343,9 @@
             bytes_accessed=keys * kv_dev * head_dim * 4 + 16 * suffix * heads_dev * head_dim,
             transcendentals=suffix * heads_dev * keys,
         ),
-    )(counts, *operands)
-    if first or final:
-        return result
-    return [state[0], *result]
+    )(counts, *operands, *relay)
+    step, relayed = result[: len(out_shape)], result[len(out_shape) :]
+    return (step if first or final else [state[0], *step]), relayed
 
 
 def per_device(
@@ -394,68 +367,62 @@
         prefix_slot, prefix_owner, prefix_len, write_slot, write_owner, capacity, num_blk
     )
     asked = {d: shift(asks[d], d) for d in shifts}
-    fresh = pick_fresh(counts, new_rows, block_tok * kv_dev, num_blk)
-    arrived_fresh = {d: shift(fresh[d - 1], d) for d in shifts}
-
-    levels = []
-    left = capacity
-    for size in LEVELS:
-        if left:
-            levels.append((capacity - left, min(size, left)))
-            left -= min(size, left)
-    if left:
-        levels.append((capacity - left, left))
-
-    arrived = {}
-
-    def send(start, size, after):
-        plan = tuple((i, start, size) for i in range(num_blk - 1))
-        sent = gather([asked[d] for d in shifts], pool_rows, plan, after)
-        for d, blocks in zip(shifts, sent):
-            arrived[start, d] = shift(blocks, num_blk - d)
-        return sent
-
-    sent = send(*levels[0], ())
-    (local,) = gather([asks[0]], pool_rows, ((0, 0, capacity),), sent[:1])
-    state = attend(
-        counts,
-        queries[0],
-        [local],
-        ((0, 0, capacity),),
-        kv_dev,
-        block_tok,
+    rows = [asked[d] for d in shifts]
+
+    most, half = 3 * capacity // 4, capacity // 2
+    plans = [
+        [(d, 0, most if d == shifts[0] else half) for d in shifts],
+        [(d, half, capacity - half) for d in shifts[1:]],
+        [(shifts[0], most, capacity - most)],
+    ]
+
+    def load(plan, first, after=()):
+        return gather(
+            counts,
+            rows,
+            pool_rows,
+            new_rows,
+            tuple(
+                (shifts.index(d), start, size, num_blk - d if first else None)
+                for d, start, size in plan
+            ),
+            after,
+        )
+
+    def send(plan, blocks):
+        return [shift(x, num_blk - d) for (d, _, _), x in zip(plan, blocks)]
+
+    loaded = load(plans[0], True)
+    arrived = [send(plans[0], loaded)]
+    local = gather(counts, [asks[0]], pool_rows, new_rows, ((0, 0, capacity, None),), loaded[:1])
+    step = functools.partial(attend, counts, queries[0], kv_dev=kv_dev, block_tok=block_tok)
+    state, _ = step(local, ((0, 0, capacity),), new_rows=new_rows)
+
+    later = load(plans[1] + plans[2], False, [arrived[0][1], state[2]])
+    arrived.append(send(plans[1], later[: len(plans[1])]))
+    for i, plan in enumerate(plans):
+        groups = [slice(at, at + 8) for at in range(0, len(plan), 8)]
+        for j, group in enumerate(groups):
+            ends = j == len(groups) - 1
+            state, relayed = step(
+                arrived[i][group],
+                tuple(plan[group]),
+                state=state,
+                final=ends and i == len(plans) - 1,
+                relay=later[len(plans[1]) :] if ends and i == 0 else [],
+            )
+            if relayed:
+                arrived.append(send(plans[2], relayed))
+    new_pool = write_back(
+        write_owner,
+        write_slot,
+        [asked[num_blk - d] for d in shifts],
+        pool_rows,
         new_rows,
-        None,
-        False,
-    )
-    for i, (start, size) in enumerate(levels):
-        if i + 1 < len(levels):
-            send(*levels[i + 1], state[2:])
-        for at in range(0, len(shifts), 4):
-            spans = tuple((d, start, size) for d in shifts[at : at + 4])
-            state = attend(
-                counts,
-                queries[0],
-                [arrived[start, d] for d, _, _ in spans],
-                spans,
-                kv_dev,
-                block_tok,
-                None,
-                state,
-                i == len(levels) - 1 and at + 4 >= len(shifts),
-            )
-        if i == 0:
-            new_pool = write_back(
-                write_owner,
-                write_slot,
-                [asked[d] for d in shifts],
-                pool_rows,
-                new_rows,
-                [arrived_fresh[d] for d in shifts],
-                capacity,
-                state[2:],
-            )
-    return state[None], new_pool.reshape(pool.shape)
+        arrived[0],
+        capacity,
+    )
+    return state[0][None], new_pool.reshape(pool.shape)
 
 
 def solution(mesh):

time: 134 us -> 132 us (0.985)
  the two profiles are of different devices: /device:TPU:0 before, /device:TPU:14 now
where the time goes in v3:
time: 132 us
  waiting for transfers between devices  65 us (49%)
  Pallas kernels  48.8 us (37%)
  starting transfers between devices  13.5 us (10%)
  local copies, waits for them, and re-layouts  3.53 us (3%)
  between operations  1.43 us (1%)
    ppermute x9, waiting for transfers between devices, shift(): lax.ppermute(array, 'blk', [(i, (i + d) % num_blk) for i in range(num_blk)])  65 us
    pallas_call x4, Pallas kernels, attend(): pl.pallas_call(functools.partial(attend_kernel, spans, len(relay), kv_dev...  35.7 us
    ppermute x9, starting transfers between devices, shift(): lax.ppermute(array, 'blk', [(i, (i + d) % num_blk) for i in range(num_blk)])  13.5 us
    pallas_call x3, Pallas kernels, gather(): pl.pallas_call(functools.partial(gather_kernel, plan, len(asked), pool.sh...  7.8 us
    pallas_call x1, Pallas kernels, write_back(): pl.pallas_call(functools.partial(write_back_kernel, capacity, pool.shape[...  3.74 us
    unnamed x20, local copies, waits for them, and re-layouts  3.53 us
  transfers between devices with their start and end apart: 9, of which 4 were waited for; matrix products, arithmetic and copies ran while one was open for 0% of the time, Pallas kernels for 30%

profile of v3, /device:TPU:14, one launch (start us, length us, event | category | flops | bytes accessed | tf_op | source)
XLA Modules:
  0.0 132.2 jit_solution(13074432758602626674)
XLA Ops:
  1.3 1.5 %shard_map.95 = (s32[1,8]{1,0:T(1,128)}, s32[1,9]{1,0:T(1,128)}, s32[1,9]{1,0:T(1,128)}, s32[1,9]{1,0:T(1,128)}, s32[1,9]{1,0:T(1,128)}) custom-call(s32[1,32]{1,0:T(1,128)} %refs_0_.1, s32[1,32]{1,0:T(1,128)} %refs_1_.1, s32[1]{0:T(128)S(6)} %copy.12.refs_2_, s32[1,2]{1,0:T(1,128)} %slot_ref.1, s32[1,2]{1,0:T(1,128)} %owner_ref.1), custom_call_target="tpu_custom_call" | custom-call | tf_op jit(solution)/shard_map/pallas_call | solution.py:69
  2.8 0.0 copy-start.8
  2.8 2.7 %collective-permute-start = (s32[1,9]{1,0:T(1,128)}, s32[1,9]{1,0:T(1,128)S(1)}, u32[]{:S(2)}, u32[]{:S(2)}) collective-permute-start(s32[1,9]{1,0:T(1,128)} %get-tuple-element.23), channel_id=1, source_target_pairs={{0,8},{4,12},{8,0},{12,4},{1,9},{5,13},{9,1},{13,5},{2,10},{6,14},... | collective-permute-start | bytes 116 | tf_op jit(solution)/shard_map/ppermute | solution.py:364
  5.5 0.0 collective-permute-start.1
  5.5 2.0 %collective-permute-start.2 = (s32[1,9]{1,0:T(1,128)}, s32[1,9]{1,0:T(1,128)S(1)}, u32[]{:S(2)}, u32[]{:S(2)}) collective-permute-start(s32[1,9]{1,0:T(1,128)} %get-tuple-element.25), channel_id=1, source_target_pairs={{0,12},{4,0},{8,4},{12,8},{1,13},{5,1},{9,5},{13,9},{2,14},{6,2},{... | collective-permute-start | bytes 116 | tf_op jit(solution)/shard_map/ppermute | solution.py:364
  7.5 0.0 collective-permute-done.refs_0_
  7.5 1.7 %collective-permute-done.1.refs_1_.refs_2_ = s32[1,9]{1,0:T(1,128)S(1)} collective-permute-done((s32[1,9]{1,0:T(1,128)}, s32[1,9]{1,0:T(1,128)S(1)}, u32[]{:S(2)}, u32[]{:S(2)}) %collective-permute-start.1) | collective-permute-done | bytes 68 | tf_op jit(solution)/shard_map/ppermute | solution.py:364
  9.2 0.0 collective-permute-done.2.refs_2_.refs_1_
  9.2 0.0 copy-start
  9.2 1.9 %copy-done = bf16[24,2,128,2,128]{4,3,2,1,0:T(2,128)(2,1)S(1)} copy-done((bf16[24,2,128,2,128]{4,3,2,1,0:T(2,128)(2,1)S(1)}, bf16[24,2,128,2,128]{4,3,2,1,0:T(2,128)(2,1)}, u32[]{:S(2)}) %copy-start) | copy-done | bytes 3145752
  11.1 0.0 copy-start.2
  11.1 0.9 copy-done.2
  12.1 0.0 copy-start.4
  12.1 0.7 copy-done.4
  12.7 0.0 copy-start.1
  12.7 0.0 copy-start.3
  12.7 3.4 %shard_map.96 = (bf16[7,2,256,128]{3,2,1,0:T(8,128)(2,1)S(1)}, bf16[5,2,256,128]{3,2,1,0:T(8,128)(2,1)S(1)}, bf16[5,2,256,128]{3,2,1,0:T(8,128)(2,1)S(1)}) custom-call(s32[1,8]{1,0:T(1,128)S(1)} %copy-done.4, s32[1,9]{1,0:T(1,128)S(1)} %collective-permute-done.refs_0_, s32[1,9]{1,0:T(1,128)S(1)} %collective-permute-done.1.refs_1_.refs_2_, ...), custom_call_target="tpu_custom_call" | custom-call | bytes 4456448 | tf_op jit(solution)/shard_map/pallas_call | solution.py:109
  16.2 4.7 %collective-permute-start.3 = (bf16[7,2,256,128]{3,2,1,0:T(8,128)(2,1)S(1)}, bf16[7,2,256,128]{3,2,1,0:T(8,128)(2,1)S(1)}, u32[]{:S(2)}, u32[]{:S(2)}) collective-permute-start(bf16[7,2,256,128]{3,2,1,0:T(8,128)(2,1)S(1)} %get-tuple-element.26.refs_3_), channel_id=1, source_target_pairs={{0,8},{4,12},{8,0},{12,4},{1,9},{5,13},{9,1},{13,5},{2,10},{6,14},... | collective-permute-start | bytes 2752520 | tf_op jit(solution)/shard_map/ppermute | solution.py:364
  20.8 0.0 collective-permute-start.4
  20.8 2.0 %collective-permute-start.5 = (bf16[5,2,256,128]{3,2,1,0:T(8,128)(2,1)S(1)}, bf16[5,2,256,128]{3,2,1,0:T(8,128)(2,1)S(1)}, u32[]{:S(2)}, u32[]{:S(2)}) collective-permute-start(bf16[5,2,256,128]{3,2,1,0:T(8,128)(2,1)S(1)} %get-tuple-element.29), channel_id=1, source_target_pairs={{0,4},{4,8},{8,12},{12,0},{1,5},{5,9},{9,13},{13,1},{2,6},{6,10},{... | collective-permute-start | bytes 1966088 | tf_op jit(solution)/shard_map/ppermute | solution.py:364
  22.9 0.0 copy-done.8
  22.9 0.0 copy-done.1
  22.9 0.0 copy-done.3
  22.9 0.0 copy-start.5
  22.9 0.0 copy-start.9
  22.9 2.0 %shard_map.97.refs_0_ = bf16[8,2,256,128]{3,2,1,0:T(8,128)(2,1)S(1)} custom-call(s32[1,8]{1,0:T(1,128)S(1)} %copy-done.4, s32[1,9]{1,0:T(1,128)S(1)} %copy-done.8, bf16[24,2,256,128]{3,2,1,0:T(8,128)(2,1)S(1)} %bitcast.6, bf16[2,512,128]{2,1,0:T(8,128)(2,1)S(1)} %bitcast.10, bf16[7,2,256,128]{3,2,1,0:T(8,128)(2,1)S(1)} %get-tuple-element.26.refs_3_), custom_call_target="tpu_custom_call" | custom-call | bytes 2097152 | tf_op jit(solution)/shard_map/pallas_call | solution.py:109
  24.9 0.0 copy-done.5
  24.9 0.0 copy-done.9
  24.9 9.0 %shard_map.98 = (bf16[2,2048,128]{2,1,0:T(8,128)(2,1)S(1)}, f32[2,128,2048]{2,1,0:T(8,128)S(1)}, f32[2,8,2048]{2,1,0:T(8,128)S(1)}) custom-call(s32[1,8]{1,0:T(1,128)S(1)} %copy-done.5, bf16[256,16,128]{2,1,0:T(8,128)(2,1)S(1)} %bitcast.14, bf16[8,2,256,128]{3,2,1,0:T(8,128)(2,1)S(1)} %shard_map.97.refs_0_, bf16[2,512,128]{2,1,0:T(8,128)(2,1)S(1)} %bitcast.11), custom_call_target="tpu_custom_call" | custom-call | flops 2684354560 | bytes 9699328 | tf_op jit(solution)/shard_map/pallas_call | solution.py:325
  34.0 52.2 %collective-permute-done.4.refs_5_.refs_1_.refs_6_ = bf16[5,2,256,128]{3,2,1,0:T(8,128)(2,1)S(1)} collective-permute-done((bf16[5,2,256,128]{3,2,1,0:T(8,128)(2,1)S(1)}, bf16[5,2,256,128]{3,2,1,0:T(8,128)(2,1)S(1)}, u32[]{:S(2)}, u32[]{:S(2)}) %collective-permute-start.4) | collective-permute-done | bytes 655392 | tf_op jit(solution)/shard_map/ppermute | solution.py:364
  86.2 2.4 %shard_map.99 = (bf16[4,2,256,128]{3,2,1,0:T(8,128)(2,1)S(1)}, bf16[4,2,256,128]{3,2,1,0:T(8,128)(2,1)S(1)}, bf16[2,2,256,128]{3,2,1,0:T(8,128)(2,1)S(1)}) custom-call(s32[1,8]{1,0:T(1,128)S(1)} %copy-done.5, s32[1,9]{1,0:T(1,128)S(1)} %collective-permute-done.refs_0_, s32[1,9]{1,0:T(1,128)S(1)} %collective-permute-done.1.refs_1_.refs_2_, ...), custom_call_target="tpu_custom_call" | custom-call | bytes 2621440 | tf_op jit(solution)/shard_map/pallas_call | solution.py:109
  88.6 0.1 collective-permute-start.7
  88.6 2.0 %collective-permute-start.8 = (bf16[4,2,256,128]{3,2,1,0:T(8,128)(2,1)S(1)}, bf16[4,2,256,128]{3,2,1,0:T(8,128)(2,1)S(1)}, u32[]{:S(2)}, u32[]{:S(2)}) collective-permute-start(bf16[4,2,256,128]{3,2,1,0:T(8,128)(2,1)S(1)} %get-tuple-element.35), channel_id=1, source_target_pairs={{0,4},{4,8},{8,12},{12,0},{1,5},{5,9},{9,13},{13,1},{2,6},{6,10},{... | collective-permute-start | bytes 1572872 | tf_op jit(solution)/shard_map/ppermute | solution.py:364
  90.6 4.9 %collective-permute-done.5.refs_2_.refs_7_ = bf16[5,2,256,128]{3,2,1,0:T(8,128)(2,1)S(1)} collective-permute-done((bf16[5,2,256,128]{3,2,1,0:T(8,128)(2,1)S(1)}, bf16[5,2,256,128]{3,2,1,0:T(8,128)(2,1)S(1)}, u32[]{:S(2)}, u32[]{:S(2)}) %collective-permute-start.5) | collective-permute-done | bytes 655392 | tf_op jit(solution)/shard_map/ppermute | solution.py:364
  95.6 0.0 collective-permute-done.3.refs_0_.refs_5_
  95.6 0.0 copy-start.6
  95.6 0.0 copy-start.7
  95.6 13.7 %shard_map.100 = (f32[2,128,2048]{2,1,0:T(8,128)S(1)}, f32[2,8,2048]{2,1,0:T(8,128)S(1)}, bf16[2,2,256,128]{3,2,1,0:T(8,128)(2,1)S(1)}) custom-call(s32[1,8]{1,0:T(1,128)S(1)} %copy-done.5, bf16[2,2048,128]{2,1,0:T(8,128)(2,1)S(1)} %get-tuple-element.27.q_ref, ...), custom_call_target="tpu_custom_call", output_to_operand_aliasing={{2}: (7, {})} | custom-call | flops 3758096384 | bytes 10223616 | tf_op jit(solution)/shard_map/pallas_call | solution.py:325
  109.3 0.1 collective-permute-start.6
  109.4 0.0 copy-done.6
  109.4 0.0 copy-done.7
  109.4 3.7 %shard_map.103 = bf16[24,2,256,128]{3,2,1,0:T(8,128)(2,1)} custom-call(s32[1,2]{1,0:T(1,128)S(1)} %copy-done.7, s32[1,2]{1,0:T(1,128)S(1)} %copy-done.6, s32[1,9]{1,0:T(1,128)S(1)} %collective-permute-done.refs_0_, s32[1,9]{1,0:T(1,128)S(1)} %collective-permute-done.2.refs_2_.refs_1_, s32[1,9]{1,0:T(1,128)S(1)} %collective-permute-done.1.refs_1_.refs_2_, ...), custom_call_target="tpu_custom_call" | custom-call | bytes 6291456 | tf_op jit(solution)/shard_map/pallas_call | solution.py:153
  113.1 6.1 %collective-permute-done.7.refs_0_ = bf16[4,2,256,128]{3,2,1,0:T(8,128)(2,1)S(1)} collective-permute-done((bf16[4,2,256,128]{3,2,1,0:T(8,128)(2,1)S(1)}, bf16[4,2,256,128]{3,2,1,0:T(8,128)(2,1)S(1)}, u32[]{:S(2)}, u32[]{:S(2)}) %collective-permute-start.7) | collective-permute-done | bytes 524320 | tf_op jit(solution)/shard_map/ppermute | solution.py:364
  119.2 0.0 collective-permute-done.8.refs_1_
  119.2 8.7 %shard_map.101 = (f32[2,128,2048]{2,1,0:T(8,128)S(1)}, f32[2,8,2048]{2,1,0:T(8,128)S(1)}) custom-call(s32[1,8]{1,0:T(1,128)S(1)} %copy-done.5, bf16[2,2048,128]{2,1,0:T(8,128)(2,1)S(1)} %get-tuple-element.27.q_ref, bf16[4,2,256,128]{3,2,1,0:T(8,128)(2,1)S(1)} %collective-permute-done.7.refs_0_, bf16[4,2,256,128]{3,2,1,0:T(8,128)(2,1)S(1)} %collective-permute-done.8.refs_1_, ...), custom_call_target="tpu_custom_call" | custom-call | flops 2147483648 | bytes 9437184 | tf_op jit(solution)/shard_map/pallas_call | solution.py:325
  127.9 0.0 collective-permute-done.6.refs_0_
  127.9 4.3 %shard_map.102 = bf16[256,16,128]{2,1,0:T(8,128)(2,1)} custom-call(s32[1,8]{1,0:T(1,128)S(1)} %copy-done.5, bf16[2,2048,128]{2,1,0:T(8,128)(2,1)S(1)} %get-tuple-element.27.q_ref, bf16[2,2,256,128]{3,2,1,0:T(8,128)(2,1)S(1)} %collective-permute-done.6.refs_0_, f32[2,128,2048]{2,1,0:T(8,128)S(1)} %get-tuple-element.38.refs_1_, ...), custom_call_target="tpu_custom_call" | custom-call | flops 536870912 | bytes 8650752 | tf_op jit(solution)/shard_map/pallas_call | solution.py:325
Async XLA Ops:
  2.8 20.0 %copy-start.8 = (s32[1,9]{1,0:T(1,128)S(1)}, s32[1,9]{1,0:T(1,128)}, u32[]{:S(2)}) copy-start(s32[1,9]{1,0:T(1,128)} %get-tuple-element.22.refs_0_) | copy-start | bytes 112
  2.8 4.7 %collective-permute-start = (s32[1,9]{1,0:T(1,128)}, s32[1,9]{1,0:T(1,128)S(1)}, u32[]{:S(2)}, u32[]{:S(2)}) collective-permute-start(s32[1,9]{1,0:T(1,128)} %get-tuple-element.23), channel_id=1, source_target_pairs={{0,8},{4,12},{8,0},{12,4},{1,9},{5,13},{9,1},{13,5},{2,10},{6,14},... | collective-permute-start | bytes 116 | tf_op jit(solution)/shard_map/ppermute | solution.py:364
  5.5 3.8 %collective-permute-start.1 = (s32[1,9]{1,0:T(1,128)}, s32[1,9]{1,0:T(1,128)S(1)}, u32[]{:S(2)}, u32[]{:S(2)}) collective-permute-start(s32[1,9]{1,0:T(1,128)} %get-tuple-element.24), channel_id=1, source_target_pairs={{0,4},{4,8},{8,12},{12,0},{1,5},{5,9},{9,13},{13,1},{2,6},{6,10},{... | collective-permute-start | bytes 116 | tf_op jit(solution)/shard_map/ppermute | solution.py:364
  5.5 3.8 %collective-permute-start.2 = (s32[1,9]{1,0:T(1,128)}, s32[1,9]{1,0:T(1,128)S(1)}, u32[]{:S(2)}, u32[]{:S(2)}) collective-permute-start(s32[1,9]{1,0:T(1,128)} %get-tuple-element.25), channel_id=1, source_target_pairs={{0,12},{4,0},{8,4},{12,8},{1,13},{5,1},{9,5},{13,9},{2,14},{6,2},{... | collective-permute-start | bytes 116 | tf_op jit(solution)/shard_map/ppermute | solution.py:364
  9.2 1.9 %copy-start = (bf16[24,2,128,2,128]{4,3,2,1,0:T(2,128)(2,1)S(1)}, bf16[24,2,128,2,128]{4,3,2,1,0:T(2,128)(2,1)}, u32[]{:S(2)}) copy-start(bf16[24,2,128,2,128]{4,3,2,1,0:T(2,128)(2,1)} %param.10) | copy-start | bytes 9437188
  11.1 0.9 copy-start.2
  12.1 0.7 copy-start.4
  12.7 10.1 %copy-start.1 = (bf16[24,2,128,2,128]{4,3,2,1,0:T(2,128)(2,1)S(1)}, bf16[24,2,128,2,128]{4,3,2,1,0:T(2,128)(2,1)}, u32[]{:S(2)}) copy-start(bf16[24,2,128,2,128]{4,3,2,1,0:T(2,128)(2,1)} %param.10) | copy-start | bytes 9437188
  12.7 10.1 %copy-start.3 = (bf16[2,1,256,2,128]{4,3,2,1,0:T(2,128)(2,1)S(1)}, bf16[2,1,256,2,128]{4,3,2,1,0:T(2,128)(2,1)}, u32[]{:S(2)}) copy-start(bf16[2,1,256,2,128]{4,3,2,1,0:T(2,128)(2,1)} %param.9) | copy-start | bytes 786436
  16.2 79.4 %collective-permute-start.3 = (bf16[7,2,256,128]{3,2,1,0:T(8,128)(2,1)S(1)}, bf16[7,2,256,128]{3,2,1,0:T(8,128)(2,1)S(1)}, u32[]{:S(2)}, u32[]{:S(2)}) collective-permute-start(bf16[7,2,256,128]{3,2,1,0:T(8,128)(2,1)S(1)} %get-tuple-element.26.refs_3_), channel_id=1, source_target_pairs={{0,8},{4,12},{8,0},{12,4},{1,9},{5,13},{9,1},{13,5},{2,10},{6,14},... | collective-permute-start | bytes 2752520 | tf_op jit(solution)/shard_map/ppermute | solution.py:364
  20.8 65.3 %collective-permute-start.4 = (bf16[5,2,256,128]{3,2,1,0:T(8,128)(2,1)S(1)}, bf16[5,2,256,128]{3,2,1,0:T(8,128)(2,1)S(1)}, u32[]{:S(2)}, u32[]{:S(2)}) collective-permute-start(bf16[5,2,256,128]{3,2,1,0:T(8,128)(2,1)S(1)} %get-tuple-element.28), channel_id=1, source_target_pairs={{0,12},{4,0},{8,4},{12,8},{1,13},{5,1},{9,5},{13,9},{2,14},{6,2},{... | collective-permute-start | bytes 1966088 | tf_op jit(solution)/shard_map/ppermute | solution.py:364
  20.8 74.7 %collective-permute-start.5 = (bf16[5,2,256,128]{3,2,1,0:T(8,128)(2,1)S(1)}, bf16[5,2,256,128]{3,2,1,0:T(8,128)(2,1)S(1)}, u32[]{:S(2)}, u32[]{:S(2)}) collective-permute-start(bf16[5,2,256,128]{3,2,1,0:T(8,128)(2,1)S(1)} %get-tuple-element.29), channel_id=1, source_target_pairs={{0,4},{4,8},{8,12},{12,0},{1,5},{5,9},{9,13},{13,1},{2,6},{6,10},{... | collective-permute-start | bytes 1966088 | tf_op jit(solution)/shard_map/ppermute | solution.py:364
  22.9 2.0 %copy-start.5 = (s32[1,8]{1,0:T(1,128)S(1)}, s32[1,8]{1,0:T(1,128)}, u32[]{:S(2)}) copy-start(s32[1,8]{1,0:T(1,128)} %get-tuple-element.21.count_ref) | copy-start | bytes 100
  22.9 2.0 %copy-start.9 = (bf16[1,256,16,128]{3,2,1,0:T(8,128)(2,1)S(1)}, bf16[1,256,16,128]{3,2,1,0:T(8,128)(2,1)}, u32[]{:S(2)}) copy-start(bf16[1,256,16,128]{3,2,1,0:T(8,128)(2,1)} %param.8) | copy-start | bytes 3145732
  88.6 30.6 %collective-permute-start.7 = (bf16[4,2,256,128]{3,2,1,0:T(8,128)(2,1)S(1)}, bf16[4,2,256,128]{3,2,1,0:T(8,128)(2,1)S(1)}, u32[]{:S(2)}, u32[]{:S(2)}) collective-permute-start(bf16[4,2,256,128]{3,2,1,0:T(8,128)(2,1)S(1)} %get-tuple-element.34), channel_id=1, source_target_pairs={{0,12},{4,0},{8,4},{12,8},{1,13},{5,1},{9,5},{13,9},{2,14},{6,2},{... | collective-permute-start | bytes 1572872 | tf_op jit(solution)/shard_map/ppermute | solution.py:364
  88.6 30.6 %collective-permute-start.8 = (bf16[4,2,256,128]{3,2,1,0:T(8,128)(2,1)S(1)}, bf16[4,2,256,128]{3,2,1,0:T(8,128)(2,1)S(1)}, u32[]{:S(2)}, u32[]{:S(2)}) collective-permute-start(bf16[4,2,256,128]{3,2,1,0:T(8,128)(2,1)S(1)} %get-tuple-element.35), channel_id=1, source_target_pairs={{0,4},{4,8},{8,12},{12,0},{1,5},{5,9},{9,13},{13,1},{2,6},{6,10},{... | collective-permute-start | bytes 1572872 | tf_op jit(solution)/shard_map/ppermute | solution.py:364
  95.6 13.8 %copy-start.6 = (s32[1,2]{1,0:T(1,128)S(1)}, s32[1,2]{1,0:T(1,128)}, u32[]{:S(2)}) copy-start(s32[1,2]{1,0:T(1,128)} %slot_ref.1) | copy-start | bytes 28
  95.6 13.8 %copy-start.7 = (s32[1,2]{1,0:T(1,128)S(1)}, s32[1,2]{1,0:T(1,128)}, u32[]{:S(2)}) copy-start(s32[1,2]{1,0:T(1,128)} %owner_ref.1) | copy-start | bytes 28
  109.3 18.7 %collective-permute-start.6 = (bf16[2,2,256,128]{3,2,1,0:T(8,128)(2,1)S(1)}, bf16[2,2,256,128]{3,2,1,0:T(8,128)(2,1)S(1)}, u32[]{:S(2)}, u32[]{:S(2)}) collective-permute-start(bf16[2,2,256,128]{3,2,1,0:T(8,128)(2,1)S(1)} %get-tuple-element.33), channel_id=1, source_target_pairs={{0,8},{4,12},{8,0},{12,4},{1,9},{5,13},{9,1},{13,5},{2,10},{6,14},... | collective-permute-start | bytes 786440 | tf_op jit(solution)/shard_map/ppermute | solution.py:364

commit v4 on v3

--- a/solution.py
+++ b/solution.py
@@ -83,15 +83,23 @@
     return results[0], results[1:]
 
 
-def gather_kernel(plan, count, block_rows, count_ref, *refs):
+def gather_kernel(plan, count, block_rows, direct, count_ref, *refs):
     asked, pool_ref, new_ref = refs[:count], refs[count], refs[count + 1]
-    outs, sems = refs[-len(plan) - 1 : -1], refs[-1]
-    copies = []
+    refs = refs[-len(plan) - (1 if direct else 3) :]
+    outs, sems = refs[: len(plan)], refs[len(plan)]
+    moves = []
 
     def move(source, target):
-        copy = pltpu.make_async_copy(source, target, sems.at[len(copies)])
-        copy.start()
-        copies.append(copy)
+        i = len(moves)
+        if direct:
+            load, store = None, pltpu.make_async_copy(source, target, sems.at[i])
+            store.start()
+        else:
+            held, in_sems = refs[len(plan) + 1 :]
+            load = pltpu.make_async_copy(source, held.at[i], in_sems.at[i])
+            store = pltpu.make_async_copy(held.at[i], target, sems.at[i])
+            load.start()
+        moves.append((load, store))
 
     for (row, start, size, to), out in zip(plan, outs):
         for place in range(size):
@@ -100,21 +108,32 @@
             chosen = count_ref[0, count_ref.shape[1] // 2 + to]
             at = pl.ds(pl.multiple_of(chosen * block_rows, block_rows), block_rows)
             move(new_ref.at[:, at], out.at[size])
-    for copy in copies:
-        copy.wait()
-
-
-def gather(counts, asked, pool, new_rows, plan, after=()):
+    if not direct:
+        for load, store in moves:
+            load.wait()
+            store.start()
+    for _, store in moves:
+        store.wait()
+
+
+def gather(counts, asked, pool, new_rows, plan, after=(), direct=True):
     sizes = [size + (to is not None) for _, _, size, to in plan]
+    blocks = sum(size for size in sizes)
+    scratch = [pltpu.SemaphoreType.DMA((blocks,))]
+    if not direct:
+        scratch.append(pltpu.VMEM((blocks,) + pool.shape[1:], pool.dtype))
+        scratch.append(pltpu.SemaphoreType.DMA((blocks,)))
     return pl.pallas_call(
-        functools.partial(gather_kernel, plan, len(asked), pool.shape[2]),
+        functools.partial(gather_kernel, plan, len(asked), pool.shape[2], direct),
         out_shape=[jax.ShapeDtypeStruct((size,) + pool.shape[1:], pool.dtype) for size in sizes],
-        in_specs=[SMEM] * (1 + len(asked)) + [VMEM] * 2 + [ANY] * len(after),
-        out_specs=[ANY] * len(plan),
-        scratch_shapes=[pltpu.SemaphoreType.DMA((sum(sizes),))],
-        compiler_params=pltpu.CompilerParams(vmem_limit_bytes=VMEM_LIMIT),
+        in_specs=[SMEM] * (1 + len(asked)) + [VMEM if direct else HBM] * 2 + [ANY] * len(after),
+        out_specs=[ANY if direct else HBM] * len(plan),
+        scratch_shapes=scratch,
+        compiler_params=pltpu.CompilerParams(
+            vmem_limit_bytes=VMEM_LIMIT if direct else WHOLE_LIMIT
+        ),
         cost_estimate=pl.CostEstimate(
-            flops=0, bytes_accessed=4 * sum(sizes) * math.prod(pool.shape[1:]), transcendentals=0
+            flops=0, bytes_accessed=4 * blocks * math.prod(pool.shape[1:]), transcendentals=0
         ),
     )(counts, *asked, pool, new_rows, *after)
 
@@ -369,12 +388,9 @@
     asked = {d: shift(asks[d], d) for d in shifts}
     rows = [asked[d] for d in shifts]
 
-    most, half = 3 * capacity // 4, capacity // 2
-    plans = [
-        [(d, 0, most if d == shifts[0] else half) for d in shifts],
-        [(d, half, capacity - half) for d in shifts[1:]],
-        [(shifts[0], most, capacity - most)],
-    ]
+    first = max(1, 3 * capacity // 8)
+    cuts = sorted({0, first, min(2 * first, capacity), capacity - 1, capacity})
+    plans = [[(d, start, end - start) for d in shifts] for start, end in zip(cuts, cuts[1:])]
 
     def load(plan, first, after=()):
         return gather(
@@ -387,6 +403,7 @@
                 for d, start, size in plan
             ),
             after,
+            not first,
         )
 
     def send(plan, blocks):
@@ -398,9 +415,11 @@
     step = functools.partial(attend, counts, queries[0], kv_dev=kv_dev, block_tok=block_tok)
     state, _ = step(local, ((0, 0, capacity),), new_rows=new_rows)
 
-    later = load(plans[1] + plans[2], False, [arrived[0][1], state[2]])
-    arrived.append(send(plans[1], later[: len(plans[1])]))
+    later = load(sum(plans[1:], []), False, [state[2]])
+    waiting = [later[i * len(shifts) : (i + 1) * len(shifts)] for i in range(len(plans) - 1)]
+    arrived.append(send(plans[1], waiting[0]))
     for i, plan in enumerate(plans):
+        relay = waiting[i + 1] if i + 2 < len(plans) else []
         groups = [slice(at, at + 8) for at in range(0, len(plan), 8)]
         for j, group in enumerate(groups):
             ends = j == len(groups) - 1
@@ -409,10 +428,10 @@
                 tuple(plan[group]),
                 state=state,
                 final=ends and i == len(plans) - 1,
-                relay=later[len(plans[1]) :] if ends and i == 0 else [],
+                relay=relay if ends else [],
             )
-            if relayed:
-                arrived.append(send(plans[2], relayed))
+        if relay:
+            arrived.append(send(plans[i + 2], relayed))
     new_pool = write_back(
         write_owner,
         write_slot,

time: 132 us -> 131 us (level)
  the two profiles are of different devices: /device:TPU:14 before, /device:TPU:0 now
where the time goes in v4:
time: 131 us
  starting transfers between devices  54.7 us (42%)
  Pallas kernels  49.1 us (37%)
  waiting for transfers between devices  23.4 us (18%)
  between operations  1.68 us (1%)
  local copies, waits for them, and re-layouts  1.67 us (1%)
    ppermute x15, starting transfers between devices, shift(): lax.ppermute(array, 'blk', [(i, (i + d) % num_blk) for i in range(num_blk)])  54.7 us
    pallas_call x5, Pallas kernels, attend(): pl.pallas_call(functools.partial(attend_kernel, spans, len(relay), kv_dev...  35.4 us
    ppermute x15, waiting for transfers between devices, shift(): lax.ppermute(array, 'blk', [(i, (i + d) % num_blk) for i in range(num_blk)])  23.4 us
    pallas_call x3, Pallas kernels, gather(): pl.pallas_call(functools.partial(gather_kernel, plan, len(asked), pool.sh...  8.32 us
    pallas_call x1, Pallas kernels, write_back(): pl.pallas_call(functools.partial(write_back_kernel, capacity, pool.shape[...  3.73 us
  transfers between devices with their start and end apart: 15, of which 2 were waited for; matrix products, arithmetic and copies ran while one was open for 0% of the time, Pallas kernels for 30%

profile of v4, /device:TPU:0, one launch (start us, length us, event | category | flops | bytes accessed | tf_op | source)
XLA Modules:
  0.0 130.5 jit_solution(14898790739801773857)
XLA Ops:
  0.6 0.0 copy-start
  0.6 0.0 copy-start.1
  1.4 1.7 %shard_map.95 = (s32[1,8]{1,0:T(1,128)}, s32[1,9]{1,0:T(1,128)}, s32[1,9]{1,0:T(1,128)}, s32[1,9]{1,0:T(1,128)}, s32[1,9]{1,0:T(1,128)}) custom-call(s32[1,32]{1,0:T(1,128)} %refs_0_.1, s32[1,32]{1,0:T(1,128)} %refs_1_.1, s32[1]{0:T(128)S(6)} %copy.22.refs_2_, s32[1,2]{1,0:T(1,128)} %slot_ref.1, s32[1,2]{1,0:T(1,128)} %owner_ref.1), custom_call_target="tpu_custom_call" | custom-call | tf_op jit(solution)/shard_map/pallas_call | solution.py:69
  3.1 4.1 %collective-permute-start = (s32[1,9]{1,0:T(1,128)}, s32[1,9]{1,0:T(1,128)S(1)}, u32[]{:S(2)}, u32[]{:S(2)}) collective-permute-start(s32[1,9]{1,0:T(1,128)} %get-tuple-element.36), channel_id=1, source_target_pairs={{0,8},{4,12},{8,0},{12,4},{1,9},{5,13},{9,1},{13,5},{2,10},{6,14},... | collective-permute-start | bytes 116 | tf_op jit(solution)/shard_map/ppermute | solution.py:383
  7.2 1.6 %collective-permute-start.1 = (s32[1,9]{1,0:T(1,128)}, s32[1,9]{1,0:T(1,128)S(1)}, u32[]{:S(2)}, u32[]{:S(2)}) collective-permute-start(s32[1,9]{1,0:T(1,128)} %get-tuple-element.37), channel_id=1, source_target_pairs={{0,4},{4,8},{8,12},{12,0},{1,5},{5,9},{9,13},{13,1},{2,6},{6,10},{... | collective-permute-start | bytes 116 | tf_op jit(solution)/shard_map/ppermute | solution.py:383
  8.8 2.2 %collective-permute-start.2 = (s32[1,9]{1,0:T(1,128)}, s32[1,9]{1,0:T(1,128)S(1)}, u32[]{:S(2)}, u32[]{:S(2)}) collective-permute-start(s32[1,9]{1,0:T(1,128)} %get-tuple-element.38), channel_id=1, source_target_pairs={{0,12},{4,0},{8,4},{12,8},{1,13},{5,1},{9,5},{13,9},{2,14},{6,2},{... | collective-permute-start | bytes 116 | tf_op jit(solution)/shard_map/ppermute | solution.py:383
  11.1 0.0 collective-permute-done.refs_0_
  11.1 1.6 %collective-permute-done.1.refs_1_.refs_2_ = s32[1,9]{1,0:T(1,128)S(1)} collective-permute-done((s32[1,9]{1,0:T(1,128)}, s32[1,9]{1,0:T(1,128)S(1)}, u32[]{:S(2)}, u32[]{:S(2)}) %collective-permute-start.1) | collective-permute-done | bytes 68 | tf_op jit(solution)/shard_map/ppermute | solution.py:383
  12.7 0.0 collective-permute-done.2.refs_2_.refs_1_
  12.7 0.0 copy-done.4
  12.7 0.5 copy-done.6
  13.3 0.0 copy-done.8
  13.3 3.0 %shard_map.96 = (bf16[4,2,256,128]{3,2,1,0:T(8,128)(2,1)}, bf16[4,2,256,128]{3,2,1,0:T(8,128)(2,1)}, bf16[4,2,256,128]{3,2,1,0:T(8,128)(2,1)}) custom-call(s32[1,8]{1,0:T(1,128)} %get-tuple-element.34.count_ref, s32[1,9]{1,0:T(1,128)} %copy-done.4, s32[1,9]{1,0:T(1,128)} %copy-done.6, s32[1,9]{1,0:T(1,128)} %copy-done.8, bf16[24,2,256,128]{3,2,1,0:T(8,128)(2,1)} %bitcast.5, ...), custom_call_target="tpu_custom_call" | custom-call | bytes 3145728 | tf_op jit(solution)/shard_map/pallas_call | solution.py:126
  16.3 3.9 %collective-permute-start.7 = (bf16[4,2,256,128]{3,2,1,0:T(8,128)(2,1)}, bf16[4,2,256,128]{3,2,1,0:T(8,128)(2,1)S(1)}, u32[]{:S(2)}, u32[]{:S(2)}) collective-permute-start(bf16[4,2,256,128]{3,2,1,0:T(8,128)(2,1)} %get-tuple-element.45), channel_id=1, source_target_pairs={{0,12},{4,0},{8,4},{12,8},{1,13},{5,1},{9,5},{13,9},{2,14},{6,2},{... | collective-permute-start | bytes 1572872 | tf_op jit(solution)/shard_map/ppermute | solution.py:383
  20.3 0.0 collective-permute-start.8
  20.3 0.6 collective-permute-start.6
  20.9 0.0 copy-done.1
  20.9 1.1 copy-done.2
  22.0 2.0 %shard_map.97.refs_0_ = bf16[8,2,256,128]{3,2,1,0:T(8,128)(2,1)S(1)} custom-call(s32[1,8]{1,0:T(1,128)S(1)} %copy-done.3, s32[1,9]{1,0:T(1,128)S(1)} %copy-done.12, bf16[24,2,256,128]{3,2,1,0:T(8,128)(2,1)S(1)} %bitcast.6, bf16[2,512,128]{2,1,0:T(8,128)(2,1)S(1)} %bitcast.10, bf16[4,2,256,128]{3,2,1,0:T(8,128)(2,1)S(1)} %copy-done.2), custom_call_target="tpu_custom_call" | custom-call | bytes 2097152 | tf_op jit(solution)/shard_map/pallas_call | solution.py:126
  24.0 9.1 %shard_map.98 = (bf16[2,2048,128]{2,1,0:T(8,128)(2,1)S(1)}, f32[2,128,2048]{2,1,0:T(8,128)S(1)}, f32[2,8,2048]{2,1,0:T(8,128)S(1)}) custom-call(s32[1,8]{1,0:T(1,128)S(1)} %copy-done.3, bf16[256,16,128]{2,1,0:T(8,128)(2,1)S(1)} %bitcast.14, bf16[8,2,256,128]{3,2,1,0:T(8,128)(2,1)S(1)} %shard_map.97.refs_0_, bf16[2,512,128]{2,1,0:T(8,128)(2,1)S(1)} %bitcast.11), custom_call_target="tpu_custom_call" | custom-call | flops 2684354560 | bytes 9699328 | tf_op jit(solution)/shard_map/pallas_call | solution.py:344
  33.1 3.3 %shard_map.99 = (bf16[3,2,256,128]{3,2,1,0:T(8,128)(2,1)S(1)}, bf16[3,2,256,128]{3,2,1,0:T(8,128)(2,1)S(1)}, bf16[3,2,256,128]{3,2,1,0:T(8,128)(2,1)S(1)}, bf16[...) custom-call(s32[1,8]{1,0:T(1,128)S(1)} %copy-done.3, ...), custom_call_target="tpu_custom_call" | custom-call | bytes 3932160 | tf_op jit(solution)/shard_map/pallas_call | solution.py:126
  36.4 2.3 %collective-permute-start.3 = (bf16[3,2,256,128]{3,2,1,0:T(8,128)(2,1)S(1)}, bf16[3,2,256,128]{3,2,1,0:T(8,128)(2,1)S(1)}, u32[]{:S(2)}, u32[]{:S(2)}) collective-permute-start(bf16[3,2,256,128]{3,2,1,0:T(8,128)(2,1)S(1)} %get-tuple-element.42), channel_id=1, source_target_pairs={{0,8},{4,12},{8,0},{12,4},{1,9},{5,13},{9,1},{13,5},{2,10},{6,14},... | collective-permute-start | bytes 1179656 | tf_op jit(solution)/shard_map/ppermute | solution.py:383
  38.8 3.8 %collective-permute-start.4 = (bf16[3,2,256,128]{3,2,1,0:T(8,128)(2,1)S(1)}, bf16[3,2,256,128]{3,2,1,0:T(8,128)(2,1)S(1)}, u32[]{:S(2)}, u32[]{:S(2)}) collective-permute-start(bf16[3,2,256,128]{3,2,1,0:T(8,128)(2,1)S(1)} %get-tuple-element.43), channel_id=1, source_target_pairs={{0,12},{4,0},{8,4},{12,8},{1,13},{5,1},{9,5},{13,9},{2,14},{6,2},{... | collective-permute-start | bytes 1179656 | tf_op jit(solution)/shard_map/ppermute | solution.py:383
  42.6 0.0 collective-permute-done.7.refs_1_.refs_6_
  42.6 17.0 %collective-permute-start.5 = (bf16[3,2,256,128]{3,2,1,0:T(8,128)(2,1)S(1)}, bf16[3,2,256,128]{3,2,1,0:T(8,128)(2,1)S(1)}, u32[]{:S(2)}, u32[]{:S(2)}) collective-permute-start(bf16[3,2,256,128]{3,2,1,0:T(8,128)(2,1)S(1)} %get-tuple-element.44), channel_id=1, source_target_pairs={{0,4},{4,8},{8,12},{12,0},{1,5},{5,9},{9,13},{13,1},{2,6},{6,10},{... | collective-permute-start | bytes 1179656 | tf_op jit(solution)/shard_map/ppermute | solution.py:383
  59.6 0.0 collective-permute-done.8.refs_2_.refs_7_
  59.6 21.7 %collective-permute-done.6.refs_0_.refs_5_ = bf16[4,2,256,128]{3,2,1,0:T(8,128)(2,1)S(1)} collective-permute-done((bf16[4,2,256,128]{3,2,1,0:T(8,128)(2,1)}, bf16[4,2,256,128]{3,2,1,0:T(8,128)(2,1)S(1)}, u32[]{:S(2)}, u32[]{:S(2)}) %collective-permute-start.6) | collective-permute-done | bytes 524320 | tf_op jit(solution)/shard_map/ppermute | solution.py:383
  81.3 8.7 %shard_map.100 = (f32[2,128,2048]{2,1,0:T(8,128)S(1)}, f32[2,8,2048]{2,1,0:T(8,128)S(1)}, bf16[1,2,256,128]{3,2,1,0:T(8,128)(2,1)S(1)}, bf16[1,2,256,128]{3,2,1,0:T(8,128)(2,1)S(1)}, bf16[1,2,256,128]{3,2,1,0:T(8,128)(2,1)S(1)}) custom-call(s32[1,8]{1,0:T(1,128)S(1)} %copy-done.3, ...), custom_call_target="tpu_custom_call", output_to_operand_aliasing={{2}: (7, {}), {3}: (8, {}), {4}: (9, {})} | custom-call | flops 2415919104 | bytes 9568256 | tf_op jit(solution)/shard_map/pallas_call | solution.py:344
  90.0 0.1 collective-permute-start.12
  90.0 4.5 %collective-permute-start.13 = (bf16[1,2,256,128]{3,2,1,0:T(8,128)(2,1)S(1)}, bf16[1,2,256,128]{3,2,1,0:T(8,128)(2,1)S(1)}, u32[]{:S(2)}, u32[]{:S(2)}) collective-permute-start(bf16[1,2,256,128]{3,2,1,0:T(8,128)(2,1)S(1)} %get-tuple-element.60), channel_id=1, source_target_pairs={{0,12},{4,0},{8,4},{12,8},{1,13},{5,1},{9,5},{13,9},{2,14},{6,2},{... | collective-permute-start | bytes 393224 | tf_op jit(solution)/shard_map/ppermute | solution.py:383
  94.6 0.0 collective-permute-done.3.refs_0_
  94.6 0.5 collective-permute-start.14
  95.1 0.0 collective-permute-done.4.refs_1_
  95.1 0.0 collective-permute-done.5.refs_2_
  95.1 0.0 copy-start.11
  95.1 8.7 %shard_map.101 = (f32[2,128,2048]{2,1,0:T(8,128)S(1)}, f32[2,8,2048]{2,1,0:T(8,128)S(1)}, bf16[1,2,256,128]{3,2,1,0:T(8,128)(2,1)S(1)}, bf16[1,2,256,128]{3,2,1,0:T(8,128)(2,1)S(1)}, bf16[1,2,256,128]{3,2,1,0:T(8,128)(2,1)S(1)}) custom-call(s32[1,8]{1,0:T(1,128)S(1)} %copy-done.3, ...), custom_call_target="tpu_custom_call", output_to_operand_aliasing={{2}: (7, {}), {3}: (8, {}), {4}: (9, {})} | custom-call | flops 2415919104 | bytes 9568256 | tf_op jit(solution)/shard_map/pallas_call | solution.py:344
  103.8 11.9 %collective-permute-start.9 = (bf16[1,2,256,128]{3,2,1,0:T(8,128)(2,1)S(1)}, bf16[1,2,256,128]{3,2,1,0:T(8,128)(2,1)S(1)}, u32[]{:S(2)}, u32[]{:S(2)}) collective-permute-start(bf16[1,2,256,128]{3,2,1,0:T(8,128)(2,1)S(1)} %get-tuple-element.56), channel_id=1, source_target_pairs={{0,8},{4,12},{8,0},{12,4},{1,9},{5,13},{9,1},{13,5},{2,10},{6,14},... | collective-permute-start | bytes 393224 | tf_op jit(solution)/shard_map/ppermute | solution.py:383
  115.7 0.7 collective-permute-start.10
  116.4 0.0 collective-permute-done.12.refs_0_
  116.4 1.3 collective-permute-start.11
  117.7 3.7 %shard_map.104 = bf16[24,2,256,128]{3,2,1,0:T(8,128)(2,1)} custom-call(s32[1,2]{1,0:T(1,128)S(1)} %copy-done.11, s32[1,2]{1,0:T(1,128)S(1)} %copy-done.10, s32[1,9]{1,0:T(1,128)S(1)} %copy-done.5, s32[1,9]{1,0:T(1,128)S(1)} %copy-done.9, s32[1,9]{1,0:T(1,128)S(1)} %copy-done.7, bf16[24,2,256,128]{3,2,1,0:T(8,128)(2,1)S(1)} %bitcast.8, ...), custom_call_target="tpu_custom_call" | custom-call | bytes 6291456 | tf_op jit(solution)/shard_map/pallas_call | solution.py:172
  121.5 0.0 collective-permute-done.13.refs_1_
  121.5 0.0 collective-permute-done.14.refs_2_
  121.5 3.9 %shard_map.102 = (f32[2,128,2048]{2,1,0:T(8,128)S(1)}, f32[2,8,2048]{2,1,0:T(8,128)S(1)}) custom-call(s32[1,8]{1,0:T(1,128)S(1)} %copy-done.3, bf16[2,2048,128]{2,1,0:T(8,128)(2,1)S(1)} %get-tuple-element.40.q_ref, bf16[1,2,256,128]{3,2,1,0:T(8,128)(2,1)S(1)} %collective-permute-done.12.refs_0_, ...), custom_call_target="tpu_custom_call" | custom-call | flops 805306368 | bytes 8781824 | tf_op jit(solution)/shard_map/pallas_call | solution.py:344
  125.4 0.0 collective-permute-done.9.refs_0_
  125.4 0.0 collective-permute-done.10.refs_1_
  125.4 0.0 collective-permute-done.11.refs_2_
  125.4 5.1 %shard_map.103 = bf16[256,16,128]{2,1,0:T(8,128)(2,1)} custom-call(s32[1,8]{1,0:T(1,128)S(1)} %copy-done.3, bf16[2,2048,128]{2,1,0:T(8,128)(2,1)S(1)} %get-tuple-element.40.q_ref, bf16[1,2,256,128]{3,2,1,0:T(8,128)(2,1)S(1)} %collective-permute-done.9.refs_0_, bf16[1,2,256,128]{3,2,1,0:T(8,128)(2,1)S(1)} %collective-permute-done.10.refs_1_, ...), custom_call_target="tpu_custom_call" | custom-call | flops 805306368 | bytes 8781824 | tf_op jit(solution)/shard_map/pallas_call | solution.py:344
  (20 shorter events, 0.0 us)
Async XLA Ops:
  0.6 20.3 %copy-start = (bf16[24,2,128,2,128]{4,3,2,1,0:T(2,128)(2,1)S(1)}, bf16[24,2,128,2,128]{4,3,2,1,0:T(2,128)(2,1)}, u32[]{:S(2)}) copy-start(bf16[24,2,128,2,128]{4,3,2,1,0:T(2,128)(2,1)} %param.10) | copy-start | bytes 9437188
  0.6 20.3 %copy-start.1 = (bf16[2,1,256,2,128]{4,3,2,1,0:T(2,128)(2,1)S(1)}, bf16[2,1,256,2,128]{4,3,2,1,0:T(2,128)(2,1)}, u32[]{:S(2)}) copy-start(bf16[2,1,256,2,128]{4,3,2,1,0:T(2,128)(2,1)} %param.9) | copy-start | bytes 786436
  3.1 17.8 %copy-start.3 = (s32[1,8]{1,0:T(1,128)S(1)}, s32[1,8]{1,0:T(1,128)}, u32[]{:S(2)}) copy-start(s32[1,8]{1,0:T(1,128)} %get-tuple-element.34.count_ref) | copy-start | bytes 100
  3.1 17.8 %copy-start.12 = (s32[1,9]{1,0:T(1,128)S(1)}, s32[1,9]{1,0:T(1,128)}, u32[]{:S(2)}) copy-start(s32[1,9]{1,0:T(1,128)} %get-tuple-element.35.refs_0_) | copy-start | bytes 112
  3.1 7.9 %collective-permute-start = (s32[1,9]{1,0:T(1,128)}, s32[1,9]{1,0:T(1,128)S(1)}, u32[]{:S(2)}, u32[]{:S(2)}) collective-permute-start(s32[1,9]{1,0:T(1,128)} %get-tuple-element.36), channel_id=1, source_target_pairs={{0,8},{4,12},{8,0},{12,4},{1,9},{5,13},{9,1},{13,5},{2,10},{6,14},... | collective-permute-start | bytes 116 | tf_op jit(solution)/shard_map/ppermute | solution.py:383
  7.2 5.5 %collective-permute-start.1 = (s32[1,9]{1,0:T(1,128)}, s32[1,9]{1,0:T(1,128)S(1)}, u32[]{:S(2)}, u32[]{:S(2)}) collective-permute-start(s32[1,9]{1,0:T(1,128)} %get-tuple-element.37), channel_id=1, source_target_pairs={{0,4},{4,8},{8,12},{12,0},{1,5},{5,9},{9,13},{13,1},{2,6},{6,10},{... | collective-permute-start | bytes 116 | tf_op jit(solution)/shard_map/ppermute | solution.py:383
  8.8 3.9 %collective-permute-start.2 = (s32[1,9]{1,0:T(1,128)}, s32[1,9]{1,0:T(1,128)S(1)}, u32[]{:S(2)}, u32[]{:S(2)}) collective-permute-start(s32[1,9]{1,0:T(1,128)} %get-tuple-element.38), channel_id=1, source_target_pairs={{0,12},{4,0},{8,4},{12,8},{1,13},{5,1},{9,5},{13,9},{2,14},{6,2},{... | collective-permute-start | bytes 116 | tf_op jit(solution)/shard_map/ppermute | solution.py:383
  11.1 1.7 %copy-start.4 = (s32[1,9]{1,0:T(1,128)}, s32[1,9]{1,0:T(1,128)S(1)}, u32[]{:S(2)}) copy-start(s32[1,9]{1,0:T(1,128)S(1)} %collective-permute-done.refs_0_) | copy-start | bytes 112
  12.7 0.5 copy-start.6
  12.7 0.6 copy-start.8
  16.3 26.3 %collective-permute-start.7 = (bf16[4,2,256,128]{3,2,1,0:T(8,128)(2,1)}, bf16[4,2,256,128]{3,2,1,0:T(8,128)(2,1)S(1)}, u32[]{:S(2)}, u32[]{:S(2)}) collective-permute-start(bf16[4,2,256,128]{3,2,1,0:T(8,128)(2,1)} %get-tuple-element.45), channel_id=1, source_target_pairs={{0,12},{4,0},{8,4},{12,8},{1,13},{5,1},{9,5},{13,9},{2,14},{6,2},{... | collective-permute-start | bytes 1572872 | tf_op jit(solution)/shard_map/ppermute | solution.py:383
  20.3 39.3 %collective-permute-start.8 = (bf16[4,2,256,128]{3,2,1,0:T(8,128)(2,1)}, bf16[4,2,256,128]{3,2,1,0:T(8,128)(2,1)S(1)}, u32[]{:S(2)}, u32[]{:S(2)}) collective-permute-start(bf16[4,2,256,128]{3,2,1,0:T(8,128)(2,1)} %get-tuple-element.46), channel_id=1, source_target_pairs={{0,4},{4,8},{8,12},{12,0},{1,5},{5,9},{9,13},{13,1},{2,6},{6,10},{... | collective-permute-start | bytes 1572872 | tf_op jit(solution)/shard_map/ppermute | solution.py:383
  20.3 61.0 %collective-permute-start.6 = (bf16[4,2,256,128]{3,2,1,0:T(8,128)(2,1)}, bf16[4,2,256,128]{3,2,1,0:T(8,128)(2,1)S(1)}, u32[]{:S(2)}, u32[]{:S(2)}) collective-permute-start(bf16[4,2,256,128]{3,2,1,0:T(8,128)(2,1)} %get-tuple-element.39.refs_3_), channel_id=1, source_target_pairs={{0,8},{4,12},{8,0},{12,4},{1,9},{5,13},{9,1},{13,5},{2,10},{6,14},... | collective-permute-start | bytes 1572872 | tf_op jit(solution)/shard_map/ppermute | solution.py:383
  20.9 1.1 copy-start.2
  22.0 2.0 %copy-start.13 = (bf16[1,256,16,128]{3,2,1,0:T(8,128)(2,1)S(1)}, bf16[1,256,16,128]{3,2,1,0:T(8,128)(2,1)}, u32[]{:S(2)}) copy-start(bf16[1,256,16,128]{3,2,1,0:T(8,128)(2,1)} %param.8) | copy-start | bytes 3145732
  24.0 9.1 %copy-start.5 = (s32[1,9]{1,0:T(1,128)S(1)}, s32[1,9]{1,0:T(1,128)}, u32[]{:S(2)}) copy-start(s32[1,9]{1,0:T(1,128)} %copy-done.4) | copy-start | bytes 112
  24.0 9.1 %copy-start.7 = (s32[1,9]{1,0:T(1,128)S(1)}, s32[1,9]{1,0:T(1,128)}, u32[]{:S(2)}) copy-start(s32[1,9]{1,0:T(1,128)} %copy-done.6) | copy-start | bytes 112
  24.0 9.1 %copy-start.9 = (s32[1,9]{1,0:T(1,128)S(1)}, s32[1,9]{1,0:T(1,128)}, u32[]{:S(2)}) copy-start(s32[1,9]{1,0:T(1,128)} %copy-done.8) | copy-start | bytes 112
  36.4 58.1 %collective-permute-start.3 = (bf16[3,2,256,128]{3,2,1,0:T(8,128)(2,1)S(1)}, bf16[3,2,256,128]{3,2,1,0:T(8,128)(2,1)S(1)}, u32[]{:S(2)}, u32[]{:S(2)}) collective-permute-start(bf16[3,2,256,128]{3,2,1,0:T(8,128)(2,1)S(1)} %get-tuple-element.42), channel_id=1, source_target_pairs={{0,8},{4,12},{8,0},{12,4},{1,9},{5,13},{9,1},{13,5},{2,10},{6,14},... | collective-permute-start | bytes 1179656 | tf_op jit(solution)/shard_map/ppermute | solution.py:383
  38.8 56.3 %collective-permute-start.4 = (bf16[3,2,256,128]{3,2,1,0:T(8,128)(2,1)S(1)}, bf16[3,2,256,128]{3,2,1,0:T(8,128)(2,1)S(1)}, u32[]{:S(2)}, u32[]{:S(2)}) collective-permute-start(bf16[3,2,256,128]{3,2,1,0:T(8,128)(2,1)S(1)} %get-tuple-element.43), channel_id=1, source_target_pairs={{0,12},{4,0},{8,4},{12,8},{1,13},{5,1},{9,5},{13,9},{2,14},{6,2},{... | collective-permute-start | bytes 1179656 | tf_op jit(solution)/shard_map/ppermute | solution.py:383
  42.6 52.5 %collective-permute-start.5 = (bf16[3,2,256,128]{3,2,1,0:T(8,128)(2,1)S(1)}, bf16[3,2,256,128]{3,2,1,0:T(8,128)(2,1)S(1)}, u32[]{:S(2)}, u32[]{:S(2)}) collective-permute-start(bf16[3,2,256,128]{3,2,1,0:T(8,128)(2,1)S(1)} %get-tuple-element.44), channel_id=1, source_target_pairs={{0,4},{4,8},{8,12},{12,0},{1,5},{5,9},{9,13},{13,1},{2,6},{6,10},{... | collective-permute-start | bytes 1179656 | tf_op jit(solution)/shard_map/ppermute | solution.py:383
  90.0 26.5 %collective-permute-start.12 = (bf16[1,2,256,128]{3,2,1,0:T(8,128)(2,1)S(1)}, bf16[1,2,256,128]{3,2,1,0:T(8,128)(2,1)S(1)}, u32[]{:S(2)}, u32[]{:S(2)}) collective-permute-start(bf16[1,2,256,128]{3,2,1,0:T(8,128)(2,1)S(1)} %get-tuple-element.59), channel_id=1, source_target_pairs={{0,8},{4,12},{8,0},{12,4},{1,9},{5,13},{9,1},{13,5},{2,10},{6,14},... | collective-permute-start | bytes 393224 | tf_op jit(solution)/shard_map/ppermute | solution.py:383
  90.0 31.4 %collective-permute-start.13 = (bf16[1,2,256,128]{3,2,1,0:T(8,128)(2,1)S(1)}, bf16[1,2,256,128]{3,2,1,0:T(8,128)(2,1)S(1)}, u32[]{:S(2)}, u32[]{:S(2)}) collective-permute-start(bf16[1,2,256,128]{3,2,1,0:T(8,128)(2,1)S(1)} %get-tuple-element.60), channel_id=1, source_target_pairs={{0,12},{4,0},{8,4},{12,8},{1,13},{5,1},{9,5},{13,9},{2,14},{6,2},{... | collective-permute-start | bytes 393224 | tf_op jit(solution)/shard_map/ppermute | solution.py:383
  94.6 26.9 %collective-permute-start.14 = (bf16[1,2,256,128]{3,2,1,0:T(8,128)(2,1)S(1)}, bf16[1,2,256,128]{3,2,1,0:T(8,128)(2,1)S(1)}, u32[]{:S(2)}, u32[]{:S(2)}) collective-permute-start(bf16[1,2,256,128]{3,2,1,0:T(8,128)(2,1)S(1)} %get-tuple-element.61), channel_id=1, source_target_pairs={{0,4},{4,8},{8,12},{12,0},{1,5},{5,9},{9,13},{13,1},{2,6},{6,10},{... | collective-permute-start | bytes 393224 | tf_op jit(solution)/shard_map/ppermute | solution.py:383
  95.1 22.7 %copy-start.10 = (s32[1,2]{1,0:T(1,128)S(1)}, s32[1,2]{1,0:T(1,128)}, u32[]{:S(2)}) copy-start(s32[1,2]{1,0:T(1,128)} %slot_ref.1) | copy-start | bytes 28
  95.1 22.7 %copy-start.11 = (s32[1,2]{1,0:T(1,128)S(1)}, s32[1,2]{1,0:T(1,128)}, u32[]{:S(2)}) copy-start(s32[1,2]{1,0:T(1,128)} %owner_ref.1) | copy-start | bytes 28
  103.8 21.6 %collective-permute-start.9 = (bf16[1,2,256,128]{3,2,1,0:T(8,128)(2,1)S(1)}, bf16[1,2,256,128]{3,2,1,0:T(8,128)(2,1)S(1)}, u32[]{:S(2)}, u32[]{:S(2)}) collective-permute-start(bf16[1,2,256,128]{3,2,1,0:T(8,128)(2,1)S(1)} %get-tuple-element.56), channel_id=1, source_target_pairs={{0,8},{4,12},{8,0},{12,4},{1,9},{5,13},{9,1},{13,5},{2,10},{6,14},... | collective-permute-start | bytes 393224 | tf_op jit(solution)/shard_map/ppermute | solution.py:383
  115.7 9.7 %collective-permute-start.10 = (bf16[1,2,256,128]{3,2,1,0:T(8,128)(2,1)S(1)}, bf16[1,2,256,128]{3,2,1,0:T(8,128)(2,1)S(1)}, u32[]{:S(2)}, u32[]{:S(2)}) collective-permute-start(bf16[1,2,256,128]{3,2,1,0:T(8,128)(2,1)S(1)} %get-tuple-element.57), channel_id=1, source_target_pairs={{0,12},{4,0},{8,4},{12,8},{1,13},{5,1},{9,5},{13,9},{2,14},{6,2},{... | collective-permute-start | bytes 393224 | tf_op jit(solution)/shard_map/ppermute | solution.py:383
  116.4 9.0 %collective-permute-start.11 = (bf16[1,2,256,128]{3,2,1,0:T(8,128)(2,1)S(1)}, bf16[1,2,256,128]{3,2,1,0:T(8,128)(2,1)S(1)}, u32[]{:S(2)}, u32[]{:S(2)}) collective-permute-start(bf16[1,2,256,128]{3,2,1,0:T(8,128)(2,1)S(1)} %get-tuple-element.58), channel_id=1, source_target_pairs={{0,4},{4,8},{8,12},{12,0},{1,5},{5,9},{9,13},{13,1},{2,6},{6,10},{... | collective-permute-start | bytes 393224 | tf_op jit(solution)/shard_map/ppermute | solution.py:383

commit v5 on v4

--- a/solution.py
+++ b/solution.py
@@ -186,12 +186,13 @@
 
 
 def attend_kernel(
-    spans, relays, kv_dev, group, block_tok, rows, first, final, count_ref, q_ref, *refs
+    spans, relays, afters, kv_dev, group, block_tok, rows, first, final, count_ref, q_ref, *refs
 ):
     parts, refs = refs[: len(spans)], refs[len(spans) :]
     ins = 1 if first else 2
     outs = 1 if final else 3 if first else 2
-    refs = refs[:ins] + refs[ins + relays : ins + relays + outs] + refs[-3:]
+    rest = refs[ins + relays + afters :]
+    refs = refs[:ins] + rest[:outs] + rest[-3:]
     if first:
         new_ref, q_out, acc_out, stat_out = refs[:4]
         head_dim = q_ref.shape[2]
@@ -321,7 +322,7 @@
 
 
 def attend(
-    counts, queries, parts, spans, kv_dev, block_tok, new_rows=None, state=None, final=False, relay=()
+    counts, queries, parts, spans, kv_dev, block_tok, new_rows=None, state=None, final=False, relay=(), after=()
 ):
     suffix, heads_dev, head_dim = queries.shape
     group = heads_dev // kv_dev
@@ -343,10 +344,10 @@
             out_shape = [jax.ShapeDtypeStruct(queries.shape, queries.dtype)]
     result = pl.pallas_call(
         functools.partial(
-            attend_kernel, spans, len(relay), kv_dev, group, block_tok, rows, first, final
+            attend_kernel, spans, len(relay), len(after), kv_dev, group, block_tok, rows, first, final
         ),
         out_shape=out_shape + [jax.ShapeDtypeStruct(x.shape, x.dtype) for x in relay],
-        in_specs=[SMEM] + [VMEM] * len(operands) + [ANY] * len(relay),
+        in_specs=[SMEM] + [VMEM] * len(operands) + [ANY] * (len(relay) + len(after)),
         out_specs=[VMEM] * len(out_shape) + [ANY] * len(relay),
         input_output_aliases={
             1 + len(operands) + i: len(out_shape) + i for i in range(len(relay))
@@ -362,7 +363,7 @@
             bytes_accessed=keys * kv_dev * head_dim * 4 + 16 * suffix * heads_dev * head_dim,
             transcendentals=suffix * heads_dev * keys,
         ),
-    )(counts, *operands, *relay)
+    )(counts, *operands, *relay, *after)
     step, relayed = result[: len(out_shape)], result[len(out_shape) :]
     return (step if first or final else [state[0], *step]), relayed
 
@@ -389,7 +390,7 @@
     rows = [asked[d] for d in shifts]
 
     first = max(1, 3 * capacity // 8)
-    cuts = sorted({0, first, min(2 * first, capacity), capacity - 1, capacity})
+    cuts = sorted({0, first, 2 * first, capacity})
     plans = [[(d, start, end - start) for d in shifts] for start, end in zip(cuts, cuts[1:])]
 
     def load(plan, first, after=()):
@@ -416,10 +417,10 @@
     state, _ = step(local, ((0, 0, capacity),), new_rows=new_rows)
 
     later = load(sum(plans[1:], []), False, [state[2]])
-    waiting = [later[i * len(shifts) : (i + 1) * len(shifts)] for i in range(len(plans) - 1)]
-    arrived.append(send(plans[1], waiting[0]))
+    arrived.append(send(plans[1], later[: len(shifts)]))
+    new_pool = None
     for i, plan in enumerate(plans):
-        relay = waiting[i + 1] if i + 2 < len(plans) else []
+        relay = later[len(shifts) :] if i == 0 else []
         groups = [slice(at, at + 8) for at in range(0, len(plan), 8)]
         for j, group in enumerate(groups):
             ends = j == len(groups) - 1
@@ -429,18 +430,21 @@
                 state=state,
                 final=ends and i == len(plans) - 1,
                 relay=relay if ends else [],
+                after=[new_pool] if i == 1 and j == 0 else [],
             )
-        if relay:
-            arrived.append(send(plans[i + 2], relayed))
-    new_pool = write_back(
-        write_owner,
-        write_slot,
-        [asked[num_blk - d] for d in shifts],
-        pool_rows,
-        new_rows,
-        arrived[0],
-        capacity,
-    )
+        if i == 0:
+            for k in range(2, len(plans)):
+                blocks, relayed = relayed[: len(plans[k])], relayed[len(plans[k]) :]
+                arrived.append(send(plans[k], blocks))
+            new_pool = write_back(
+                write_owner,
+                write_slot,
+                [asked[num_blk - d] for d in shifts],
+                pool_rows,
+                new_rows,
+                arrived[0],
+                capacity,
+            )
     return state[0][None], new_pool.reshape(pool.shape)
 
 

time: 131 us -> 127 us (0.969)
  the two profiles are of different devices: /device:TPU:0 before, /device:TPU:14 now
where the time goes in v5:
time: 127 us; the launch traced here: 125 us
  waiting for transfers between devices  54.9 us (43%)
  Pallas kernels  47.6 us (37%)
  starting transfers between devices  17.3 us (14%)
  local copies, waits for them, and re-layouts  3.57 us (3%)
  between operations  1.64 us (1%)
    ppermute x12, waiting for transfers between devices, shift(): lax.ppermute(array, 'blk', [(i, (i + d) % num_blk) for i in range(num_blk)])  54.9 us
    pallas_call x4, Pallas kernels, attend(): pl.pallas_call(functools.partial(attend_kernel, spans, len(relay), len(af...  33.9 us
    ppermute x12, starting transfers between devices, shift(): lax.ppermute(array, 'blk', [(i, (i + d) % num_blk) for i in range(num_blk)])  17.3 us
    pallas_call x3, Pallas kernels, gather(): pl.pallas_call(functools.partial(gather_kernel, plan, len(asked), pool.sh...  8.33 us
    pallas_call x1, Pallas kernels, write_back(): pl.pallas_call(functools.partial(write_back_kernel, capacity, pool.shape[...  3.73 us
    unnamed x30, local copies, waits for them, and re-layouts  3.57 us
  transfers between devices with their start and end apart: 12, of which 6 were waited for; matrix products, arithmetic and copies ran while one was open for 0% of the time, Pallas kernels for 28%

profile of v5, /device:TPU:14, one launch (start us, length us, event | category | flops | bytes accessed | tf_op | source)
XLA Modules:
  0.0 125.0 jit_solution(10790725888014309793)
XLA Ops:
  0.6 0.0 copy-start
  0.6 0.0 copy-start.1
  1.4 1.7 %shard_map.95 = (s32[1,8]{1,0:T(1,128)}, s32[1,9]{1,0:T(1,128)}, s32[1,9]{1,0:T(1,128)}, s32[1,9]{1,0:T(1,128)}, s32[1,9]{1,0:T(1,128)}) custom-call(s32[1,32]{1,0:T(1,128)} %refs_0_.1, s32[1,32]{1,0:T(1,128)} %refs_1_.1, s32[1]{0:T(128)S(6)} %copy.16.refs_2_, s32[1,2]{1,0:T(1,128)} %slot_ref.1, s32[1,2]{1,0:T(1,128)} %owner_ref.1), custom_call_target="tpu_custom_call" | custom-call | tf_op jit(solution)/shard_map/pallas_call | solution.py:69
  3.1 0.0 copy-start.10
  3.1 0.0 copy-start.13
  3.1 2.7 %collective-permute-start = (s32[1,9]{1,0:T(1,128)}, s32[1,9]{1,0:T(1,128)S(1)}, u32[]{:S(2)}, u32[]{:S(2)}) collective-permute-start(s32[1,9]{1,0:T(1,128)} %get-tuple-element.28), channel_id=1, source_target_pairs={{0,8},{4,12},{8,0},{12,4},{1,9},{5,13},{9,1},{13,5},{2,10},{6,14},... | collective-permute-start | bytes 116 | tf_op jit(solution)/shard_map/ppermute | solution.py:384
  5.8 0.0 collective-permute-start.1
  5.8 2.0 %collective-permute-start.2 = (s32[1,9]{1,0:T(1,128)}, s32[1,9]{1,0:T(1,128)S(1)}, u32[]{:S(2)}, u32[]{:S(2)}) collective-permute-start(s32[1,9]{1,0:T(1,128)} %get-tuple-element.30), channel_id=1, source_target_pairs={{0,12},{4,0},{8,4},{12,8},{1,13},{5,1},{9,5},{13,9},{2,14},{6,2},{... | collective-permute-start | bytes 116 | tf_op jit(solution)/shard_map/ppermute | solution.py:384
  7.8 0.0 collective-permute-done.refs_0_
  7.8 1.6 %collective-permute-done.1.refs_1_.refs_2_ = s32[1,9]{1,0:T(1,128)S(1)} collective-permute-done((s32[1,9]{1,0:T(1,128)}, s32[1,9]{1,0:T(1,128)S(1)}, u32[]{:S(2)}, u32[]{:S(2)}) %collective-permute-start.1) | collective-permute-done | bytes 68 | tf_op jit(solution)/shard_map/ppermute | solution.py:384
  9.5 0.1 collective-permute-done.2.refs_2_.refs_1_
  9.6 0.0 copy-done.4
  9.6 0.4 copy-done.6
  10.0 0.2 copy-done.8
  10.1 3.0 %shard_map.96 = (bf16[4,2,256,128]{3,2,1,0:T(8,128)(2,1)}, bf16[4,2,256,128]{3,2,1,0:T(8,128)(2,1)}, bf16[4,2,256,128]{3,2,1,0:T(8,128)(2,1)}) custom-call(s32[1,8]{1,0:T(1,128)} %get-tuple-element.26.count_ref, s32[1,9]{1,0:T(1,128)} %copy-done.4, s32[1,9]{1,0:T(1,128)} %copy-done.6, s32[1,9]{1,0:T(1,128)} %copy-done.8, bf16[24,2,256,128]{3,2,1,0:T(8,128)(2,1)} %bitcast.5, ...), custom_call_target="tpu_custom_call" | custom-call | bytes 3145728 | tf_op jit(solution)/shard_map/pallas_call | solution.py:126
  13.2 2.2 %collective-permute-start.4 = (bf16[4,2,256,128]{3,2,1,0:T(8,128)(2,1)}, bf16[4,2,256,128]{3,2,1,0:T(8,128)(2,1)S(1)}, u32[]{:S(2)}, u32[]{:S(2)}) collective-permute-start(bf16[4,2,256,128]{3,2,1,0:T(8,128)(2,1)} %get-tuple-element.33), channel_id=1, source_target_pairs={{0,12},{4,0},{8,4},{12,8},{1,13},{5,1},{9,5},{13,9},{2,14},{6,2},{... | collective-permute-start | bytes 1572872 | tf_op jit(solution)/shard_map/ppermute | solution.py:384
  15.4 0.0 collective-permute-start.5
  15.4 6.3 %collective-permute-start.3 = (bf16[4,2,256,128]{3,2,1,0:T(8,128)(2,1)}, bf16[4,2,256,128]{3,2,1,0:T(8,128)(2,1)S(1)}, u32[]{:S(2)}, u32[]{:S(2)}) collective-permute-start(bf16[4,2,256,128]{3,2,1,0:T(8,128)(2,1)} %get-tuple-element.31.refs_3_), channel_id=1, source_target_pairs={{0,8},{4,12},{8,0},{12,4},{1,9},{5,13},{9,1},{13,5},{2,10},{6,14},... | collective-permute-start | bytes 1572872 | tf_op jit(solution)/shard_map/ppermute | solution.py:384
  21.6 0.0 copy-done
  21.6 0.0 copy-done.10
  21.7 1.1 copy-done.3
  22.7 2.0 %shard_map.97.refs_0_ = bf16[8,2,256,128]{3,2,1,0:T(8,128)(2,1)S(1)} custom-call(s32[1,8]{1,0:T(1,128)S(1)} %copy-done.10, s32[1,9]{1,0:T(1,128)S(1)} %copy-done.13, bf16[24,2,256,128]{3,2,1,0:T(8,128)(2,1)S(1)} %bitcast.6, bf16[2,512,128]{2,1,0:T(8,128)(2,1)S(1)} %bitcast.10, bf16[4,2,256,128]{3,2,1,0:T(8,128)(2,1)S(1)} %copy-done.3), custom_call_target="tpu_custom_call" | custom-call | bytes 2097152 | tf_op jit(solution)/shard_map/pallas_call | solution.py:126
  24.7 0.0 copy-done.14
  24.7 0.0 copy-start.5
  24.8 0.0 copy-start.7
  24.8 0.0 copy-start.9
  24.8 9.1 %shard_map.98 = (bf16[2,2048,128]{2,1,0:T(8,128)(2,1)S(1)}, f32[2,128,2048]{2,1,0:T(8,128)S(1)}, f32[2,8,2048]{2,1,0:T(8,128)S(1)}) custom-call(s32[1,8]{1,0:T(1,128)S(1)} %copy-done.10, bf16[256,16,128]{2,1,0:T(8,128)(2,1)S(1)} %bitcast.15, bf16[8,2,256,128]{3,2,1,0:T(8,128)(2,1)S(1)} %shard_map.97.refs_0_, bf16[2,512,128]{2,1,0:T(8,128)(2,1)S(1)} %bitcast.11), custom_call_target="tpu_custom_call" | custom-call | flops 2684354560 | bytes 9699328 | tf_op jit(solution)/shard_map/pallas_call | solution.py:345
  33.9 3.3 %shard_map.99 = (bf16[3,2,256,128]{3,2,1,0:T(8,128)(2,1)S(1)}, bf16[3,2,256,128]{3,2,1,0:T(8,128)(2,1)S(1)}, bf16[3,2,256,128]{3,2,1,0:T(8,128)(2,1)S(1)}, bf16[...) custom-call(s32[1,8]{1,0:T(1,128)S(1)} %copy-done.10, ...), custom_call_target="tpu_custom_call" | custom-call | bytes 3932160 | tf_op jit(solution)/shard_map/pallas_call | solution.py:126
  37.2 0.1 collective-permute-start.9
  37.3 0.5 collective-permute-start.10
  37.8 18.8 %collective-permute-done.4.refs_1_.refs_6_ = bf16[4,2,256,128]{3,2,1,0:T(8,128)(2,1)S(1)} collective-permute-done((bf16[4,2,256,128]{3,2,1,0:T(8,128)(2,1)}, bf16[4,2,256,128]{3,2,1,0:T(8,128)(2,1)S(1)}, u32[]{:S(2)}, u32[]{:S(2)}) %collective-permute-start.4) | collective-permute-done | bytes 524320 | tf_op jit(solution)/shard_map/ppermute | solution.py:384
  56.5 0.0 collective-permute-start.11
  56.5 0.0 collective-permute-done.5.refs_2_.refs_7_
  56.5 24.9 %collective-permute-done.3.refs_0_.refs_5_ = bf16[4,2,256,128]{3,2,1,0:T(8,128)(2,1)S(1)} collective-permute-done((bf16[4,2,256,128]{3,2,1,0:T(8,128)(2,1)}, bf16[4,2,256,128]{3,2,1,0:T(8,128)(2,1)S(1)}, u32[]{:S(2)}, u32[]{:S(2)}) %collective-permute-start.3) | collective-permute-done | bytes 524320 | tf_op jit(solution)/shard_map/ppermute | solution.py:384
  81.5 8.6 %shard_map.100 = (f32[2,128,2048]{2,1,0:T(8,128)S(1)}, f32[2,8,2048]{2,1,0:T(8,128)S(1)}, bf16[2,2,256,128]{3,2,1,0:T(8,128)(2,1)S(1)}, bf16[2,2,256,128]{3,2,1,0:T(8,128)(2,1)S(1)}, bf16[2,2,256,128]{3,2,1,0:T(8,128)(2,1)S(1)}) custom-call(s32[1,8]{1,0:T(1,128)S(1)} %copy-done.10, ...), custom_call_target="tpu_custom_call", output_to_operand_aliasing={{2}: (7, {}), {3}: (8, {}), {4}: (9, {})} | custom-call | flops 2415919104 | bytes 9568256 | tf_op jit(solution)/shard_map/pallas_call | solution.py:345
  90.1 3.3 %collective-permute-start.6 = (bf16[2,2,256,128]{3,2,1,0:T(8,128)(2,1)S(1)}, bf16[2,2,256,128]{3,2,1,0:T(8,128)(2,1)S(1)}, u32[]{:S(2)}, u32[]{:S(2)}) collective-permute-start(bf16[2,2,256,128]{3,2,1,0:T(8,128)(2,1)S(1)} %get-tuple-element.40), channel_id=1, source_target_pairs={{0,8},{4,12},{8,0},{12,4},{1,9},{5,13},{9,1},{13,5},{2,10},{6,14},... | collective-permute-start | bytes 786440 | tf_op jit(solution)/shard_map/ppermute | solution.py:384
  93.4 0.0 collective-permute-start.7
  93.5 1.8 %collective-permute-done.9.refs_0_ = bf16[3,2,256,128]{3,2,1,0:T(8,128)(2,1)S(1)} collective-permute-done((bf16[3,2,256,128]{3,2,1,0:T(8,128)(2,1)S(1)}, bf16[3,2,256,128]{3,2,1,0:T(8,128)(2,1)S(1)}, u32[]{:S(2)}, u32[]{:S(2)}) %collective-permute-start.9) | collective-permute-done | bytes 393248 | tf_op jit(solution)/shard_map/ppermute | solution.py:384
  95.3 0.2 collective-permute-start.8
  95.5 3.7 %shard_map.101.refs_5_ = bf16[24,2,256,128]{3,2,1,0:T(8,128)(2,1)} custom-call(s32[1,2]{1,0:T(1,128)S(1)} %copy-done.12, s32[1,2]{1,0:T(1,128)S(1)} %copy-done.11, s32[1,9]{1,0:T(1,128)S(1)} %copy-done.5, s32[1,9]{1,0:T(1,128)S(1)} %copy-done.9, s32[1,9]{1,0:T(1,128)S(1)} %copy-done.7, bf16[24,2,256,128]{3,2,1,0:T(8,128)(2,1)S(1)} %bitcast.8, ...), custom_call_target="tpu_custom_call" | custom-call | bytes 6291456 | tf_op jit(solution)/shard_map/pallas_call | solution.py:172
  99.2 7.7 %collective-permute-done.10.refs_1_ = bf16[3,2,256,128]{3,2,1,0:T(8,128)(2,1)S(1)} collective-permute-done((bf16[3,2,256,128]{3,2,1,0:T(8,128)(2,1)S(1)}, bf16[3,2,256,128]{3,2,1,0:T(8,128)(2,1)S(1)}, u32[]{:S(2)}, u32[]{:S(2)}) %collective-permute-start.10) | collective-permute-done | bytes 393248 | tf_op jit(solution)/shard_map/ppermute | solution.py:384
  106.9 0.0 collective-permute-done.11.refs_2_
  106.9 1.9 %copy-done.2 = bf16[24,2,256,128]{3,2,1,0:T(8,128)(2,1)S(1)} copy-done((bf16[24,2,256,128]{3,2,1,0:T(8,128)(2,1)S(1)}, bf16[24,2,256,128]{3,2,1,0:T(8,128)(2,1)}, u32[]{:S(2)}) %copy-start.2) | copy-done | bytes 3145752
  108.8 8.7 %shard_map.102 = (f32[2,128,2048]{2,1,0:T(8,128)S(1)}, f32[2,8,2048]{2,1,0:T(8,128)S(1)}) custom-call(s32[1,8]{1,0:T(1,128)S(1)} %copy-done.10, bf16[2,2048,128]{2,1,0:T(8,128)(2,1)S(1)} %get-tuple-element.32.q_ref, bf16[3,2,256,128]{3,2,1,0:T(8,128)(2,1)S(1)} %collective-permute-done.9.refs_0_, ...), custom_call_target="tpu_custom_call" | custom-call | flops 2415919104 | bytes 9568256 | tf_op jit(solution)/shard_map/pallas_call | solution.py:345
  117.5 0.0 collective-permute-done.6.refs_0_
  117.5 0.0 collective-permute-done.7.refs_1_
  117.5 0.0 collective-permute-done.8.refs_2_
  117.6 7.5 %shard_map.103 = bf16[256,16,128]{2,1,0:T(8,128)(2,1)} custom-call(s32[1,8]{1,0:T(1,128)S(1)} %copy-done.10, bf16[2,2048,128]{2,1,0:T(8,128)(2,1)S(1)} %get-tuple-element.32.q_ref, bf16[2,2,256,128]{3,2,1,0:T(8,128)(2,1)S(1)} %collective-permute-done.6.refs_0_, bf16[2,2,256,128]{3,2,1,0:T(8,128)(2,1)S(1)} %collective-permute-done.7.refs_1_, ...), custom_call_target="tpu_custom_call" | custom-call | flops 1610612736 | bytes 9175040 | tf_op jit(solution)/shard_map/pallas_call | solution.py:345
  (15 shorter events, 0.0 us)
Async XLA Ops:
  0.6 21.0 %copy-start = (bf16[24,2,128,2,128]{4,3,2,1,0:T(2,128)(2,1)S(1)}, bf16[24,2,128,2,128]{4,3,2,1,0:T(2,128)(2,1)}, u32[]{:S(2)}) copy-start(bf16[24,2,128,2,128]{4,3,2,1,0:T(2,128)(2,1)} %param.10) | copy-start | bytes 9437188
  0.6 21.0 %copy-start.1 = (bf16[2,1,256,2,128]{4,3,2,1,0:T(2,128)(2,1)S(1)}, bf16[2,1,256,2,128]{4,3,2,1,0:T(2,128)(2,1)}, u32[]{:S(2)}) copy-start(bf16[2,1,256,2,128]{4,3,2,1,0:T(2,128)(2,1)} %param.9) | copy-start | bytes 786436
  3.1 18.5 %copy-start.10 = (s32[1,8]{1,0:T(1,128)S(1)}, s32[1,8]{1,0:T(1,128)}, u32[]{:S(2)}) copy-start(s32[1,8]{1,0:T(1,128)} %get-tuple-element.26.count_ref) | copy-start | bytes 100
  3.1 18.5 %copy-start.13 = (s32[1,9]{1,0:T(1,128)S(1)}, s32[1,9]{1,0:T(1,128)}, u32[]{:S(2)}) copy-start(s32[1,9]{1,0:T(1,128)} %get-tuple-element.27.refs_0_) | copy-start | bytes 112
  3.1 4.7 %collective-permute-start = (s32[1,9]{1,0:T(1,128)}, s32[1,9]{1,0:T(1,128)S(1)}, u32[]{:S(2)}, u32[]{:S(2)}) collective-permute-start(s32[1,9]{1,0:T(1,128)} %get-tuple-element.28), channel_id=1, source_target_pairs={{0,8},{4,12},{8,0},{12,4},{1,9},{5,13},{9,1},{13,5},{2,10},{6,14},... | collective-permute-start | bytes 116 | tf_op jit(solution)/shard_map/ppermute | solution.py:384
  5.8 3.7 %collective-permute-start.1 = (s32[1,9]{1,0:T(1,128)}, s32[1,9]{1,0:T(1,128)S(1)}, u32[]{:S(2)}, u32[]{:S(2)}) collective-permute-start(s32[1,9]{1,0:T(1,128)} %get-tuple-element.29), channel_id=1, source_target_pairs={{0,4},{4,8},{8,12},{12,0},{1,5},{5,9},{9,13},{13,1},{2,6},{6,10},{... | collective-permute-start | bytes 116 | tf_op jit(solution)/shard_map/ppermute | solution.py:384
  5.8 3.8 %collective-permute-start.2 = (s32[1,9]{1,0:T(1,128)}, s32[1,9]{1,0:T(1,128)S(1)}, u32[]{:S(2)}, u32[]{:S(2)}) collective-permute-start(s32[1,9]{1,0:T(1,128)} %get-tuple-element.30), channel_id=1, source_target_pairs={{0,12},{4,0},{8,4},{12,8},{1,13},{5,1},{9,5},{13,9},{2,14},{6,2},{... | collective-permute-start | bytes 116 | tf_op jit(solution)/shard_map/ppermute | solution.py:384
  7.8 1.7 %copy-start.4 = (s32[1,9]{1,0:T(1,128)}, s32[1,9]{1,0:T(1,128)S(1)}, u32[]{:S(2)}) copy-start(s32[1,9]{1,0:T(1,128)S(1)} %collective-permute-done.refs_0_) | copy-start | bytes 112
  9.5 0.5 copy-start.6
  9.6 0.6 copy-start.8
  13.2 43.4 %collective-permute-start.4 = (bf16[4,2,256,128]{3,2,1,0:T(8,128)(2,1)}, bf16[4,2,256,128]{3,2,1,0:T(8,128)(2,1)S(1)}, u32[]{:S(2)}, u32[]{:S(2)}) collective-permute-start(bf16[4,2,256,128]{3,2,1,0:T(8,128)(2,1)} %get-tuple-element.33), channel_id=1, source_target_pairs={{0,12},{4,0},{8,4},{12,8},{1,13},{5,1},{9,5},{13,9},{2,14},{6,2},{... | collective-permute-start | bytes 1572872 | tf_op jit(solution)/shard_map/ppermute | solution.py:384
  15.4 41.2 %collective-permute-start.5 = (bf16[4,2,256,128]{3,2,1,0:T(8,128)(2,1)}, bf16[4,2,256,128]{3,2,1,0:T(8,128)(2,1)S(1)}, u32[]{:S(2)}, u32[]{:S(2)}) collective-permute-start(bf16[4,2,256,128]{3,2,1,0:T(8,128)(2,1)} %get-tuple-element.34), channel_id=1, source_target_pairs={{0,4},{4,8},{8,12},{12,0},{1,5},{5,9},{9,13},{13,1},{2,6},{6,10},{... | collective-permute-start | bytes 1572872 | tf_op jit(solution)/shard_map/ppermute | solution.py:384
  15.4 66.1 %collective-permute-start.3 = (bf16[4,2,256,128]{3,2,1,0:T(8,128)(2,1)}, bf16[4,2,256,128]{3,2,1,0:T(8,128)(2,1)S(1)}, u32[]{:S(2)}, u32[]{:S(2)}) collective-permute-start(bf16[4,2,256,128]{3,2,1,0:T(8,128)(2,1)} %get-tuple-element.31.refs_3_), channel_id=1, source_target_pairs={{0,8},{4,12},{8,0},{12,4},{1,9},{5,13},{9,1},{13,5},{2,10},{6,14},... | collective-permute-start | bytes 1572872 | tf_op jit(solution)/shard_map/ppermute | solution.py:384
  21.7 1.1 copy-start.3
  22.7 2.0 %copy-start.14 = (bf16[1,256,16,128]{3,2,1,0:T(8,128)(2,1)S(1)}, bf16[1,256,16,128]{3,2,1,0:T(8,128)(2,1)}, u32[]{:S(2)}) copy-start(bf16[1,256,16,128]{3,2,1,0:T(8,128)(2,1)} %param.8) | copy-start | bytes 3145732
  24.7 9.1 %copy-start.5 = (s32[1,9]{1,0:T(1,128)S(1)}, s32[1,9]{1,0:T(1,128)}, u32[]{:S(2)}) copy-start(s32[1,9]{1,0:T(1,128)} %copy-done.4) | copy-start | bytes 112
  24.8 9.1 %copy-start.7 = (s32[1,9]{1,0:T(1,128)S(1)}, s32[1,9]{1,0:T(1,128)}, u32[]{:S(2)}) copy-start(s32[1,9]{1,0:T(1,128)} %copy-done.6) | copy-start | bytes 112
  24.8 9.1 %copy-start.9 = (s32[1,9]{1,0:T(1,128)S(1)}, s32[1,9]{1,0:T(1,128)}, u32[]{:S(2)}) copy-start(s32[1,9]{1,0:T(1,128)} %copy-done.8) | copy-start | bytes 112
  37.2 58.1 %collective-permute-start.9 = (bf16[3,2,256,128]{3,2,1,0:T(8,128)(2,1)S(1)}, bf16[3,2,256,128]{3,2,1,0:T(8,128)(2,1)S(1)}, u32[]{:S(2)}, u32[]{:S(2)}) collective-permute-start(bf16[3,2,256,128]{3,2,1,0:T(8,128)(2,1)S(1)} %get-tuple-element.43), channel_id=1, source_target_pairs={{0,8},{4,12},{8,0},{12,4},{1,9},{5,13},{9,1},{13,5},{2,10},{6,14},... | collective-permute-start | bytes 1179656 | tf_op jit(solution)/shard_map/ppermute | solution.py:384
  37.3 69.7 %collective-permute-start.10 = (bf16[3,2,256,128]{3,2,1,0:T(8,128)(2,1)S(1)}, bf16[3,2,256,128]{3,2,1,0:T(8,128)(2,1)S(1)}, u32[]{:S(2)}, u32[]{:S(2)}) collective-permute-start(bf16[3,2,256,128]{3,2,1,0:T(8,128)(2,1)S(1)} %get-tuple-element.44), channel_id=1, source_target_pairs={{0,12},{4,0},{8,4},{12,8},{1,13},{5,1},{9,5},{13,9},{2,14},{6,2},{... | collective-permute-start | bytes 1179656 | tf_op jit(solution)/shard_map/ppermute | solution.py:384
  56.5 50.4 %collective-permute-start.11 = (bf16[3,2,256,128]{3,2,1,0:T(8,128)(2,1)S(1)}, bf16[3,2,256,128]{3,2,1,0:T(8,128)(2,1)S(1)}, u32[]{:S(2)}, u32[]{:S(2)}) collective-permute-start(bf16[3,2,256,128]{3,2,1,0:T(8,128)(2,1)S(1)} %get-tuple-element.45), channel_id=1, source_target_pairs={{0,4},{4,8},{8,12},{12,0},{1,5},{5,9},{9,13},{13,1},{2,6},{6,10},{... | collective-permute-start | bytes 1179656 | tf_op jit(solution)/shard_map/ppermute | solution.py:384
  81.5 14.0 %copy-start.11 = (s32[1,2]{1,0:T(1,128)S(1)}, s32[1,2]{1,0:T(1,128)}, u32[]{:S(2)}) copy-start(s32[1,2]{1,0:T(1,128)} %slot_ref.1) | copy-start | bytes 28
  81.5 14.0 %copy-start.12 = (s32[1,2]{1,0:T(1,128)S(1)}, s32[1,2]{1,0:T(1,128)}, u32[]{:S(2)}) copy-start(s32[1,2]{1,0:T(1,128)} %owner_ref.1) | copy-start | bytes 28
  90.1 27.4 %collective-permute-start.6 = (bf16[2,2,256,128]{3,2,1,0:T(8,128)(2,1)S(1)}, bf16[2,2,256,128]{3,2,1,0:T(8,128)(2,1)S(1)}, u32[]{:S(2)}, u32[]{:S(2)}) collective-permute-start(bf16[2,2,256,128]{3,2,1,0:T(8,128)(2,1)S(1)} %get-tuple-element.40), channel_id=1, source_target_pairs={{0,8},{4,12},{8,0},{12,4},{1,9},{5,13},{9,1},{13,5},{2,10},{6,14},... | collective-permute-start | bytes 786440 | tf_op jit(solution)/shard_map/ppermute | solution.py:384
  93.4 24.1 %collective-permute-start.7 = (bf16[2,2,256,128]{3,2,1,0:T(8,128)(2,1)S(1)}, bf16[2,2,256,128]{3,2,1,0:T(8,128)(2,1)S(1)}, u32[]{:S(2)}, u32[]{:S(2)}) collective-permute-start(bf16[2,2,256,128]{3,2,1,0:T(8,128)(2,1)S(1)} %get-tuple-element.41), channel_id=1, source_target_pairs={{0,12},{4,0},{8,4},{12,8},{1,13},{5,1},{9,5},{13,9},{2,14},{6,2},{... | collective-permute-start | bytes 786440 | tf_op jit(solution)/shard_map/ppermute | solution.py:384
  95.3 22.3 %collective-permute-start.8 = (bf16[2,2,256,128]{3,2,1,0:T(8,128)(2,1)S(1)}, bf16[2,2,256,128]{3,2,1,0:T(8,128)(2,1)S(1)}, u32[]{:S(2)}, u32[]{:S(2)}) collective-permute-start(bf16[2,2,256,128]{3,2,1,0:T(8,128)(2,1)S(1)} %get-tuple-element.42), channel_id=1, source_target_pairs={{0,4},{4,8},{8,12},{12,0},{1,5},{5,9},{9,13},{13,1},{2,6},{6,10},{... | collective-permute-start | bytes 786440 | tf_op jit(solution)/shard_map/ppermute | solution.py:384
  106.9 1.9 %copy-start.2 = (bf16[24,2,256,128]{3,2,1,0:T(8,128)(2,1)S(1)}, bf16[24,2,256,128]{3,2,1,0:T(8,128)(2,1)}, u32[]{:S(2)}) copy-start(bf16[24,2,256,128]{3,2,1,0:T(8,128)(2,1)} %shard_map.101.refs_5_) | copy-start | bytes 9437188
